TPU v7x, 256 devices: a whole 4x4x8 slice. The times are simulated.
256 devices in a mesh: col: 32 (over y, z), lay: 8 (over x, core).
Axes of the slice: x: 4, y: 4, z: 8, core: 2. Of those that a mesh axis runs over, the one named last changes fastest.
Arguments:
- flux_operator: bfloat16 [32, 8, 4, 1024, 1024], P('col', 'lay'), as said below
- dof_order: int32 [32, 8, 1024], P('col', 'lay'), may hold values from 0 to 1023, each once within a row
- local_gap: float32 [32, 8, 4, 1024, 128], P('col', 'lay'), may hold values from -6 to 6
- rigid_load: float32 [32, 8, 4, 128], P('col', 'lay'), may hold values from -96 to 96
Outputs:
- multipliers: float32 [32, 8, 4, 1024, 128], P('col', 'lay')
Inputs may be any that keep to these rules, and one draw needn't show every extreme that they name: `flux_operator`: each subdomain's operator of each species is symmetric positive definite.
All inputs are finite; a program needn't handle non-finite values.
Results may differ from a plain program's by a relative error of at most 0.0005.
The roundings to bfloat16 on the way count: a program that leaves them out, or rounds other values in their place, can miss the bound.
Values sent between devices are 32-bit elements; how exact they have to be, the bound alone decides.
No kernel may reach another device: no remote copies, remote signals or barrier semaphores. Data moves between devices by JAX's collectives and lax.ppermute only.
A program may use at most 128 MiB of HBM per device.

v0:
```python
import jax
import jax.numpy as jnp
from jax import lax
from jax.sharding import PartitionSpec as P

FACE_SIDE = 192
FACE_TOP = 128
YCOLS = 4
ITERS = 3


def passed_along(value, axis, steps):
    count = lax.axis_size(axis)
    leading, last = (max(0, -steps), min(count, count - steps))
    return lax.ppermute(value, axis, [(source, source + steps) for source in range(leading, last)])


def coarse_matrix(xcount, ycount, zcount, side, top):
    count = xcount * ycount * zcount
    index = jnp.arange(count)
    zpos = index % zcount
    cpos = index // zcount
    ypos = cpos % ycount
    xpos = cpos // ycount
    dx = jnp.abs(xpos[:, None] - xpos[None, :])
    dy = jnp.abs(ypos[:, None] - ypos[None, :])
    dz = jnp.abs(zpos[:, None] - zpos[None, :])
    lateral = (dx == 1) & (dy == 0) & (dz == 0) | (dx == 0) & (dy == 1) & (dz == 0)
    upward = (dx == 0) & (dy == 0) & (dz == 1)
    width = 4 * side + 2 * top
    matrix = width * jnp.eye(count, dtype=jnp.float32)
    matrix = matrix - side * lateral.astype(jnp.float32) - top * upward.astype(jnp.float32)
    return matrix


def coarse_solve(chol, rhs):
    count = chol.shape[0]
    flat = rhs.reshape(count, -1)
    inner_z = lax.linalg.triangular_solve(chol, flat, left_side=True, lower=True)
    result = lax.linalg.triangular_solve(
        chol, inner_z, left_side=True, lower=True, transpose_a=True
    )
    return result.reshape(rhs.shape)


def shards(flux_operator, dof_order, local_gap, rigid_load):
    flux = flux_operator[0, 0]
    order = dof_order[0, 0]
    gap = local_gap[0, 0]
    load = rigid_load[0, 0]
    species, width, cases = gap.shape
    ncol = lax.axis_size("col")
    nlay = lax.axis_size("lay")
    xcount = ncol // YCOLS
    count = ncol * nlay
    col = lax.axis_index("col")
    lay = lax.axis_index("lay")
    xpos = col // YCOLS
    ypos = col % YCOLS
    me = col * nlay + lay
    flags = [xpos > 0, xpos < xcount - 1, ypos > 0, ypos < YCOLS - 1, lay > 0, lay < nlay - 1]
    offsets = [-YCOLS * nlay, YCOLS * nlay, -nlay, nlay, -1, 1]
    sizes = [FACE_SIDE, FACE_SIDE, FACE_SIDE, FACE_SIDE, FACE_TOP, FACE_TOP]
    starts = [0]
    for size in sizes:
        starts.append(starts[-1] + size)
    weight = jnp.concatenate(
        [
            jnp.broadcast_to(jnp.where(flags[f], 0.5, 1.0).astype(jnp.float32), (sizes[f],))
            for f in range(6)
        ]
    )[None, :, None]
    inverse = jnp.argsort(order)
    chol = jnp.linalg.cholesky(coarse_matrix(xcount, YCOLS, nlay, FACE_SIDE, FACE_TOP))

    def split(field):
        return [field[:, starts[f] : starts[f + 1], :] for f in range(6)]

    def assemble(field):
        blocks = split(field)
        result = list(blocks)
        for target, source, step in ((1, 0, -YCOLS), (0, 1, YCOLS), (3, 2, -1), (2, 3, 1)):
            arrived = passed_along(blocks[source], "col", step)
            result[target] = blocks[target] - jnp.where(flags[target], arrived, 0.0)
        for target, source, step in ((5, 4, -1), (4, 5, 1)):
            arrived = passed_along(blocks[source], "lay", step)
            result[target] = blocks[target] - jnp.where(flags[target], arrived, 0.0)
        return jnp.concatenate(result, axis=1)

    def inner_local(left, right):
        return jnp.sum(weight * left * right, axis=1)

    def apply(field):
        local = jnp.take(field, order, axis=1).astype(jnp.bfloat16)
        image = jnp.einsum("kij,kjn->kin", flux, local, preferred_element_type=jnp.float32)
        return jnp.take(image, inverse, axis=1)

    def spread(coarse_y):
        mine = lax.dynamic_index_in_dim(coarse_y, me, 0, keepdims=False)
        blocks = []
        for f in range(6):
            peer_index = jnp.clip(me + offsets[f], 0, count - 1)
            peer = lax.dynamic_index_in_dim(coarse_y, peer_index, 0, keepdims=False)
            value = mine - jnp.where(flags[f], peer, 0.0)
            blocks.append(jnp.broadcast_to(value[:, None, :], (species, sizes[f], cases)))
        return jnp.concatenate(blocks, axis=1)

    def project(resid):
        sums = jnp.sum(resid, axis=1)
        all_sums = lax.all_gather(sums[None], ("col", "lay"), axis=0, tiled=True)
        coarse_y = coarse_solve(chol, all_sums)
        projected = resid - spread(coarse_y)
        energy = lax.psum(inner_local(projected, projected), ("col", "lay"))
        return (projected, energy)

    all_loads = lax.all_gather(load[None], ("col", "lay"), axis=0, tiled=True)
    multipliers = spread(coarse_solve(chol, all_loads))
    resid = assemble(gap - apply(multipliers))
    projected, energy = project(resid)
    direction = projected
    for step in range(ITERS):
        image = assemble(apply(direction))
        curvature = lax.psum(inner_local(direction, image), ("col", "lay"))
        alpha = energy / curvature
        multipliers = multipliers + alpha[:, None, :] * direction
        if step + 1 < ITERS:
            resid = resid - alpha[:, None, :] * image
            projected, new_energy = project(resid)
            direction = projected + (new_energy / energy)[:, None, :] * direction
            energy = new_energy
    return multipliers[None, None]


def solution(mesh):
    return jax.shard_map(
        shards,
        mesh=mesh,
        in_specs=(
            P("col", "lay", None, None, None),
            P("col", "lay", None),
            P("col", "lay", None, None, None),
            P("col", "lay", None, None),
        ),
        out_specs=P("col", "lay", None, None, None),
        check_vma=False,
    )
```

profile of v0, /device:TPU:1, one launch (start us, length us, event | category | flops | bytes accessed | tf_op | source)
XLA Modules:
  0.0 1142.6 jit_solution(5150536015416559685)
XLA Ops:
  7.3 11.7 %cholesky.49 = f32[128,128]{1,0:T(8,128)S(1)} custom-call(f32[128,128]{1,0:T(8,128)S(1)} %cholesky.115), custom_call_target="Cholesky" | custom-call | tf_op jit(solution)/shard_map/jit(cholesky)/cholesky | solution.py:74
  19.0 9.8 custom-call.17
  29.4 11.7 %cholesky.103 = f32[128,128]{1,0:T(8,128)S(1)} custom-call(f32[128,128]{1,0:T(8,128)S(1)} %convolution_subtract_fusion.8), custom_call_target="Cholesky" | custom-call | tf_op jit(solution)/shard_map/jit(cholesky)/cholesky | solution.py:74
  47.9 19.7 %custom-call.25 = f32[2,128,128]{1,2,0:T(8,128)S(1)} custom-call(f32[2,128,128]{2,1,0:T(8,128)S(1)} %get-tuple-element.63), custom_call_target="InvertDiagBlocksLowerTriangular" | custom-call | tf_op jit(solution)/shard_map/triangular_solve/custom-call.4 | solution.py:40
  67.6 73.1 %all-gather = f32[256,1,4,128]{3,2,1,0:T(4,128)S(1)} all-gather(f32[1,1,4,128]{3,2,1,0:T(4,128)S(1)} %copy-done.56), channel_id=2, replica_groups=mesh['col'=32,'lay'=8] {'col','lay'}, dimensions={0}, use_global_device_ids=true | all-gather | bytes 526336 | tf_op jit(solution)/shard_map/all_gather | solution.py:116
  161.0 7.9 gather_fusion.1
  216.6 81.0 %all-gather.4 = f32[256,4,128]{2,1,0:T(4,128)S(1)} all-gather(f32[1,4,128]{2,1,0:T(4,128)S(1)} %add_bitcast_fusion), channel_id=3, replica_groups=mesh['col'=32,'lay'=8] {'col','lay'}, dimensions={0}, use_global_device_ids=true | all-gather | bytes 526336 | tf_op jit(solution)/shard_map/all_gather | solution.py:110
  321.1 9.5 gather_fusion.3
  342.4 8.7 collective-permute-done.6
  356.9 14.0 %collective-permute-done.7 = f32[4,192,128]{2,0,1:T(4,128)S(1)} collective-permute-done((f32[4,192,128]{2,0,1:T(4,128)S(1)}, f32[4,192,128]{2,0,1:T(4,128)S(1)}, u32[]{:S(2)}, u32[]{:S(2)}) %collective-permute-start.7) | collective-permute-done | bytes 393248 | tf_op jit(solution)/shard_map/ppermute | solution.py:15
  384.9 91.5 %all-reduce.1 = (f32[4,128]{1,0:T(4,128)S(1)}, f32[4,128]{1,0:T(4,128)S(1)}) all-reduce(f32[4,128]{1,0:T(4,128)S(1)} %get-tuple-element.71, f32[4,128]{1,0:T(4,128)S(1)} %get-tuple-element.70), channel_id=1, replica_groups=mesh['col'=32,'lay'=8] {'col','lay'}, use_global_device_ids=true, to_apply=%region_12.16 | all-reduce | flops 1024 | bytes 8192 | tf_op jit(solution)/shard_map/psum | solution.py:113
  479.7 66.1 %all-gather.5 = f32[256,4,128]{2,1,0:T(4,128)S(1)} all-gather(f32[1,4,128]{2,1,0:T(4,128)S(1)} %bitcast.301), channel_id=4, replica_groups=mesh['col'=32,'lay'=8] {'col','lay'}, dimensions={0}, use_global_device_ids=true | all-gather | bytes 526336 | tf_op jit(solution)/shard_map/all_gather | solution.py:110
  553.0 74.5 %psum.44 = f32[4,128]{1,0:T(4,128)S(1)} all-reduce(f32[4,128]{1,0:T(4,128)S(1)} %get-tuple-element.96), channel_id=1, replica_groups=mesh['col'=32,'lay'=8] {'col','lay'}, use_global_device_ids=true, to_apply=%region_17.21 | all-reduce | flops 512 | bytes 4096 | tf_op jit(solution)/shard_map/psum | solution.py:113
  640.3 7.7 fusion.18
  650.9 9.5 gather_fusion.5
  676.1 12.6 %collective-permute-done.12 = f32[4,192,128]{2,0,1:T(4,128)S(1)} collective-permute-done((f32[4,192,128]{2,0,1:T(4,128)S(1)}, f32[4,192,128]{2,0,1:T(4,128)S(1)}, u32[]{:S(2)}, u32[]{:S(2)}) %collective-permute-start.12) | collective-permute-done | bytes 393248 | tf_op jit(solution)/shard_map/ppermute | solution.py:15
  694.1 11.8 %collective-permute-done.13 = f32[4,192,128]{2,0,1:T(4,128)S(1)} collective-permute-done((f32[4,192,128]{2,0,1:T(4,128)S(1)}, f32[4,192,128]{2,0,1:T(4,128)S(1)}, u32[]{:S(2)}, u32[]{:S(2)}) %collective-permute-start.13) | collective-permute-done | bytes 393248 | tf_op jit(solution)/shard_map/ppermute | solution.py:15
  718.7 88.3 %psum.45 = f32[4,128]{1,0:T(4,128)S(1)} all-reduce(f32[4,128]{1,0:T(4,128)S(1)} %multiply_reduce_fusion.1), channel_id=1, replica_groups=mesh['col'=32,'lay'=8] {'col','lay'}, use_global_device_ids=true, to_apply=%region_19.23 | all-reduce | flops 512 | bytes 4096 | tf_op jit(solution)/shard_map/psum | solution.py:123
  809.6 66.4 %all-gather.6 = f32[256,4,128]{2,1,0:T(4,128)S(1)} all-gather(f32[1,4,128]{2,1,0:T(4,128)S(1)} %bitcast.300), channel_id=5, replica_groups=mesh['col'=32,'lay'=8] {'col','lay'}, dimensions={0}, use_global_device_ids=true | all-gather | bytes 526336 | tf_op jit(solution)/shard_map/all_gather | solution.py:110
  884.1 74.9 %psum.46 = f32[4,128]{1,0:T(4,128)S(1)} all-reduce(f32[4,128]{1,0:T(4,128)S(1)} %get-tuple-element.82), channel_id=1, replica_groups=mesh['col'=32,'lay'=8] {'col','lay'}, use_global_device_ids=true, to_apply=%region_22.26 | all-reduce | flops 512 | bytes 4096 | tf_op jit(solution)/shard_map/psum | solution.py:113
  979.2 9.5 gather_fusion.7
  1001.9 14.5 %collective-permute-done.18 = f32[4,192,128]{2,0,1:T(4,128)S(1)} collective-permute-done((f32[4,192,128]{2,0,1:T(4,128)S(1)}, f32[4,192,128]{2,0,1:T(4,128)S(1)}, u32[]{:S(2)}, u32[]{:S(2)}) %collective-permute-start.18) | collective-permute-done | bytes 393248 | tf_op jit(solution)/shard_map/ppermute | solution.py:15
  1021.5 12.1 %collective-permute-done.19 = f32[4,192,128]{2,0,1:T(4,128)S(1)} collective-permute-done((f32[4,192,128]{2,0,1:T(4,128)S(1)}, f32[4,192,128]{2,0,1:T(4,128)S(1)}, u32[]{:S(2)}, u32[]{:S(2)}) %collective-permute-start.19) | collective-permute-done | bytes 393248 | tf_op jit(solution)/shard_map/ppermute | solution.py:15
  1045.2 89.0 %psum.47 = f32[4,128]{1,0:T(4,128)S(1)} all-reduce(f32[4,128]{1,0:T(4,128)S(1)} %multiply_reduce_fusion), channel_id=1, replica_groups=mesh['col'=32,'lay'=8] {'col','lay'}, use_global_device_ids=true, to_apply=%region_24.28 | all-reduce | flops 512 | bytes 4096 | tf_op jit(solution)/shard_map/psum | solution.py:123
  (371 shorter events, 267.4 us)
Async XLA Ops:
  177.4 26.9 %collective-permute-start = (f32[4,192,128]{2,0,1:T(4,128)}, f32[4,192,128]{2,0,1:T(4,128)}, u32[]{:S(2)}, u32[]{:S(2)}) collective-permute-start(f32[4,192,128]{2,0,1:T(4,128)} %get-tuple-element.124), channel_id=1, source_target_pairs={{0,32},{8,40},{16,48},{24,56},{32,64},{40,72},{48,80},{56,88},{64,... | collective-permute-start | bytes 1179656 | tf_op jit(solution)/shard_map/ppermute | solution.py:15
  183.3 28.2 %collective-permute-start.1 = (f32[4,192,128]{2,0,1:T(4,128)}, f32[4,192,128]{2,0,1:T(4,128)}, u32[]{:S(2)}, u32[]{:S(2)}) collective-permute-start(f32[4,192,128]{2,0,1:T(4,128)} %get-tuple-element.125), channel_id=1, source_target_pairs={{32,0},{40,8},{48,16},{56,24},{64,32},{72,40},{80,48},{88,56},{96,... | collective-permute-start | bytes 1179656 | tf_op jit(solution)/shard_map/ppermute | solution.py:15
  184.6 28.5 %collective-permute-start.2 = (f32[4,192,128]{2,0,1:T(4,128)S(1)}, f32[4,192,128]{2,0,1:T(4,128)}, u32[]{:S(2)}, u32[]{:S(2)}) collective-permute-start(f32[4,192,128]{2,0,1:T(4,128)S(1)} %get-tuple-element.123), channel_id=1, source_target_pairs={{0,8},{8,16},{16,24},{24,32},{32,40},{40,48},{48,56},{56,64},{64,7... | collective-permute-start | bytes 1179656 | tf_op jit(solution)/shard_map/ppermute | solution.py:15
  186.9 26.5 %collective-permute-start.3 = (f32[4,192,128]{2,0,1:T(4,128)S(1)}, f32[4,192,128]{2,0,1:T(4,128)}, u32[]{:S(2)}, u32[]{:S(2)}) collective-permute-start(f32[4,192,128]{2,0,1:T(4,128)S(1)} %get-tuple-element.122), channel_id=1, source_target_pairs={{8,0},{16,8},{24,16},{32,24},{40,32},{48,40},{56,48},{64,56},{72,6... | collective-permute-start | bytes 1179656 | tf_op jit(solution)/shard_map/ppermute | solution.py:15
  188.9 26.1 %collective-permute-start.4 = (f32[4,128,128]{2,0,1:T(4,128)}, f32[4,128,128]{2,0,1:T(4,128)}, u32[]{:S(2)}, u32[]{:S(2)}) collective-permute-start(f32[4,128,128]{2,0,1:T(4,128)} %get-tuple-element.121), channel_id=1, source_target_pairs={{0,1},{1,2},{2,3},{3,4},{4,5},{5,6},{6,7},{8,9},{9,10},{10,11},{11... | collective-permute-start | bytes 786440 | tf_op jit(solution)/shard_map/ppermute | solution.py:15
  204.3 12.0 %collective-permute-start.5 = (f32[4,128,128]{2,0,1:T(4,128)S(1)}, f32[4,128,128]{2,0,1:T(4,128)S(1)}, u32[]{:S(2)}, u32[]{:S(2)}) collective-permute-start(f32[4,128,128]{2,0,1:T(4,128)S(1)} %get-tuple-element.120), channel_id=1, source_target_pairs={{1,0},{2,1},{3,2},{4,3},{5,4},{6,5},{7,6},{9,8},{10,9},{11,10},{12... | collective-permute-start | bytes 786440 | tf_op jit(solution)/shard_map/ppermute | solution.py:15
  336.2 14.8 %collective-permute-start.6 = (f32[4,192,128]{2,0,1:T(4,128)S(1)}, f32[4,192,128]{2,0,1:T(4,128)S(1)}, u32[]{:S(2)}, u32[]{:S(2)}) collective-permute-start(f32[4,192,128]{2,0,1:T(4,128)S(1)} %slice.292), channel_id=1, source_target_pairs={{0,32},{8,40},{16,48},{24,56},{32,64},{40,72},{48,80},{56,88},{64,... | collective-permute-start | bytes 1179656 | tf_op jit(solution)/shard_map/ppermute | solution.py:15
  339.4 34.0 %collective-permute-start.10 = (f32[4,128,128]{2,0,1:T(4,128)S(1)}, f32[4,128,128]{2,0,1:T(4,128)S(1)}, u32[]{:S(2)}, u32[]{:S(2)}) collective-permute-start(f32[4,128,128]{2,0,1:T(4,128)S(1)} %slice.296), channel_id=1, source_target_pairs={{0,1},{1,2},{2,3},{3,4},{4,5},{5,6},{6,7},{8,9},{9,10},{10,11},{11... | collective-permute-start | bytes 786440 | tf_op jit(solution)/shard_map/ppermute | solution.py:15
  351.3 19.6 %collective-permute-start.7 = (f32[4,192,128]{2,0,1:T(4,128)S(1)}, f32[4,192,128]{2,0,1:T(4,128)S(1)}, u32[]{:S(2)}, u32[]{:S(2)}) collective-permute-start(f32[4,192,128]{2,0,1:T(4,128)S(1)} %get-tuple-element.119), channel_id=1, source_target_pairs={{32,0},{40,8},{48,16},{56,24},{64,32},{72,40},{80,48},{88,56},{96,... | collective-permute-start | bytes 1179656 | tf_op jit(solution)/shard_map/ppermute | solution.py:15
  352.7 18.4 %collective-permute-start.8 = (f32[4,192,128]{2,0,1:T(4,128)S(1)}, f32[4,192,128]{2,0,1:T(4,128)S(1)}, u32[]{:S(2)}, u32[]{:S(2)}) collective-permute-start(f32[4,192,128]{2,0,1:T(4,128)S(1)} %get-tuple-element.118), channel_id=1, source_target_pairs={{0,8},{8,16},{16,24},{24,32},{32,40},{40,48},{48,56},{56,64},{64,7... | collective-permute-start | bytes 1179656 | tf_op jit(solution)/shard_map/ppermute | solution.py:15
  355.3 17.9 %collective-permute-start.9 = (f32[4,192,128]{2,0,1:T(4,128)S(1)}, f32[4,192,128]{2,0,1:T(4,128)S(1)}, u32[]{:S(2)}, u32[]{:S(2)}) collective-permute-start(f32[4,192,128]{2,0,1:T(4,128)S(1)} %get-tuple-element.116), channel_id=1, source_target_pairs={{8,0},{16,8},{24,16},{32,24},{40,32},{48,40},{56,48},{64,56},{72,6... | collective-permute-start | bytes 1179656 | tf_op jit(solution)/shard_map/ppermute | solution.py:15
  373.5 8.3 collective-permute-start.11
  666.1 22.6 %collective-permute-start.12 = (f32[4,192,128]{2,0,1:T(4,128)S(1)}, f32[4,192,128]{2,0,1:T(4,128)S(1)}, u32[]{:S(2)}, u32[]{:S(2)}) collective-permute-start(f32[4,192,128]{2,0,1:T(4,128)S(1)} %slice.300), channel_id=1, source_target_pairs={{0,32},{8,40},{16,48},{24,56},{32,64},{40,72},{48,80},{56,88},{64,... | collective-permute-start | bytes 1179656 | tf_op jit(solution)/shard_map/ppermute | solution.py:15
  671.4 35.0 %collective-permute-start.16 = (f32[4,128,128]{2,0,1:T(4,128)S(1)}, f32[4,128,128]{2,0,1:T(4,128)S(1)}, u32[]{:S(2)}, u32[]{:S(2)}) collective-permute-start(f32[4,128,128]{2,0,1:T(4,128)S(1)} %slice.304), channel_id=1, source_target_pairs={{0,1},{1,2},{2,3},{3,4},{4,5},{5,6},{6,7},{8,9},{9,10},{10,11},{11... | collective-permute-start | bytes 786440 | tf_op jit(solution)/shard_map/ppermute | solution.py:15
  688.9 17.0 %collective-permute-start.13 = (f32[4,192,128]{2,0,1:T(4,128)S(1)}, f32[4,192,128]{2,0,1:T(4,128)S(1)}, u32[]{:S(2)}, u32[]{:S(2)}) collective-permute-start(f32[4,192,128]{2,0,1:T(4,128)S(1)} %get-tuple-element.113), channel_id=1, source_target_pairs={{32,0},{40,8},{48,16},{56,24},{64,32},{72,40},{80,48},{88,56},{96,... | collective-permute-start | bytes 1179656 | tf_op jit(solution)/shard_map/ppermute | solution.py:15
  690.3 15.8 %collective-permute-start.14 = (f32[4,192,128]{2,0,1:T(4,128)S(1)}, f32[4,192,128]{2,0,1:T(4,128)S(1)}, u32[]{:S(2)}, u32[]{:S(2)}) collective-permute-start(f32[4,192,128]{2,0,1:T(4,128)S(1)} %get-tuple-element.112), channel_id=1, source_target_pairs={{0,8},{8,16},{16,24},{24,32},{32,40},{40,48},{48,56},{56,64},{64,7... | collective-permute-start | bytes 1179656 | tf_op jit(solution)/shard_map/ppermute | solution.py:15
  692.7 13.6 %collective-permute-start.15 = (f32[4,192,128]{2,0,1:T(4,128)S(1)}, f32[4,192,128]{2,0,1:T(4,128)S(1)}, u32[]{:S(2)}, u32[]{:S(2)}) collective-permute-start(f32[4,192,128]{2,0,1:T(4,128)S(1)} %get-tuple-element.110), channel_id=1, source_target_pairs={{8,0},{16,8},{24,16},{32,24},{40,32},{48,40},{56,48},{64,56},{72,6... | collective-permute-start | bytes 1179656 | tf_op jit(solution)/shard_map/ppermute | solution.py:15
  706.6 7.7 collective-permute-start.17
  994.3 22.1 %collective-permute-start.18 = (f32[4,192,128]{2,0,1:T(4,128)S(1)}, f32[4,192,128]{2,0,1:T(4,128)S(1)}, u32[]{:S(2)}, u32[]{:S(2)}) collective-permute-start(f32[4,192,128]{2,0,1:T(4,128)S(1)} %slice.308), channel_id=1, source_target_pairs={{0,32},{8,40},{16,48},{24,56},{32,64},{40,72},{48,80},{56,88},{64,... | collective-permute-start | bytes 1179656 | tf_op jit(solution)/shard_map/ppermute | solution.py:15
  999.2 35.0 %collective-permute-start.22 = (f32[4,128,128]{2,0,1:T(4,128)S(1)}, f32[4,128,128]{2,0,1:T(4,128)S(1)}, u32[]{:S(2)}, u32[]{:S(2)}) collective-permute-start(f32[4,128,128]{2,0,1:T(4,128)S(1)} %slice.312), channel_id=1, source_target_pairs={{0,1},{1,2},{2,3},{3,4},{4,5},{5,6},{6,7},{8,9},{9,10},{10,11},{11... | collective-permute-start | bytes 786440 | tf_op jit(solution)/shard_map/ppermute | solution.py:15
  1016.6 17.1 %collective-permute-start.19 = (f32[4,192,128]{2,0,1:T(4,128)S(1)}, f32[4,192,128]{2,0,1:T(4,128)S(1)}, u32[]{:S(2)}, u32[]{:S(2)}) collective-permute-start(f32[4,192,128]{2,0,1:T(4,128)S(1)} %get-tuple-element.107), channel_id=1, source_target_pairs={{32,0},{40,8},{48,16},{56,24},{64,32},{72,40},{80,48},{88,56},{96,... | collective-permute-start | bytes 1179656 | tf_op jit(solution)/shard_map/ppermute | solution.py:15
  1018.0 15.9 %collective-permute-start.20 = (f32[4,192,128]{2,0,1:T(4,128)S(1)}, f32[4,192,128]{2,0,1:T(4,128)S(1)}, u32[]{:S(2)}, u32[]{:S(2)}) collective-permute-start(f32[4,192,128]{2,0,1:T(4,128)S(1)} %get-tuple-element.106), channel_id=1, source_target_pairs={{0,8},{8,16},{16,24},{24,32},{32,40},{40,48},{48,56},{56,64},{64,7... | collective-permute-start | bytes 1179656 | tf_op jit(solution)/shard_map/ppermute | solution.py:15
  1020.2 13.8 %collective-permute-start.21 = (f32[4,192,128]{2,0,1:T(4,128)S(1)}, f32[4,192,128]{2,0,1:T(4,128)S(1)}, u32[]{:S(2)}, u32[]{:S(2)}) collective-permute-start(f32[4,192,128]{2,0,1:T(4,128)S(1)} %get-tuple-element.104), channel_id=1, source_target_pairs={{8,0},{16,8},{24,16},{32,24},{40,32},{48,40},{56,48},{64,56},{72,6... | collective-permute-start | bytes 1179656 | tf_op jit(solution)/shard_map/ppermute | solution.py:15
  1034.4 7.7 collective-permute-start.23
  (57 other events, 1408.8 us)
where the time goes:
time: 1150 us; the launch traced here: 1140 us
  blocking collectives  705 us (61%)
  other arithmetic  152 us (13%)
  waiting for transfers between devices  89.4 us (8%)
  local copies, waits for them, and re-layouts  89.2 us (8%)
  starting transfers between devices  63.5 us (6%)
  matrix products  40.4 us (4%)
    psum x3, blocking collectives, project(): energy = lax.psum(inner_local(projected, projected), ('col', 'lay'))  241 us
    all_gather x3, blocking collectives, project(): all_sums = lax.all_gather(sums[None], ('col', 'lay'), axis=0, tiled=True)  213 us
    psum x2, blocking collectives, shards(): curvature = lax.psum(inner_local(direction, image), ('col', 'lay'))  177 us
    ppermute x24, waiting for transfers between devices, passed_along(): lax.ppermute(value, axis, [(source, source + steps) for source in range(l...  89.4 us
    all_gather x1, blocking collectives, shards(): all_loads = lax.all_gather(load[None], ('col', 'lay'), axis=0, tiled=True)  73.1 us
    ppermute x24, starting transfers between devices, passed_along(): lax.ppermute(value, axis, [(source, source + steps) for source in range(l...  63.5 us
    gather x4, local copies, waits for them, and re-layouts, apply(): return jnp.take(image, inverse, axis=1)  36.4 us
    another operation x7, other arithmetic, shards(): jnp.linalg.cholesky(coarse_matrix(xcount, YCOLS, nlay, FACE_SIDE, FACE_TOP))  34.6 us
  transfers between devices with their start and end apart: 24, of which 11 were waited for; matrix products, arithmetic and copies ran while one was open for 2% of the time, Pallas kernels for 0%

commit v1 on v0

v1 whole, which is shorter than its diff:
```python
import functools

import jax
import jax.numpy as jnp
import numpy as np
from jax import lax
from jax.experimental import pallas as pl
from jax.experimental.pallas import tpu as pltpu
from jax.sharding import PartitionSpec as P

SIDE = 192
TOP = 128
YCOLS = 4
SPECIES = 4
CASES = 128
M = 1024
NCOL = 32
NLAY = 8
COUNT = NCOL * NLAY
SIZES = (SIDE, SIDE, SIDE, SIDE, TOP, TOP)
STARTS = (0, 192, 384, 576, 768, 896)
TAILS = (16, 16, 16, 16, 8, 8)
CHUNK = 256
F32 = jnp.float32
BF16 = jnp.bfloat16
VMEM_LIMIT = 44 * 1024 * 1024


def coarse_inverse():
    index = np.arange(COUNT)
    zpos, cpos = index % NLAY, index // NLAY
    ypos, xpos = cpos % YCOLS, cpos // YCOLS
    dx = np.abs(xpos[:, None] - xpos[None, :])
    dy = np.abs(ypos[:, None] - ypos[None, :])
    dz = np.abs(zpos[:, None] - zpos[None, :])
    lateral = (dx + dy == 1) & (dz == 0)
    upward = (dx + dy == 0) & (dz == 1)
    matrix = M * np.eye(COUNT) - SIDE * lateral - TOP * upward
    return np.linalg.inv(matrix).astype(np.float32)


def params():
    return pltpu.CompilerParams(
        dimension_semantics=("arbitrary",), vmem_limit_bytes=VMEM_LIMIT
    )


def cost(flops, nbytes):
    return pl.CostEstimate(flops=int(flops), bytes_accessed=int(nbytes), transcendentals=0)


SMEM = pl.BlockSpec(memory_space=pltpu.SMEM)


def per_species(*shape):
    zeros = (0,) * len(shape)
    return pl.BlockSpec((1,) + shape, lambda k: (k,) + zeros)


def whole(*shape):
    zeros = (0,) * len(shape)
    return pl.BlockSpec(shape, lambda k: zeros)


def even(*shape):
    zeros = (0,) * len(shape)
    return pl.BlockSpec((1,) + shape, lambda k: (2 * k,) + zeros)


def pair(*shape):
    zeros = (0,) * len(shape)
    return pl.BlockSpec((2,) + shape, lambda k: (k,) + zeros)


def out(shape, dtype=F32):
    return jax.ShapeDtypeStruct(shape, dtype)


def exact_dot(a, b, dims):
    return lax.dot_general(
        a, b, (dims, ((), ())), precision=lax.Precision.HIGHEST, preferred_element_type=F32
    )


def prep_kernel(row_ref, col_ref, flux_ref, gap_ref, load_ref, *outs):
    o_ref, ot_ref, rt_ref, msg_ref = outs[:4]
    face_refs = outs[4:]
    row = row_ref[...]

    @pl.when(pl.program_id(0) == 0)
    def _():
        for i in range(0, M, CHUNK):
            lanes = lax.broadcasted_iota(jnp.int32, (CHUNK, M), 1)
            hit = col_ref[i : i + CHUNK, :] == lanes
            o_ref[i : i + CHUNK, :] = jnp.where(hit, 1.0, 0.0).astype(BF16)
            rows = lax.broadcasted_iota(jnp.int32, (CHUNK, M), 0) + i
            ot_ref[i : i + CHUNK, :] = jnp.where(row == rows, 1.0, 0.0).astype(BF16)

    face = lax.broadcasted_iota(jnp.int32, (16, M), 0)
    low = jnp.where(face <= 4, SIDE * face, jnp.where(face == 5, STARTS[5], M))
    high = jnp.where(face <= 3, SIDE * (face + 1), jnp.where(face == 4, STARTS[5], M))
    member = jnp.where((row >= low) & (row < high), 1.0, 0.0).astype(BF16)
    sums = lax.dot_general(
        member, flux_ref[0], (((1,), (1,)), ((), ())), preferred_element_type=F32
    )
    first = sums.astype(BF16)
    rest = sums - first.astype(F32)
    second = rest.astype(BF16)
    third = (rest - second.astype(F32)).astype(BF16)
    o = o_ref[...]
    rt = jnp.dot(first, o, preferred_element_type=F32)
    rt = rt + jnp.dot(second, o, preferred_element_type=F32)
    rt = rt + jnp.dot(third, o, preferred_element_type=F32)
    rt = rt[:8]
    rt_ref[0] = rt

    lane = lax.broadcasted_iota(jnp.int32, (8, M), 1)
    slot = lax.broadcasted_iota(jnp.int32, (8, CASES), 1)
    peer = lax.broadcasted_iota(jnp.int32, (8, CASES), 0)
    table = jnp.zeros((8, CASES), F32)
    for f in range(6):
        inside = (lane >= STARTS[f]) & (lane < STARTS[f] + SIZES[f])
        total = jnp.sum(jnp.where(inside, rt, 0.0), axis=1, keepdims=True)
        here = (slot == 6 * f + peer) & (peer < 6)
        table = table + jnp.where(here, total, 0.0)
    rows = [
        jnp.sum(gap_ref[0, STARTS[f] : STARTS[f] + SIZES[f], :], axis=0, keepdims=True)
        for f in range(6)
    ]
    rows.append(load_ref[0])
    rows.append(jnp.sum(table, axis=0, keepdims=True))
    for r in range(8):
        msg_ref[0, r : r + 1, :] = rows[r]
        msg_ref[1, r : r + 1, :] = rows[r]

    for f in range(6):
        size = SIZES[f]
        face_refs[f][0, :size, :] = gap_ref[0, STARTS[f] : STARTS[f] + size, :]
        turned = rt if STARTS[f] == 0 else pltpu.roll(rt, M - STARTS[f], 1)
        face_refs[f][0, size : size + 8, :] = turned[:, :CASES]
        if size > CASES:
            face_refs[f][0, size + 8 : size + 16, :] = turned[:, CASES : 2 * CASES]


def prep(order, flux, gap, load):
    faces = [(SPECIES, SIZES[f] + TAILS[f], CASES) for f in range(6)]
    return pl.pallas_call(
        prep_kernel,
        grid=(SPECIES,),
        in_specs=[
            whole(1, M),
            whole(M, 1),
            per_species(M, M),
            per_species(M, CASES),
            per_species(1, CASES),
        ],
        out_specs=[whole(M, M), whole(M, M), per_species(8, M), pair(8, CASES)]
        + [per_species(*shape[1:]) for shape in faces],
        out_shape=[
            out((M, M), BF16),
            out((M, M), BF16),
            out((SPECIES, 8, M)),
            out((8, 8, CASES)),
        ]
        + [out(shape) for shape in faces],
        compiler_params=params(),
        cost_estimate=cost(1e9, 20e6),
        name="prep",
    )(order.reshape(1, M), order.reshape(M, 1), flux, gap, load.reshape(SPECIES, 1, CASES))


def shifted(value, f):
    row = lax.broadcasted_iota(jnp.int32, value.shape, 0)
    zpos = row % NLAY
    ypos = (row // NLAY) % YCOLS
    xpos = row // (NLAY * YCOLS)
    step, ok = (
        (NLAY * YCOLS, xpos > 0),
        (-NLAY * YCOLS, xpos < NCOL // YCOLS - 1),
        (NLAY, ypos > 0),
        (-NLAY, ypos < YCOLS - 1),
        (1, zpos > 0),
        (-1, zpos < NLAY - 1),
    )[f]
    return jnp.where(ok, pltpu.roll(value, step % COUNT, 0), 0.0)


def solve0_kernel(info_ref, inv_ref, gathered_ref, out_ref, vals_ref):
    col = info_ref[0]

    def rows(r):
        return gathered_ref[:, r].reshape(COUNT, CASES)

    inv = inv_ref[...]
    y0 = exact_dot(inv, rows(6), ((1,), (0,)))
    vals = [y0 - shifted(y0, f) for f in range(6)]
    rounded = [v.astype(BF16).astype(F32) for v in vals]
    table = rows(7)
    tau = []
    for f in range(6):
        total = rows(f)
        for g in range(6):
            total = total - table[:, 6 * f + g : 6 * f + g + 1] * rounded[g]
        tau.append(total)
    h = jnp.zeros((COUNT, CASES), F32)
    for f in range(6):
        h = h + (tau[f] - shifted(tau[f ^ 1], f))
    y1 = exact_dot(inv, h, ((1,), (0,)))
    here = pl.ds(pl.multiple_of(col * NLAY, NLAY), NLAY)
    zero = jnp.zeros((NLAY, CASES), F32)
    for f in range(6):
        vals_ref[0] = y1 - shifted(y1, f)
        out_ref[:, f, :] = vals_ref[0, here, :]
    for f in range(6):
        vals_ref[f] = vals[f]
    for g in range(6):
        out_ref[:, 8 + g, :] = vals_ref[g, here, :]
    for f in range(4):
        away = jnp.clip(col + (-YCOLS, YCOLS, -1, 1)[f], 0, NCOL - 1)
        there = pl.ds(pl.multiple_of(away * NLAY, NLAY), NLAY)
        for g in range(6):
            out_ref[:, 16 + 8 * f + g, :] = vals_ref[g, there, :]
    for f in (4, 5):
        for g in range(6):
            out_ref[:, 16 + 8 * f + g, :] = pltpu.roll(
                vals_ref[g, here, :], (1, NLAY - 1)[f - 4], 0
            )
    for group in range(8):
        out_ref[:, 8 * group + 6, :] = zero
        out_ref[:, 8 * group + 7, :] = zero


def solve0(info, inverse, gathered):
    return pl.pallas_call(
        solve0_kernel,
        in_specs=[SMEM, pl.BlockSpec(memory_space=pltpu.VMEM), pl.BlockSpec(memory_space=pltpu.VMEM)],
        out_specs=pl.BlockSpec(memory_space=pltpu.VMEM),
        out_shape=out((8, 64, CASES)),
        scratch_shapes=[pltpu.VMEM((6, COUNT, CASES), F32)],
        compiler_params=pltpu.CompilerParams(vmem_limit_bytes=VMEM_LIMIT),
        cost_estimate=cost(1e8, 2e6),
        name="solve_start",
    )(info, inverse, gathered)


def mid_kernel(got_ref, out_ref):
    total = got_ref[0]
    top = got_ref[0, 5:6, :]
    for l in range(1, NLAY):
        total = total + got_ref[l]
        top = jnp.maximum(top, got_ref[l, 5:6, :])
    qq = jnp.zeros((1, CASES), F32)
    for l in range(NLAY):
        part = got_ref[l, 5:6, :] / top
        qq = qq + got_ref[l, 2:3, :] * (part * part)
    row = lax.broadcasted_iota(jnp.int32, (8, CASES), 0)
    dots = jnp.where(row == 2, qq, jnp.where(row == 5, top, total))
    heads = jnp.concatenate([got_ref[l, 0:1, :] for l in range(NLAY)], axis=0)
    for c in range(NCOL):
        out_ref[c, 0:8, :] = heads
        out_ref[c, 8:16, :] = dots


def mid(got):
    return pl.pallas_call(
        mid_kernel,
        in_specs=[pl.BlockSpec(memory_space=pltpu.VMEM)],
        out_specs=pl.BlockSpec(memory_space=pltpu.VMEM),
        out_shape=out((NCOL, 16, CASES)),
        cost_estimate=cost(1e5, 3e5),
        name="combine_layers",
    )(got)


def solve_kernel(info_ref, inv_ref, gathered_ref, out_ref, y_ref):
    col = info_ref[0]
    dots = jnp.sum(gathered_ref[:, 8:16, :], axis=0)
    tops = gathered_ref[:, 13, :]
    top = jnp.max(tops, axis=0, keepdims=True)
    part = tops / top
    qq = jnp.sum(gathered_ref[:, 10, :] * (part * part), axis=0, keepdims=True)
    h = gathered_ref[:, 0:8, :].reshape(COUNT, CASES) / top
    y = exact_dot(inv_ref[...], h, ((1,), (0,)))
    hy = jnp.sum(h * y, axis=0, keepdims=True)
    pq, wq, energy = dots[1:2], dots[3:4], dots[4:5]
    alpha = energy / pq
    scaled = alpha * top
    new = energy - 2.0 * (alpha * wq) + (scaled * scaled) * (qq - hy)
    beta = new / energy
    y = y * top
    here = pl.ds(pl.multiple_of(col * NLAY, NLAY), NLAY)
    for f in range(6):
        y_ref[...] = y - shifted(y, f)
        out_ref[:, f, :] = y_ref[here, :]
    out_ref[:, 6, :] = jnp.broadcast_to(alpha, (NLAY, CASES))
    out_ref[:, 7, :] = jnp.broadcast_to(beta, (NLAY, CASES))


def solve(info, inverse, gathered):
    return pl.pallas_call(
        solve_kernel,
        in_specs=[SMEM, pl.BlockSpec(memory_space=pltpu.VMEM), pl.BlockSpec(memory_space=pltpu.VMEM)],
        out_specs=pl.BlockSpec(memory_space=pltpu.VMEM),
        out_shape=out((8, 8, CASES)),
        scratch_shapes=[pltpu.VMEM((COUNT, CASES), F32)],
        cost_estimate=cost(1e8, 1e6),
        name="solve_step",
    )(info, inverse, gathered)


def apply_to(vector, o_ref, ot_ref, flux_ref, first_ref, second_ref):
    first_ref[...] = vector.astype(BF16)

    def gather(i, _):
        here = pl.ds(pl.multiple_of(i * CHUNK, CHUNK), CHUNK)
        moved = jnp.dot(o_ref[here, :], first_ref[...], preferred_element_type=F32)
        second_ref[here, :CASES] = moved.astype(BF16)
        return 0

    lax.fori_loop(0, M // CHUNK, gather, 0)
    first_ref[...] = second_ref[:, :CASES]

    def image(i, _):
        here = pl.ds(pl.multiple_of(i * CHUNK, CHUNK), CHUNK)
        part = jnp.dot(flux_ref[0, here, :], first_ref[...], preferred_element_type=F32)
        high = part.astype(BF16)
        second_ref[here, :CASES] = high
        second_ref[here, CASES:] = (part - high.astype(F32)).astype(BF16)
        return 0

    lax.fori_loop(0, M // CHUNK, image, 0)

    def back(start, size):
        both = jnp.dot(
            ot_ref[start : start + size, :], second_ref[...], preferred_element_type=F32
        )
        return both[:, :CASES] + both[:, CASES:]

    return back


def start_kernel(gap_ref, rt_ref, back_ref, o_ref, ot_ref, flux_ref, *refs):
    arrived = refs[:6]
    p_ref = refs[6]
    faces = refs[7:13]
    first_ref, second_ref = refs[13:]
    mine = back_ref[0, 8:16, :].astype(BF16).astype(F32)
    own = exact_dot(rt_ref[0], mine, ((0,), (0,)))
    for f in range(6):
        start, size = STARTS[f], SIZES[f]
        theirs = back_ref[0, 16 + 8 * f : 24 + 8 * f, :].astype(BF16).astype(F32)
        other = exact_dot(arrived[f][0, size : size + 8, :], theirs, ((0,), (0,)))
        if size > CASES:
            more = exact_dot(arrived[f][0, size + 8 : size + 16, :], theirs, ((0,), (0,)))
            other = jnp.concatenate([other, more[: size - CASES]], axis=0)
        resid = (gap_ref[0, start : start + size, :] - own[start : start + size]) - (
            arrived[f][0, :size, :] - other
        )
        p_ref[0, start : start + size, :] = resid - back_ref[0, f : f + 1, :]
    back = apply_to(p_ref[0], o_ref, ot_ref, flux_ref, first_ref, second_ref)
    for f in range(6):
        faces[f][0] = back(STARTS[f], SIZES[f])


VECTOR = (SPECIES, M, CASES)
FACES = [(SPECIES, size, CASES) for size in SIZES]
SCRATCH = [pltpu.VMEM((M, CASES), BF16), pltpu.VMEM((M, 2 * CASES), BF16)]


def start(gap, rt, back, o, ot, flux, arrived):
    return pl.pallas_call(
        start_kernel,
        grid=(SPECIES,),
        in_specs=[
            per_species(M, CASES),
            per_species(8, M),
            even(64, CASES),
            whole(M, M),
            whole(M, M),
            per_species(M, M),
        ]
        + [per_species(SIZES[f] + TAILS[f], CASES) for f in range(6)],
        out_specs=[per_species(M, CASES)] + [per_species(s, CASES) for s in SIZES],
        out_shape=[out(VECTOR)] + [out(shape) for shape in FACES],
        scratch_shapes=SCRATCH,
        compiler_params=params(),
        cost_estimate=cost(4e9, 20e6),
        name="start",
    )(gap, rt, back, o, ot, flux, *arrived)


def weights(info_ref):
    col, lay = info_ref[0], info_ref[1]
    xpos, ypos = col // YCOLS, col % YCOLS
    flags = [
        xpos > 0,
        xpos < NCOL // YCOLS - 1,
        ypos > 0,
        ypos < YCOLS - 1,
        lay > 0,
        lay < NLAY - 1,
    ]
    return [jnp.where(flag, 0.5, 1.0).astype(F32) for flag in flags]


def dots_kernel(same, info_ref, *refs):
    count = 1 if same else 2
    p_ref = refs[0]
    w_ref = refs[count - 1]
    faces = refs[count : count + 6]
    arrived = refs[count + 6 : count + 12]
    q_ref, msg_ref = refs[count + 12 :]
    weight = weights(info_ref)
    top = jnp.zeros((1, CASES), F32)
    for f in range(6):
        q = faces[f][0] - arrived[f][0]
        q_ref[0, STARTS[f] : STARTS[f] + SIZES[f], :] = q
        top = jnp.maximum(top, jnp.max(jnp.abs(q), axis=0, keepdims=True))
    top = jnp.where(top > 0.0, top, 1e-30)
    head, pq, qq, wq, ww = [jnp.zeros((1, CASES), F32) for _ in range(5)]

    def total(value):
        return jnp.sum(value, axis=0, keepdims=True)

    for f in range(6):
        here = slice(STARTS[f], STARTS[f] + SIZES[f])
        q = q_ref[0, here, :]
        p = p_ref[0, here, :]
        unit = q / top
        head = head + total(q)
        pq = pq + weight[f] * total(p * q)
        qq = qq + weight[f] * total(unit * unit)
        if same:
            ww = ww + weight[f] * total(p * p)
        else:
            w = w_ref[0, here, :]
            wq = wq + weight[f] * total(w * q)
            ww = ww + weight[f] * total(w * w)
    if same:
        wq = pq
    zero = jnp.zeros((1, CASES), F32)
    rows = (head, pq, qq, wq, ww, top, zero, zero)
    for r in range(8):
        msg_ref[0, r : r + 1, :] = rows[r]
        msg_ref[1, r : r + 1, :] = rows[r]


def dots(info, vectors, faces, arrived):
    same = len(vectors) == 1
    return pl.pallas_call(
        functools.partial(dots_kernel, same),
        grid=(SPECIES,),
        in_specs=[SMEM]
        + [per_species(M, CASES)] * len(vectors)
        + [per_species(s, CASES) for s in SIZES] * 2,
        out_specs=[per_species(M, CASES), pair(8, CASES)],
        out_shape=[out(VECTOR), out((8, 8, CASES))],
        compiler_params=params(),
        cost_estimate=cost(1e7, 10e6),
        name="dots",
    )(info, *vectors, *faces, *arrived)


def step_kernel(same, last, info_ref, back_ref, o_ref, ot_ref, flux_ref, *refs):
    count = 1 if same else 2
    p_ref = refs[0]
    w_ref = refs[count - 1]
    q_ref = refs[count]
    outs = refs[count + 1 : -2]
    first_ref, second_ref = refs[-2:]
    alpha = back_ref[0, 6:7, :]
    beta = back_ref[0, 7:8, :]
    weight = weights(info_ref)
    pnew_ref = outs[0]
    ww = jnp.zeros((1, CASES), F32)
    for f in range(6):
        here = slice(STARTS[f], STARTS[f] + SIZES[f])
        w = w_ref[0, here, :] - alpha * (q_ref[0, here, :] - back_ref[0, f : f + 1, :])
        if last:
            ww = ww + weight[f] * jnp.sum(w * w, axis=0, keepdims=True)
        else:
            outs[1][0, here, :] = w
        pnew_ref[0, here, :] = w + beta * p_ref[0, here, :]
    back = apply_to(pnew_ref[0], o_ref, ot_ref, flux_ref, first_ref, second_ref)
    if not last:
        for f in range(6):
            outs[2 + f][0] = back(STARTS[f], SIZES[f])
        return
    pq = jnp.zeros((1, CASES), F32)
    for i in range(0, M, CHUNK):
        g = back(i, CHUNK)
        pq = pq + jnp.sum(pnew_ref[0, i : i + CHUNK, :] * g, axis=0, keepdims=True)
    k = pl.program_id(0)
    msg_ref = outs[1]
    row = lax.broadcasted_iota(jnp.int32, (NLAY, 8, CASES), 1)
    held = msg_ref[...]
    held = jnp.where(row == k, pq[None], held)
    held = jnp.where(row == k + SPECIES, ww[None], held)
    msg_ref[...] = held


def step(info, back, o, ot, flux, vectors, q, last):
    same = len(vectors) == 1
    out_specs = [per_species(M, CASES)]
    out_shape = [out(VECTOR)]
    if last:
        out_specs += [whole(NLAY, 8, CASES)]
        out_shape += [out((NLAY, 8, CASES))]
    else:
        out_specs += [per_species(M, CASES)] + [per_species(s, CASES) for s in SIZES]
        out_shape += [out(VECTOR)] + [out(shape) for shape in FACES]
    return pl.pallas_call(
        functools.partial(step_kernel, same, last),
        grid=(SPECIES,),
        in_specs=[SMEM, even(8, CASES), whole(M, M), whole(M, M), per_species(M, M)]
        + [per_species(M, CASES)] * (len(vectors) + 1),
        out_specs=out_specs,
        out_shape=out_shape,
        scratch_shapes=SCRATCH,
        compiler_params=params(),
        cost_estimate=cost(4e9, 20e6),
        name="step",
    )(info, back, o, ot, flux, *vectors, q)


def finish_kernel(first_ref, back0_ref, back1_ref, sums_ref, p0_ref, p1_ref, p2_ref, out_ref):
    k = pl.program_id(0)
    sums = jnp.sum(sums_ref[...], axis=0)
    row = lax.broadcasted_iota(jnp.int32, (8, CASES), 0)
    pq = jnp.sum(jnp.where(row == k, sums, 0.0), axis=0, keepdims=True)
    ww = jnp.sum(jnp.where(row == k + SPECIES, sums, 0.0), axis=0, keepdims=True)
    alpha0 = back0_ref[0, 6:7, :]
    alpha1 = back1_ref[0, 6:7, :]
    alpha2 = ww / pq
    for f in range(6):
        here = slice(STARTS[f], STARTS[f] + SIZES[f])
        value = first_ref[0, 8 + f : 9 + f, :] + alpha0 * p0_ref[0, here, :]
        value = value + alpha1 * p1_ref[0, here, :]
        out_ref[0, here, :] = value + alpha2 * p2_ref[0, here, :]


def finish(first, back0, back1, sums, p0, p1, p2):
    return pl.pallas_call(
        finish_kernel,
        grid=(SPECIES,),
        in_specs=[even(64, CASES), even(8, CASES), even(8, CASES), whole(NCOL, 8, CASES)]
        + [per_species(M, CASES)] * 3,
        out_specs=per_species(M, CASES),
        out_shape=out(VECTOR),
        compiler_params=params(),
        cost_estimate=cost(1e7, 8e6),
        name="finish",
    )(first, back0, back1, sums, p0, p1, p2)


def exchange(blocks):
    def moved(value, axis, pairs):
        return lax.ppermute(value, axis, pairs)

    def along_x(step):
        return [(c, c + step) for c in range(NCOL) if 0 <= c + step < NCOL]

    def along_y(step):
        return [(c, c + step) for c in range(NCOL) if 0 <= c % YCOLS + step < YCOLS]

    def along_z(step):
        return [(l, l + step) for l in range(NLAY) if 0 <= l + step < NLAY]

    return [
        moved(blocks[1], "col", along_x(YCOLS)),
        moved(blocks[0], "col", along_x(-YCOLS)),
        moved(blocks[3], "col", along_y(1)),
        moved(blocks[2], "col", along_y(-1)),
        moved(blocks[5], "lay", along_z(1)),
        moved(blocks[4], "lay", along_z(-1)),
    ]


def swap(value, axis):
    return lax.all_to_all(value, axis, 0, 0, tiled=True)


def to_columns(value):
    return swap(jnp.broadcast_to(value[None], (NCOL,) + value.shape), "col")


def shards(flux_operator, dof_order, local_gap, rigid_load):
    flux = flux_operator[0, 0]
    order = dof_order[0, 0]
    gap = local_gap[0, 0]
    load = rigid_load[0, 0]
    info = jnp.stack([lax.axis_index("col"), lax.axis_index("lay")]).astype(jnp.int32)
    inverse = jnp.asarray(coarse_inverse())

    o, ot, rt, message, *faces = prep(order, flux, gap, load)
    arrived = exchange(faces)
    got = jnp.transpose(swap(message, "lay"), (1, 0, 2))
    back_first = swap(solve0(info, inverse, to_columns(got)), "lay")
    p0, *faces = start(gap, rt, back_first, o, ot, flux, arrived)

    q, message = dots(info, [p0], faces, exchange(faces))
    gathered = swap(mid(swap(message, "lay")), "col")
    back0 = swap(solve(info, inverse, gathered), "lay")
    p1, w1, *faces = step(info, back0, o, ot, flux, [p0], q, False)

    q, message = dots(info, [p1, w1], faces, exchange(faces))
    gathered = swap(mid(swap(message, "lay")), "col")
    back1 = swap(solve(info, inverse, gathered), "lay")
    p2, message = step(info, back1, o, ot, flux, [p1, w1], q, True)

    sums = to_columns(jnp.sum(swap(message, "lay"), axis=0))
    return finish(back_first, back0, back1, sums, p0, p1, p2)[None, None]


def solution(mesh):
    return jax.shard_map(
        shards,
        mesh=mesh,
        in_specs=(
            P("col", "lay", None, None, None),
            P("col", "lay", None),
            P("col", "lay", None, None, None),
            P("col", "lay", None, None),
        ),
        out_specs=P("col", "lay", None, None, None),
        check_vma=False,
    )
```

time: 1150 us -> 399 us (0.35)
  blocking collectives: 705 us -> 122 us
  other arithmetic: 152 us -> 0.09 us
  Pallas kernels: 0 us -> 78 us
  local copies, waits for them, and re-layouts: 89.2 us -> 32.2 us
  starting transfers between devices: 63.5 us -> 106 us
  matrix products: 40.4 us -> 0 us
  waiting for transfers between devices: 89.4 us -> 59.2 us
    psum x5 -> x0, blocking collectives: 418 us -> none  [the longest x3 241 us: project(): energy = lax.psum(inner_local(projected, projected), ('col', 'lay'))]
    all_gather x4 -> x0, blocking collectives: 287 us -> none  [the longest x3 213 us: project(): all_sums = lax.all_gather(sums[None], ('col', 'lay'), axis=0, tiled=True)]
    all_to_all x0 -> x9, blocking collectives: none -> 122 us  [swap(): return lax.all_to_all(value, axis, 0, 0, tiled=True)]
    pallas_call x0 -> x12, Pallas kernels: none -> 78 us  [the longest x2 30.9 us: step(): pl.pallas_call(functools.partial(step_kernel, same, last), grid=(SPECIES,...]
    another operation x15 -> x1, other arithmetic: 54.4 us -> 0.08 us  [shards(): jnp.stack([lax.axis_index('col'), lax.axis_index('lay')]).astype(jnp.int32)]
    gather x8 -> x0, local copies, waits for them, and re-layouts: 52.2 us -> none  [the longest x4 36.4 us: apply(): return jnp.take(image, inverse, axis=1)]
    ppermute x24 -> x18, waiting for transfers between devices: 89.4 us -> 49.6 us  [moved(): return lax.ppermute(value, axis, pairs)]
    all_to_all x0 -> x2, starting transfers between devices: none -> 35.9 us  [swap(): return lax.all_to_all(value, axis, 0, 0, tiled=True)]
  transfers between devices with their start and end apart: 24 -> 20, of which waited for: 11 -> 10; matrix products, arithmetic and copies ran while one was open for 2% -> 0% of each run, Pallas kernels for 0% -> 1%
where the time goes in v1:
time: 399 us; the launch traced here: 397 us
  blocking collectives  122 us (31%)
  starting transfers between devices  106 us (27%)
  Pallas kernels  78 us (20%)
  waiting for transfers between devices  59.2 us (15%)
  local copies, waits for them, and re-layouts  32.2 us (8%)
    all_to_all x9, blocking collectives, swap(): return lax.all_to_all(value, axis, 0, 0, tiled=True)  122 us
    ppermute x18, starting transfers between devices, moved(): return lax.ppermute(value, axis, pairs)  70.1 us
    ppermute x18, waiting for transfers between devices, moved(): return lax.ppermute(value, axis, pairs)  49.6 us
    all_to_all x2, starting transfers between devices, swap(): return lax.all_to_all(value, axis, 0, 0, tiled=True)  35.9 us
    pallas_call x2, Pallas kernels, step(): pl.pallas_call(functools.partial(step_kernel, same, last), grid=(SPECIES,...  30.9 us
    unnamed x68, local copies, waits for them, and re-layouts  30.2 us
    pallas_call x1, Pallas kernels, start(): pl.pallas_call(start_kernel, grid=(SPECIES,), in_specs=[per_species(M, CA...  20 us
    pallas_call x1, Pallas kernels, prep(): pl.pallas_call(prep_kernel, grid=(SPECIES,), in_specs=[whole(1, M), whole...  9.76 us
  transfers between devices with their start and end apart: 20, of which 10 were waited for; matrix products, arithmetic and copies ran while one was open for 0% of the time, Pallas kernels for 1%

profile of v1, /device:TPU:1, one launch (start us, length us, event | category | flops | bytes accessed | tf_op | source)
XLA Modules:
  0.0 397.4 jit_solution(11348086145755979815)
XLA Ops:
  3.9 9.8 %prep.1 = (bf16[1024,1024]{1,0:T(8,128)(2,1)S(1)}, bf16[1024,1024]{1,0:T(8,128)(2,1)S(1)}, f32[4,8,1024]{2,1,0:T(8,128)S(1)}, f32[8,8,128]{2,1,0:T(8,128)S(1)}, ...) custom-call(s32[1,1024]{1,0:T(1,128)S(1)} %bitcast.12, ...), custom_call_target="tpu_custom_call" | custom-call | flops 1000000000 | bytes 20000000 | tf_op jit(solution)/shard_map/prep/pallas_call | solution.py:147
  18.5 10.4 %all_to_all.55 = f32[8,8,128]{2,1,0:T(8,128)S(1)} all-to-all(f32[8,8,128]{2,1,0:T(8,128)S(1)} %get-tuple-element.36), channel_id=1, replica_groups=mesh['col'=32,'lay'=8] {'lay'}, dimensions={0} | all-to-all | bytes 65536 | tf_op jit(solution)/shard_map/all_to_all | solution.py:580
  30.0 11.2 %all-to-all-start.1 = ((f32[32,8,8,128]{3,2,1,0:T(8,128)}), f32[32,8,8,128]{3,2,1,0:T(8,128)S(1)}, u32[]{:S(2)}, u32[]{:S(2)}) async-start(f32[32,8,8,128]{3,2,1,0:T(8,128)} %broadcast_in_dim.6), calls=%async_computation.1 | async-start | bytes 2097152 | tf_op jit(solution)/shard_map/all_to_all | solution.py:580
  44.3 7.3 %collective-permute-start = (f32[4,208,128]{2,1,0:T(8,128)}, f32[4,208,128]{2,1,0:T(8,128)S(1)}, u32[]{:S(2)}, u32[]{:S(2)}) collective-permute-start(f32[4,208,128]{2,1,0:T(8,128)} %get-tuple-element.40), channel_id=1, source_target_pairs={{0,32},{8,40},{16,48},{24,56},{32,64},{40,72},{48,80},{56,88},{64,... | collective-permute-start | bytes 1277960 | tf_op jit(solution)/shard_map/ppermute | solution.py:558
  58.5 7.3 %all-to-all-done.1.gathered_ref = f32[32,8,8,128]{3,2,1,0:T(8,128)S(1)} async-done(((f32[32,8,8,128]{3,2,1,0:T(8,128)}), f32[32,8,8,128]{3,2,1,0:T(8,128)S(1)}, u32[]{:S(2)}, u32[]{:S(2)}) %all-to-all-start.1) | async-done | bytes 1048608 | tf_op jit(solution)/shard_map/all_to_all | solution.py:580
  69.5 24.7 %all-to-all-start.2 = ((f32[8,64,128]{2,1,0:T(8,128)}), f32[8,64,128]{2,1,0:T(8,128)S(1)}, u32[]{:S(2)}, u32[]{:S(2)}) async-start(f32[8,64,128]{2,1,0:T(8,128)} %solve_start.1), calls=%async_computation.2 | async-start | bytes 524288 | tf_op jit(solution)/shard_map/all_to_all | solution.py:580
  106.1 20.0 %start.1 = (f32[4,1024,128]{2,1,0:T(8,128)S(1)}, f32[4,192,128]{2,1,0:T(8,128)S(1)}, f32[4,192,128]{2,1,0:T(8,128)S(1)}, f32[4,192,128]{2,1,0:T(8,128)S(1)}, f32...) custom-call(f32[4,1024,128]{2,1,0:T(8,128)S(1)} %bitcast.10, ...), custom_call_target="tpu_custom_call" | custom-call | flops 4000000000 | bytes 20000000 | tf_op jit(solution)/shard_map/start/pallas_call | solution.py:371
  130.4 18.1 %collective-permute-start.6 = (f32[4,192,128]{2,1,0:T(8,128)S(1)}, f32[4,192,128]{2,1,0:T(8,128)S(1)}, u32[]{:S(2)}, u32[]{:S(2)}) collective-permute-start(f32[4,192,128]{2,1,0:T(8,128)S(1)} %get-tuple-element.48.refs_2_), channel_id=1, source_target_pairs={{0,32},{8,40},{16,48},{24,56},{32,64},{40,72},{48,80},{56,88},{64,... | collective-permute-start | bytes 1179656 | tf_op jit(solution)/shard_map/ppermute | solution.py:558
  162.0 12.1 %collective-permute-done.9.refs_10_ = f32[4,192,128]{2,1,0:T(8,128)S(1)} collective-permute-done((f32[4,192,128]{2,1,0:T(8,128)S(1)}, f32[4,192,128]{2,1,0:T(8,128)S(1)}, u32[]{:S(2)}, u32[]{:S(2)}) %collective-permute-start.9) | collective-permute-done | bytes 393248 | tf_op jit(solution)/shard_map/ppermute | solution.py:558
  174.0 6.7 %collective-permute-done.8.refs_9_ = f32[4,192,128]{2,1,0:T(8,128)S(1)} collective-permute-done((f32[4,192,128]{2,1,0:T(8,128)S(1)}, f32[4,192,128]{2,1,0:T(8,128)S(1)}, u32[]{:S(2)}, u32[]{:S(2)}) %collective-permute-start.8) | collective-permute-done | bytes 393248 | tf_op jit(solution)/shard_map/ppermute | solution.py:558
  183.5 7.9 %all_to_all.56.got_ref = f32[8,8,128]{2,1,0:T(8,128)} all-to-all(f32[8,8,128]{2,1,0:T(8,128)S(1)} %get-tuple-element.53), channel_id=1, replica_groups=mesh['col'=32,'lay'=8] {'lay'}, dimensions={0} | all-to-all | bytes 65536 | tf_op jit(solution)/shard_map/all_to_all | solution.py:580
  193.0 29.7 %all_to_all.57.gathered_ref = f32[32,16,128]{2,1,0:T(8,128)} all-to-all(f32[32,16,128]{2,1,0:T(8,128)} %combine_layers.2), channel_id=1, replica_groups=mesh['col'=32,'lay'=8] {'col'}, dimensions={0} | all-to-all | bytes 524288 | tf_op jit(solution)/shard_map/all_to_all | solution.py:580
  224.8 11.6 %all_to_all.58.back_ref.back0_ref = f32[8,8,128]{2,1,0:T(8,128)S(1)} all-to-all(f32[8,8,128]{2,1,0:T(8,128)} %solve_step.2), channel_id=1, replica_groups=mesh['col'=32,'lay'=8] {'lay'}, dimensions={0} | all-to-all | bytes 65536 | tf_op jit(solution)/shard_map/all_to_all | solution.py:580
  238.6 15.8 %step.2 = (f32[4,1024,128]{2,1,0:T(8,128)S(1)}, f32[4,1024,128]{2,1,0:T(8,128)S(1)}, f32[4,192,128]{2,1,0:T(8,128)S(1)}, f32[4,192,128]{2,1,0:T(8,128)S(1)}, f32...) custom-call(s32[2]{0:T(128)S(1)} %copy-done.27, ...), custom_call_target="tpu_custom_call" | custom-call | flops 4000000000 | bytes 20000000 | tf_op jit(solution)/shard_map/step/pallas_call | solution.py:512
  259.7 7.9 %collective-permute-start.12 = (f32[4,192,128]{2,1,0:T(8,128)S(1)}, f32[4,192,128]{2,1,0:T(8,128)S(1)}, u32[]{:S(2)}, u32[]{:S(2)}) collective-permute-start(f32[4,192,128]{2,1,0:T(8,128)S(1)} %get-tuple-element.58.refs_3_), channel_id=1, source_target_pairs={{0,32},{8,40},{16,48},{24,56},{32,64},{40,72},{48,80},{56,88},{64,... | collective-permute-start | bytes 1179656 | tf_op jit(solution)/shard_map/ppermute | solution.py:558
  268.9 4.2 %collective-permute-start.14 = (f32[4,192,128]{2,1,0:T(8,128)S(1)}, f32[4,192,128]{2,1,0:T(8,128)S(1)}, u32[]{:S(2)}, u32[]{:S(2)}) collective-permute-start(f32[4,192,128]{2,1,0:T(8,128)S(1)} %get-tuple-element.60.refs_5_), channel_id=1, source_target_pairs={{0,8},{8,16},{16,24},{32,40},{40,48},{48,56},{64,72},{72,80},{80,8... | collective-permute-start | bytes 1179656 | tf_op jit(solution)/shard_map/ppermute | solution.py:558
  280.5 14.9 %collective-permute-done.15.refs_11_ = f32[4,192,128]{2,1,0:T(8,128)S(1)} collective-permute-done((f32[4,192,128]{2,1,0:T(8,128)S(1)}, f32[4,192,128]{2,1,0:T(8,128)S(1)}, u32[]{:S(2)}, u32[]{:S(2)}) %collective-permute-start.15) | collective-permute-done | bytes 393248 | tf_op jit(solution)/shard_map/ppermute | solution.py:558
  295.3 5.8 %collective-permute-done.14.refs_10_ = f32[4,192,128]{2,1,0:T(8,128)S(1)} collective-permute-done((f32[4,192,128]{2,1,0:T(8,128)S(1)}, f32[4,192,128]{2,1,0:T(8,128)S(1)}, u32[]{:S(2)}, u32[]{:S(2)}) %collective-permute-start.14) | collective-permute-done | bytes 393248 | tf_op jit(solution)/shard_map/ppermute | solution.py:558
  305.5 8.3 %all_to_all.59.got_ref = f32[8,8,128]{2,1,0:T(8,128)} all-to-all(f32[8,8,128]{2,1,0:T(8,128)S(1)} %get-tuple-element.63), channel_id=1, replica_groups=mesh['col'=32,'lay'=8] {'lay'}, dimensions={0} | all-to-all | bytes 65536 | tf_op jit(solution)/shard_map/all_to_all | solution.py:580
  315.2 21.0 %all_to_all.60.gathered_ref = f32[32,16,128]{2,1,0:T(8,128)} all-to-all(f32[32,16,128]{2,1,0:T(8,128)} %combine_layers.3), channel_id=1, replica_groups=mesh['col'=32,'lay'=8] {'col'}, dimensions={0} | all-to-all | bytes 524288 | tf_op jit(solution)/shard_map/all_to_all | solution.py:580
  338.4 11.6 %all_to_all.61.back_ref.back1_ref = f32[8,8,128]{2,1,0:T(8,128)S(1)} all-to-all(f32[8,8,128]{2,1,0:T(8,128)} %solve_step.3), channel_id=1, replica_groups=mesh['col'=32,'lay'=8] {'lay'}, dimensions={0} | all-to-all | bytes 65536 | tf_op jit(solution)/shard_map/all_to_all | solution.py:580
  354.8 15.1 %step.3 = (f32[4,1024,128]{2,1,0:T(8,128)S(1)}, f32[8,8,128]{2,1,0:T(8,128)S(1)}) custom-call(s32[2]{0:T(128)S(1)} %copy-done.29, f32[8,8,128]{2,1,0:T(8,128)S(1)} %all_to_all.61.back_ref.back1_ref, bf16[1024,1024]{1,0:T(8,128)(2,1)S(1)} %copy-done.4, bf16[1024,1024]{1,0:T(8,128)(2,1)S(1)} %copy-done.6, bf16[4,1024,1024]{2,1,0:T(8,128)(2,1)} %bitcast.17, ...), custom_call_target="tpu_custom_call" | custom-call | flops 4000000000 | bytes 20000000 | tf_op jit(solution)/shard_map/step/pallas_call | solution.py:512
  371.2 7.8 %all_to_all.62 = f32[8,8,128]{2,1,0:T(8,128)S(1)} all-to-all(f32[8,8,128]{2,1,0:T(8,128)S(1)} %get-tuple-element.65), channel_id=1, replica_groups=mesh['col'=32,'lay'=8] {'lay'}, dimensions={0} | all-to-all | bytes 65536 | tf_op jit(solution)/shard_map/all_to_all | solution.py:580
  379.1 13.1 %all_to_all.63.sums_ref = f32[32,8,128]{2,1,0:T(8,128)S(1)} all-to-all(f32[32,8,128]{2,1,0:T(8,128)S(1)} %broadcast_in_dim.7), channel_id=1, replica_groups=mesh['col'=32,'lay'=8] {'col'}, dimensions={0} | all-to-all | bytes 262144 | tf_op jit(solution)/shard_map/all_to_all | solution.py:580
  (111 shorter events, 94.7 us)
Async XLA Ops:
  30.0 35.8 %all-to-all-start.1 = ((f32[32,8,8,128]{3,2,1,0:T(8,128)}), f32[32,8,8,128]{3,2,1,0:T(8,128)S(1)}, u32[]{:S(2)}, u32[]{:S(2)}) async-start(f32[32,8,8,128]{3,2,1,0:T(8,128)} %broadcast_in_dim.6), calls=%async_computation.1 | async-start | bytes 2097152 | tf_op jit(solution)/shard_map/all_to_all | solution.py:580
  41.2 15.3 %collective-permute-start.4 = (f32[4,136,128]{2,1,0:T(8,128)}, f32[4,136,128]{2,1,0:T(8,128)S(1)}, u32[]{:S(2)}, u32[]{:S(2)}) collective-permute-start(f32[4,136,128]{2,1,0:T(8,128)} %get-tuple-element.44), channel_id=1, source_target_pairs={{0,1},{1,2},{2,3},{3,4},{4,5},{5,6},{6,7},{8,9},{9,10},{10,11},{11... | collective-permute-start | bytes 835592 | tf_op jit(solution)/shard_map/ppermute | solution.py:558
  44.3 49.9 %collective-permute-start = (f32[4,208,128]{2,1,0:T(8,128)}, f32[4,208,128]{2,1,0:T(8,128)S(1)}, u32[]{:S(2)}, u32[]{:S(2)}) collective-permute-start(f32[4,208,128]{2,1,0:T(8,128)} %get-tuple-element.40), channel_id=1, source_target_pairs={{0,32},{8,40},{16,48},{24,56},{32,64},{40,72},{48,80},{56,88},{64,... | collective-permute-start | bytes 1277960 | tf_op jit(solution)/shard_map/ppermute | solution.py:558
  51.7 45.1 %collective-permute-start.1 = (f32[4,208,128]{2,1,0:T(8,128)}, f32[4,208,128]{2,1,0:T(8,128)S(1)}, u32[]{:S(2)}, u32[]{:S(2)}) collective-permute-start(f32[4,208,128]{2,1,0:T(8,128)} %get-tuple-element.41), channel_id=1, source_target_pairs={{32,0},{40,8},{48,16},{56,24},{64,32},{72,40},{80,48},{88,56},{96,... | collective-permute-start | bytes 1277960 | tf_op jit(solution)/shard_map/ppermute | solution.py:558
  53.0 43.8 %collective-permute-start.2 = (f32[4,208,128]{2,1,0:T(8,128)}, f32[4,208,128]{2,1,0:T(8,128)S(1)}, u32[]{:S(2)}, u32[]{:S(2)}) collective-permute-start(f32[4,208,128]{2,1,0:T(8,128)} %get-tuple-element.42), channel_id=1, source_target_pairs={{0,8},{8,16},{16,24},{32,40},{40,48},{48,56},{64,72},{72,80},{80,8... | collective-permute-start | bytes 1277960 | tf_op jit(solution)/shard_map/ppermute | solution.py:558
  55.2 42.4 %collective-permute-start.3 = (f32[4,208,128]{2,1,0:T(8,128)}, f32[4,208,128]{2,1,0:T(8,128)S(1)}, u32[]{:S(2)}, u32[]{:S(2)}) collective-permute-start(f32[4,208,128]{2,1,0:T(8,128)} %copy-done.32), channel_id=1, source_target_pairs={{8,0},{16,8},{24,16},{40,32},{48,40},{56,48},{72,64},{80,72},{88,8... | collective-permute-start | bytes 1277960 | tf_op jit(solution)/shard_map/ppermute | solution.py:558
  56.5 37.6 %collective-permute-start.5 = (f32[4,136,128]{2,1,0:T(8,128)}, f32[4,136,128]{2,1,0:T(8,128)}, u32[]{:S(2)}, u32[]{:S(2)}) collective-permute-start(f32[4,136,128]{2,1,0:T(8,128)} %copy-done.33), channel_id=1, source_target_pairs={{1,0},{2,1},{3,2},{4,3},{5,4},{6,5},{7,6},{9,8},{10,9},{11,10},{12... | collective-permute-start | bytes 835592 | tf_op jit(solution)/shard_map/ppermute | solution.py:558
  58.5 122.2 %copy-start.26 = (s32[2]{0:T(128)}, s32[2]{0:T(128)S(1)}, u32[]{:S(2)}) copy-start(s32[2]{0:T(128)S(1)} %pad_add_fusion.info_ref) | copy-start | bytes 28
  69.5 31.2 %all-to-all-start.2 = ((f32[8,64,128]{2,1,0:T(8,128)}), f32[8,64,128]{2,1,0:T(8,128)S(1)}, u32[]{:S(2)}, u32[]{:S(2)}) async-start(f32[8,64,128]{2,1,0:T(8,128)} %solve_start.1), calls=%async_computation.2 | async-start | bytes 524288 | tf_op jit(solution)/shard_map/all_to_all | solution.py:580
  126.2 56.0 %copy-start = (f32[4,1024,128]{2,1,0:T(8,128)}, f32[4,1024,128]{2,1,0:T(8,128)S(1)}, u32[]{:S(2)}) copy-start(f32[4,1024,128]{2,1,0:T(8,128)S(1)} %get-tuple-element.46.refs_0_.p0_ref) | copy-start | bytes 6291460
  126.2 27.7 %collective-permute-start.11 = (f32[4,128,128]{2,1,0:T(8,128)S(1)}, f32[4,128,128]{2,1,0:T(8,128)S(1)}, u32[]{:S(2)}, u32[]{:S(2)}) collective-permute-start(f32[4,128,128]{2,1,0:T(8,128)S(1)} %get-tuple-element.51.refs_5_), channel_id=1, source_target_pairs={{1,0},{2,1},{3,2},{4,3},{5,4},{6,5},{7,6},{9,8},{10,9},{11,10},{12... | collective-permute-start | bytes 786440 | tf_op jit(solution)/shard_map/ppermute | solution.py:558
  129.1 31.9 %collective-permute-start.7 = (f32[4,192,128]{2,1,0:T(8,128)S(1)}, f32[4,192,128]{2,1,0:T(8,128)S(1)}, u32[]{:S(2)}, u32[]{:S(2)}) collective-permute-start(f32[4,192,128]{2,1,0:T(8,128)S(1)} %get-tuple-element.47.refs_1_), channel_id=1, source_target_pairs={{32,0},{40,8},{48,16},{56,24},{64,32},{72,40},{80,48},{88,56},{96,... | collective-permute-start | bytes 1179656 | tf_op jit(solution)/shard_map/ppermute | solution.py:558
  130.4 31.5 %collective-permute-start.6 = (f32[4,192,128]{2,1,0:T(8,128)S(1)}, f32[4,192,128]{2,1,0:T(8,128)S(1)}, u32[]{:S(2)}, u32[]{:S(2)}) collective-permute-start(f32[4,192,128]{2,1,0:T(8,128)S(1)} %get-tuple-element.48.refs_2_), channel_id=1, source_target_pairs={{0,32},{8,40},{16,48},{24,56},{32,64},{40,72},{48,80},{56,88},{64,... | collective-permute-start | bytes 1179656 | tf_op jit(solution)/shard_map/ppermute | solution.py:558
  148.5 25.5 %collective-permute-start.9 = (f32[4,192,128]{2,1,0:T(8,128)S(1)}, f32[4,192,128]{2,1,0:T(8,128)S(1)}, u32[]{:S(2)}, u32[]{:S(2)}) collective-permute-start(f32[4,192,128]{2,1,0:T(8,128)S(1)} %get-tuple-element.49.refs_3_), channel_id=1, source_target_pairs={{8,0},{16,8},{24,16},{40,32},{48,40},{56,48},{72,64},{80,72},{88,8... | collective-permute-start | bytes 1179656 | tf_op jit(solution)/shard_map/ppermute | solution.py:558
  149.8 30.9 %collective-permute-start.8 = (f32[4,192,128]{2,1,0:T(8,128)S(1)}, f32[4,192,128]{2,1,0:T(8,128)S(1)}, u32[]{:S(2)}, u32[]{:S(2)}) collective-permute-start(f32[4,192,128]{2,1,0:T(8,128)S(1)} %get-tuple-element.50.refs_4_), channel_id=1, source_target_pairs={{0,8},{8,16},{16,24},{32,40},{40,48},{48,56},{64,72},{72,80},{80,8... | collective-permute-start | bytes 1179656 | tf_op jit(solution)/shard_map/ppermute | solution.py:558
  153.8 7.2 %collective-permute-start.10 = (f32[4,128,128]{2,1,0:T(8,128)S(1)}, f32[4,128,128]{2,1,0:T(8,128)S(1)}, u32[]{:S(2)}, u32[]{:S(2)}) collective-permute-start(f32[4,128,128]{2,1,0:T(8,128)S(1)} %get-tuple-element.52.refs_6_), channel_id=1, source_target_pairs={{0,1},{1,2},{2,3},{3,4},{4,5},{5,6},{6,7},{8,9},{9,10},{10,11},{11... | collective-permute-start | bytes 786440 | tf_op jit(solution)/shard_map/ppermute | solution.py:558
  238.6 62.6 %copy-start.28 = (s32[2]{0:T(128)S(1)}, s32[2]{0:T(128)}, u32[]{:S(2)}) copy-start(s32[2]{0:T(128)} %copy-done.26) | copy-start | bytes 28
  255.7 17.4 %collective-permute-start.17 = (f32[4,128,128]{2,1,0:T(8,128)S(1)}, f32[4,128,128]{2,1,0:T(8,128)S(1)}, u32[]{:S(2)}, u32[]{:S(2)}) collective-permute-start(f32[4,128,128]{2,1,0:T(8,128)S(1)} %get-tuple-element.61.refs_6_), channel_id=1, source_target_pairs={{1,0},{2,1},{3,2},{4,3},{5,4},{6,5},{7,6},{9,8},{10,9},{11,10},{12... | collective-permute-start | bytes 786440 | tf_op jit(solution)/shard_map/ppermute | solution.py:558
  258.4 22.1 %collective-permute-start.13 = (f32[4,192,128]{2,1,0:T(8,128)S(1)}, f32[4,192,128]{2,1,0:T(8,128)S(1)}, u32[]{:S(2)}, u32[]{:S(2)}) collective-permute-start(f32[4,192,128]{2,1,0:T(8,128)S(1)} %get-tuple-element.57.refs_2_), channel_id=1, source_target_pairs={{32,0},{40,8},{48,16},{56,24},{64,32},{72,40},{80,48},{88,56},{96,... | collective-permute-start | bytes 1179656 | tf_op jit(solution)/shard_map/ppermute | solution.py:558
  259.7 20.8 %collective-permute-start.12 = (f32[4,192,128]{2,1,0:T(8,128)S(1)}, f32[4,192,128]{2,1,0:T(8,128)S(1)}, u32[]{:S(2)}, u32[]{:S(2)}) collective-permute-start(f32[4,192,128]{2,1,0:T(8,128)S(1)} %get-tuple-element.58.refs_3_), channel_id=1, source_target_pairs={{0,32},{8,40},{16,48},{24,56},{32,64},{40,72},{48,80},{56,88},{64,... | collective-permute-start | bytes 1179656 | tf_op jit(solution)/shard_map/ppermute | solution.py:558
  267.6 27.7 %collective-permute-start.15 = (f32[4,192,128]{2,1,0:T(8,128)S(1)}, f32[4,192,128]{2,1,0:T(8,128)S(1)}, u32[]{:S(2)}, u32[]{:S(2)}) collective-permute-start(f32[4,192,128]{2,1,0:T(8,128)S(1)} %get-tuple-element.59.refs_4_), channel_id=1, source_target_pairs={{8,0},{16,8},{24,16},{40,32},{48,40},{56,48},{72,64},{80,72},{88,8... | collective-permute-start | bytes 1179656 | tf_op jit(solution)/shard_map/ppermute | solution.py:558
  268.9 32.2 %collective-permute-start.14 = (f32[4,192,128]{2,1,0:T(8,128)S(1)}, f32[4,192,128]{2,1,0:T(8,128)S(1)}, u32[]{:S(2)}, u32[]{:S(2)}) collective-permute-start(f32[4,192,128]{2,1,0:T(8,128)S(1)} %get-tuple-element.60.refs_5_), channel_id=1, source_target_pairs={{0,8},{8,16},{16,24},{32,40},{40,48},{48,56},{64,72},{72,80},{80,8... | collective-permute-start | bytes 1179656 | tf_op jit(solution)/shard_map/ppermute | solution.py:558
  273.1 7.3 %collective-permute-start.16 = (f32[4,128,128]{2,1,0:T(8,128)S(1)}, f32[4,128,128]{2,1,0:T(8,128)S(1)}, u32[]{:S(2)}, u32[]{:S(2)}) collective-permute-start(f32[4,128,128]{2,1,0:T(8,128)S(1)} %get-tuple-element.62.refs_7_), channel_id=1, source_target_pairs={{0,1},{1,2},{2,3},{3,4},{4,5},{5,6},{6,7},{8,9},{9,10},{10,11},{11... | collective-permute-start | bytes 786440 | tf_op jit(solution)/shard_map/ppermute | solution.py:558
  301.1 48.9 %copy-start.29 = (s32[2]{0:T(128)S(1)}, s32[2]{0:T(128)}, u32[]{:S(2)}) copy-start(s32[2]{0:T(128)} %copy-done.26) | copy-start | bytes 28
  (30 other events, 176.3 us)

commit v2 on v1

v2 whole, which is shorter than its diff:
```python
import functools

import jax
import jax.numpy as jnp
import numpy as np
from jax import lax
from jax.experimental import pallas as pl
from jax.experimental.pallas import tpu as pltpu
from jax.sharding import PartitionSpec as P

SIDE = 192
TOP = 128
YCOLS = 4
SPECIES = 4
CASES = 128
M = 1024
NCOL = 32
NLAY = 8
COUNT = NCOL * NLAY
SIZES = (SIDE, SIDE, SIDE, SIDE, TOP, TOP)
STARTS = (0, 192, 384, 576, 768, 896)
TAILS = (16, 16, 16, 16, 8, 8)
CHUNK = 256
HALF = CASES // 2
F32 = jnp.float32
BF16 = jnp.bfloat16
VMEM_LIMIT = 40 * 1024 * 1024


def coarse_inverse():
    index = np.arange(COUNT)
    zpos, cpos = index % NLAY, index // NLAY
    ypos, xpos = cpos % YCOLS, cpos // YCOLS
    dx = np.abs(xpos[:, None] - xpos[None, :])
    dy = np.abs(ypos[:, None] - ypos[None, :])
    dz = np.abs(zpos[:, None] - zpos[None, :])
    lateral = (dx + dy == 1) & (dz == 0)
    upward = (dx + dy == 0) & (dz == 1)
    matrix = M * np.eye(COUNT) - SIDE * lateral - TOP * upward
    return np.linalg.inv(matrix).astype(np.float32)


def params():
    return pltpu.CompilerParams(
        dimension_semantics=("arbitrary",), vmem_limit_bytes=VMEM_LIMIT
    )


def cost(flops, nbytes):
    return pl.CostEstimate(flops=int(flops), bytes_accessed=int(nbytes), transcendentals=0)


SMEM = pl.BlockSpec(memory_space=pltpu.SMEM)


def per_species(*shape):
    zeros = (0,) * len(shape)
    return pl.BlockSpec((1,) + shape, lambda k: (jnp.minimum(k, SPECIES - 1),) + zeros)


def whole(*shape):
    zeros = (0,) * len(shape)
    return pl.BlockSpec(shape, lambda k: zeros)


def pair(*shape):
    zeros = (0,) * len(shape)
    return pl.BlockSpec((2,) + shape, lambda k: (jnp.minimum(k, SPECIES - 1),) + zeros)


def out(shape, dtype=F32):
    return jax.ShapeDtypeStruct(shape, dtype)


def exact_dot(a, b, dims):
    return lax.dot_general(
        a, b, (dims, ((), ())), precision=lax.Precision.HIGHEST, preferred_element_type=F32
    )


def split3(value):
    first = value.astype(BF16).astype(F32)
    rest = value - first
    second = rest.astype(BF16).astype(F32)
    return [first, second, rest - second]


def fill_gather(col_ref, o_ref):
    lanes = lax.broadcasted_iota(jnp.int32, (CHUNK, M), 1)
    for i in range(0, M, CHUNK):
        hit = col_ref[i : i + CHUNK, :] == lanes
        o_ref[i : i + CHUNK, :] = jnp.where(hit, 1.0, 0.0).astype(BF16)


def fill_scatter(row_ref, ot_ref):
    row = row_ref[...]
    index = lax.broadcasted_iota(jnp.int32, (CHUNK, M), 0)
    for i in range(0, M, CHUNK):
        hit = row == index + i
        ot_ref[i : i + CHUNK, :] = jnp.where(hit, 1.0, 0.0).astype(BF16)


def prep_kernel(row_ref, col_ref, flux_ref, gap_ref, load_ref, *refs):
    rt_ref, msg_ref = refs[:2]
    face_refs = refs[2:8]
    parts_ref, o_ref = refs[8:]
    k = pl.program_id(0)
    row = row_ref[...]

    face = lax.broadcasted_iota(jnp.int32, (16, M), 0)
    low = jnp.where(face <= 4, SIDE * face, jnp.where(face == 5, STARTS[5], M))
    high = jnp.where(face <= 3, SIDE * (face + 1), jnp.where(face == 4, STARTS[5], M))
    member = jnp.where((row >= low) & (row < high), 1.0, 0.0).astype(BF16)
    sums = jnp.dot(member, flux_ref[0], preferred_element_type=F32)
    for i, part in enumerate(split3(sums)):
        parts_ref[k, 16 * i : 16 * i + 16, :] = part.astype(BF16)
    rows = [
        jnp.sum(gap_ref[0, STARTS[f] : STARTS[f] + SIZES[f], :], axis=0, keepdims=True)
        for f in range(6)
    ]
    rows.append(load_ref[0])
    held = jnp.concatenate(rows + [jnp.zeros((1, CASES), F32)], axis=0)
    msg_ref[2 * k] = held
    msg_ref[2 * k + 1] = held
    for f in range(6):
        face_refs[f][k, : SIZES[f], :] = gap_ref[0, STARTS[f] : STARTS[f] + SIZES[f], :]

    @pl.when(k == SPECIES - 1)
    def _():
        fill_gather(col_ref, o_ref)
        parts = parts_ref[...].reshape(SPECIES * 48, M)
        moved = jnp.dot(parts, o_ref[...], preferred_element_type=F32)
        lane = lax.broadcasted_iota(jnp.int32, (8, M), 1)
        slot = lax.broadcasted_iota(jnp.int32, (8, CASES), 1)
        peer = lax.broadcasted_iota(jnp.int32, (8, CASES), 0)
        for s in range(SPECIES):
            base = 48 * s
            rt = moved[base : base + 8] + moved[base + 16 : base + 24]
            rt = rt + moved[base + 32 : base + 40]
            rt_ref[s] = rt
            table = jnp.zeros((8, CASES), F32)
            for f in range(6):
                inside = (lane >= STARTS[f]) & (lane < STARTS[f] + SIZES[f])
                total = jnp.sum(jnp.where(inside, rt, 0.0), axis=1, keepdims=True)
                here = (slot == 6 * f + peer) & (peer < 6)
                table = table + jnp.where(here, total, 0.0)
            table = jnp.sum(table, axis=0, keepdims=True)
            msg_ref[2 * s, 7:8, :] = table
            msg_ref[2 * s + 1, 7:8, :] = table
            for f in range(6):
                size = SIZES[f]
                turned = rt if STARTS[f] == 0 else pltpu.roll(rt, M - STARTS[f], 1)
                face_refs[f][s, size : size + 8, :] = turned[:, :CASES]
                if size > CASES:
                    face_refs[f][s, size + 8 : size + 16, :] = turned[:, CASES : 2 * CASES]


def prep(row, column, flux, gap, load):
    faces = [(SPECIES, SIZES[f] + TAILS[f], CASES) for f in range(6)]
    return pl.pallas_call(
        prep_kernel,
        grid=(SPECIES,),
        in_specs=[
            whole(1, M),
            whole(M, 1),
            per_species(M, M),
            per_species(M, CASES),
            per_species(1, CASES),
        ],
        out_specs=[whole(SPECIES, 8, M), whole(8, 8, CASES)]
        + [whole(*shape) for shape in faces],
        out_shape=[
            out((SPECIES, 8, M)),
            out((8, 8, CASES)),
        ]
        + [out(shape) for shape in faces],
        scratch_shapes=[pltpu.VMEM((SPECIES, 48, M), BF16), pltpu.VMEM((M, M), BF16)],
        compiler_params=params(),
        cost_estimate=cost(1e9, 20e6),
        name="prep",
    )(row, column, flux, gap, load.reshape(SPECIES, 1, CASES))


def shifted(value, f):
    row = lax.broadcasted_iota(jnp.int32, value.shape, 0)
    zpos = row % NLAY
    ypos = (row // NLAY) % YCOLS
    xpos = row // (NLAY * YCOLS)
    step, ok = (
        (NLAY * YCOLS, xpos > 0),
        (-NLAY * YCOLS, xpos < NCOL // YCOLS - 1),
        (NLAY, ypos > 0),
        (-NLAY, ypos < YCOLS - 1),
        (1, zpos > 0),
        (-1, zpos < NLAY - 1),
    )[f]
    return jnp.where(ok, pltpu.roll(value, step % COUNT, 0), 0.0)


def own_half(value, lay):
    return jnp.where(lay % 2 == 0, value, pltpu.roll(value, HALF, value.ndim - 1))


def packed(first, second):
    lane = lax.broadcasted_iota(jnp.int32, first.shape, first.ndim - 1)
    return jnp.where(lane < HALF, first, pltpu.roll(second, HALF, second.ndim - 1))


def mid0_kernel(info_ref, got_ref, out_ref):
    lay = info_ref[1]

    def rows(r):
        return jnp.concatenate([got_ref[l, r : r + 1, :] for l in range(NLAY)], axis=0)

    halves = [own_half(rows(r), lay) for r in range(7)] + [rows(7)]
    tiles = [packed(halves[r], halves[r + 4]) for r in range(4)]
    for c in range(NCOL):
        for r in range(4):
            out_ref[c, r] = tiles[r]


def mid0(info, got):
    return pl.pallas_call(
        mid0_kernel,
        in_specs=[SMEM, pl.BlockSpec(memory_space=pltpu.VMEM)],
        out_specs=pl.BlockSpec(memory_space=pltpu.VMEM),
        out_shape=out((NCOL, 4, 8, CASES)),
        cost_estimate=cost(1e5, 6e5),
        name="pack_start",
    )(info, got)


def solve0_kernel(info_ref, inv_ref, gathered_ref, out_ref, vals_ref):
    col = info_ref[0]

    def rows(r):
        value = gathered_ref[:, r % 4].reshape(COUNT, CASES)
        return value if r < 4 else pltpu.roll(value, HALF, 1)

    inv = inv_ref[...]
    y0 = exact_dot(inv, rows(6), ((1,), (0,)))
    vals = [y0 - shifted(y0, f) for f in range(6)]
    rounded = [v.astype(BF16).astype(F32) for v in vals]
    table = rows(7)
    tau = []
    for f in range(6):
        total = rows(f)
        for g in range(6):
            total = total - table[:, 6 * f + g : 6 * f + g + 1] * rounded[g]
        tau.append(total)
    h = jnp.zeros((COUNT, CASES), F32)
    for f in range(6):
        h = h + (tau[f] - shifted(tau[f ^ 1], f))
    y1 = exact_dot(inv, h, ((1,), (0,)))
    here = pl.ds(pl.multiple_of(col * NLAY, NLAY), NLAY)
    zero = jnp.zeros((NLAY, CASES), F32)
    for f in range(6):
        vals_ref[0] = y1 - shifted(y1, f)
        out_ref[:, f, :] = vals_ref[0, here, :]
    for f in range(6):
        vals_ref[f] = vals[f]
    for g in range(6):
        out_ref[:, 8 + g, :] = vals_ref[g, here, :]
    for f in range(4):
        away = jnp.clip(col + (-YCOLS, YCOLS, -1, 1)[f], 0, NCOL - 1)
        there = pl.ds(pl.multiple_of(away * NLAY, NLAY), NLAY)
        for g in range(6):
            out_ref[:, 16 + 8 * f + g, :] = vals_ref[g, there, :]
    for f in (4, 5):
        for g in range(6):
            out_ref[:, 16 + 8 * f + g, :] = pltpu.roll(
                vals_ref[g, here, :], (1, NLAY - 1)[f - 4], 0
            )
    for group in range(8):
        out_ref[:, 8 * group + 6, :] = zero
        out_ref[:, 8 * group + 7, :] = zero


def solve0(info, inverse, gathered):
    return pl.pallas_call(
        solve0_kernel,
        in_specs=[SMEM, pl.BlockSpec(memory_space=pltpu.VMEM), pl.BlockSpec(memory_space=pltpu.VMEM)],
        out_specs=pl.BlockSpec(memory_space=pltpu.VMEM),
        out_shape=out((8, 64, CASES)),
        scratch_shapes=[pltpu.VMEM((6, COUNT, CASES), F32)],
        compiler_params=pltpu.CompilerParams(vmem_limit_bytes=VMEM_LIMIT),
        cost_estimate=cost(1e8, 2e6),
        name="solve_start",
    )(info, inverse, gathered)


def mid_kernel(info_ref, got_ref, out_ref):
    lay = info_ref[1]
    total = got_ref[0]
    top = got_ref[0, 5:6, :]
    for l in range(1, NLAY):
        total = total + got_ref[l]
        top = jnp.maximum(top, got_ref[l, 5:6, :])
    qq = jnp.zeros((1, CASES), F32)
    for l in range(NLAY):
        part = got_ref[l, 5:6, :] / top
        qq = qq + got_ref[l, 2:3, :] * (part * part)
    heads = [got_ref[l, 0:1, :] for l in range(NLAY)]
    zero = jnp.zeros((1, CASES), F32)
    first = jnp.concatenate(heads[:4] + [total[1:2], total[3:4], top, zero], axis=0)
    second = jnp.concatenate(heads[4:] + [qq, total[4:5], top, zero], axis=0)
    tile = packed(own_half(first, lay), own_half(second, lay))
    for c in range(NCOL):
        out_ref[c] = tile


def mid(info, got):
    return pl.pallas_call(
        mid_kernel,
        in_specs=[SMEM, pl.BlockSpec(memory_space=pltpu.VMEM)],
        out_specs=pl.BlockSpec(memory_space=pltpu.VMEM),
        out_shape=out((NCOL, 8, CASES)),
        cost_estimate=cost(1e5, 3e5),
        name="combine_layers",
    )(info, got)


def solve_kernel(info_ref, inv_ref, gathered_ref, out_ref, y_ref):
    col = info_ref[0]
    tiles = gathered_ref[...].reshape(COUNT, CASES)
    upper = pltpu.roll(tiles, HALF, 1)
    row = lax.broadcasted_iota(jnp.int32, (COUNT, CASES), 0) % 8
    tops = jnp.where(row == 6, tiles, 0.0)
    top = jnp.max(tops, axis=0, keepdims=True)
    part = pltpu.roll(tops, COUNT - 2, 0) / top
    qq = jnp.sum(jnp.where(row == 4, upper * (part * part), 0.0), axis=0, keepdims=True)
    pq = jnp.sum(jnp.where(row == 4, tiles, 0.0), axis=0, keepdims=True)
    wq = jnp.sum(jnp.where(row == 5, tiles, 0.0), axis=0, keepdims=True)
    energy = jnp.sum(jnp.where(row == 5, upper, 0.0), axis=0, keepdims=True)
    h = jnp.where(row < 4, tiles, pltpu.roll(upper, 4, 0)) / top
    y = exact_dot(inv_ref[...], h, ((1,), (0,)))
    hy = jnp.sum(h * y, axis=0, keepdims=True)
    alpha = energy / pq
    scaled = alpha * top
    new = energy - 2.0 * (alpha * wq) + (scaled * scaled) * (qq - hy)
    beta = new / energy
    y = y * top
    here = pl.ds(pl.multiple_of(col * NLAY, NLAY), NLAY)
    for f in range(6):
        y_ref[...] = y - shifted(y, f)
        out_ref[:, f, :] = y_ref[here, :]
    out_ref[:, 6, :] = jnp.broadcast_to(alpha, (NLAY, CASES))
    out_ref[:, 7, :] = jnp.broadcast_to(beta, (NLAY, CASES))


def solve(info, inverse, gathered):
    return pl.pallas_call(
        solve_kernel,
        in_specs=[SMEM, pl.BlockSpec(memory_space=pltpu.VMEM), pl.BlockSpec(memory_space=pltpu.VMEM)],
        out_specs=pl.BlockSpec(memory_space=pltpu.VMEM),
        out_shape=out((8, 8, CASES)),
        scratch_shapes=[pltpu.VMEM((COUNT, CASES), F32)],
        cost_estimate=cost(1e8, 1e6),
        name="solve_step",
    )(info, inverse, gathered)


ANY = pl.BlockSpec(memory_space=pl.ANY)
SCRATCH = [
    pltpu.VMEM((M, SPECIES * CASES), BF16),
    pltpu.VMEM((M, 2 * SPECIES * CASES), BF16),
    pltpu.VMEM((M, M), BF16),
    pltpu.VMEM((M, M), BF16),
    pltpu.VMEM((SPECIES, M, M), BF16),
    pltpu.SemaphoreType.DMA((SPECIES,)),
]


def fetches(flux_ref, scratch):
    flux_vmem, sems = scratch[4:]
    return [
        pltpu.make_async_copy(flux_ref.at[k], flux_vmem.at[k], sems.at[k])
        for k in range(SPECIES)
    ]


def store_direction(k, value, scratch):
    for s in range(SPECIES):

        @pl.when(k == s)
        def _():
            scratch[0][:, s * CASES : (s + 1) * CASES] = value.astype(BF16)


def apply_all(row_ref, col_ref, copies, scratch):
    x_ref, both_ref, o_vmem, ot_vmem, flux_vmem, _ = scratch
    wide = SPECIES * CASES
    fill_gather(col_ref, o_vmem)
    x_ref[...] = jnp.dot(o_vmem[...], x_ref[...], preferred_element_type=F32).astype(BF16)
    fill_scatter(row_ref, ot_vmem)
    for k in range(SPECIES):
        here = slice(k * CASES, (k + 1) * CASES)
        copies[k].wait()
        image = jnp.dot(flux_vmem[k], x_ref[:, here], preferred_element_type=F32)
        high = image.astype(BF16)
        both_ref[:, here] = high
        both_ref[:, wide + k * CASES : wide + (k + 1) * CASES] = (
            image - high.astype(F32)
        ).astype(BF16)


def moved_back(scratch, start, size):
    both_ref, ot_vmem = scratch[1], scratch[3]
    wide = SPECIES * CASES
    both = jnp.dot(ot_vmem[start : start + size, :], both_ref[...], preferred_element_type=F32)
    return both[:, :wide] + both[:, wide:]


def store_faces(scratch, faces):
    for first in (0, 2, 4):
        begin = STARTS[first]
        image = moved_back(scratch, begin, SIZES[first] + SIZES[first + 1])
        for f in (first, first + 1):
            offset = STARTS[f] - begin
            for k in range(SPECIES):
                faces[f][k] = image[offset : offset + SIZES[f], k * CASES : (k + 1) * CASES]


def merged(ref):
    lane = lax.broadcasted_iota(jnp.int32, ref.shape[1:], 1)
    return jnp.where(lane < HALF, ref[0], pltpu.roll(ref[1], HALF, 1))


def turned_dot(rt, values):
    left = jnp.concatenate(split3(rt), axis=0).astype(BF16)
    right = jnp.concatenate([values] * 3, axis=0).astype(BF16)
    return lax.dot_general(left, right, (((0,), (0,)), ((), ())), preferred_element_type=F32)


def start_kernel(gap_ref, rt_ref, back_ref, row_ref, col_ref, flux_ref, *refs):
    arrived = refs[:6]
    p_ref = refs[6]
    faces = refs[7:13]
    scratch = refs[13:]
    k = pl.program_id(0)
    copies = fetches(flux_ref, scratch)

    @pl.when(k == 0)
    def _():
        for copy in copies:
            copy.start()

    @pl.when(k < SPECIES)
    def _():
        table = merged(back_ref)
        own = turned_dot(rt_ref[0], table[8:16])
        for f in range(6):
            start, size = STARTS[f], SIZES[f]
            theirs = table[16 + 8 * f : 24 + 8 * f]
            other = turned_dot(arrived[f][0, size : size + 8, :], theirs)
            if size > CASES:
                more = turned_dot(arrived[f][0, size + 8 : size + 16, :], theirs)
                other = jnp.concatenate([other, more[: size - CASES]], axis=0)
            resid = (gap_ref[0, start : start + size, :] - own[start : start + size]) - (
                arrived[f][0, :size, :] - other
            )
            p_ref[0, start : start + size, :] = resid - table[f : f + 1, :]
        store_direction(k, p_ref[0], scratch)

    @pl.when(k == SPECIES)
    def _():
        apply_all(row_ref, col_ref, copies, scratch)
        store_faces(scratch, faces)


VECTOR = (SPECIES, M, CASES)
FACES = [(SPECIES, size, CASES) for size in SIZES]


def start(gap, rt, back, row, column, flux, arrived):
    return pl.pallas_call(
        start_kernel,
        grid=(SPECIES + 1,),
        in_specs=[
            per_species(M, CASES),
            per_species(8, M),
            pair(64, CASES),
            whole(1, M),
            whole(M, 1),
            ANY,
        ]
        + [per_species(SIZES[f] + TAILS[f], CASES) for f in range(6)],
        out_specs=[per_species(M, CASES)] + [whole(*shape) for shape in FACES],
        out_shape=[out(VECTOR)] + [out(shape) for shape in FACES],
        scratch_shapes=SCRATCH,
        compiler_params=params(),
        cost_estimate=cost(4e9, 20e6),
        name="start",
    )(gap, rt, back, row, column, flux, *arrived)


def weights(info_ref):
    col, lay = info_ref[0], info_ref[1]
    xpos, ypos = col // YCOLS, col % YCOLS
    flags = [
        xpos > 0,
        xpos < NCOL // YCOLS - 1,
        ypos > 0,
        ypos < YCOLS - 1,
        lay > 0,
        lay < NLAY - 1,
    ]
    return [jnp.where(flag, 0.5, 1.0).astype(F32) for flag in flags]


def dots_kernel(same, info_ref, *refs):
    count = 1 if same else 2
    p_ref = refs[0]
    w_ref = refs[count - 1]
    faces = refs[count : count + 6]
    arrived = refs[count + 6 : count + 12]
    q_ref, msg_ref = refs[count + 12 :]
    weight = weights(info_ref)
    top = jnp.zeros((1, CASES), F32)
    for f in range(6):
        q = faces[f][0] - arrived[f][0]
        q_ref[0, STARTS[f] : STARTS[f] + SIZES[f], :] = q
        top = jnp.maximum(top, jnp.max(jnp.abs(q), axis=0, keepdims=True))
    top = jnp.where(top > 0.0, top, 1e-30)
    head, pq, qq, wq, ww = [jnp.zeros((1, CASES), F32) for _ in range(5)]

    def total(value):
        return jnp.sum(value, axis=0, keepdims=True)

    for f in range(6):
        here = slice(STARTS[f], STARTS[f] + SIZES[f])
        q = q_ref[0, here, :]
        p = p_ref[0, here, :]
        unit = q / top
        head = head + total(q)
        pq = pq + weight[f] * total(p * q)
        qq = qq + weight[f] * total(unit * unit)
        if same:
            ww = ww + weight[f] * total(p * p)
        else:
            w = w_ref[0, here, :]
            wq = wq + weight[f] * total(w * q)
            ww = ww + weight[f] * total(w * w)
    if same:
        wq = pq
    zero = jnp.zeros((1, CASES), F32)
    rows = (head, pq, qq, wq, ww, top, zero, zero)
    for r in range(8):
        msg_ref[0, r : r + 1, :] = rows[r]
        msg_ref[1, r : r + 1, :] = rows[r]


def dots(info, vectors, faces, arrived):
    same = len(vectors) == 1
    return pl.pallas_call(
        functools.partial(dots_kernel, same),
        grid=(SPECIES,),
        in_specs=[SMEM]
        + [per_species(M, CASES)] * len(vectors)
        + [per_species(s, CASES) for s in SIZES] * 2,
        out_specs=[per_species(M, CASES), pair(8, CASES)],
        out_shape=[out(VECTOR), out((8, 8, CASES))],
        compiler_params=params(),
        cost_estimate=cost(1e7, 10e6),
        name="dots",
    )(info, *vectors, *faces, *arrived)


def step_kernel(same, last, info_ref, back_ref, row_ref, col_ref, flux_ref, *refs):
    count = 1 if same else 2
    p_ref = refs[0]
    w_ref = refs[count - 1]
    q_ref = refs[count]
    outs = refs[count + 1 : -len(SCRATCH) - 1]
    scratch = refs[-len(SCRATCH) - 1 : -1]
    held_ref = refs[-1]
    k = pl.program_id(0)
    copies = fetches(flux_ref, scratch)

    @pl.when(k == 0)
    def _():
        for copy in copies:
            copy.start()

    @pl.when(k < SPECIES)
    def _():
        table = merged(back_ref)
        alpha, beta = table[6:7], table[7:8]
        weight = weights(info_ref)
        ww = jnp.zeros((1, CASES), F32)
        for f in range(6):
            here = slice(STARTS[f], STARTS[f] + SIZES[f])
            w = w_ref[0, here, :] - alpha * (q_ref[0, here, :] - table[f : f + 1, :])
            if last:
                ww = ww + weight[f] * jnp.sum(w * w, axis=0, keepdims=True)
            else:
                outs[1][0, here, :] = w
            outs[0][0, here, :] = w + beta * p_ref[0, here, :]
        store_direction(k, outs[0][0], scratch)
        if last:
            held_ref[k] = outs[0][0]
            row = lax.broadcasted_iota(jnp.int32, (NLAY, 8, CASES), 1)
            outs[1][...] = jnp.where(row == k + SPECIES, ww[None], outs[1][...])

    @pl.when(k == SPECIES)
    def _():
        apply_all(row_ref, col_ref, copies, scratch)
        if not last:
            store_faces(scratch, outs[2:])
            return
        sums = [jnp.zeros((1, CASES), F32) for _ in range(SPECIES)]
        for i in range(0, M, M // 2):
            image = moved_back(scratch, i, M // 2)
            for s in range(SPECIES):
                part = held_ref[s, i : i + M // 2] * image[:, s * CASES : (s + 1) * CASES]
                sums[s] = sums[s] + jnp.sum(part, axis=0, keepdims=True)
        for s in range(SPECIES):
            pq = sums[s]
            for l in range(NLAY):
                outs[1][l, s : s + 1, :] = pq


def step(info, back, row, column, flux, vectors, q, last):
    same = len(vectors) == 1
    out_specs = [per_species(M, CASES)]
    out_shape = [out(VECTOR)]
    if last:
        out_specs += [whole(NLAY, 8, CASES)]
        out_shape += [out((NLAY, 8, CASES))]
    else:
        out_specs += [per_species(M, CASES)] + [whole(*shape) for shape in FACES]
        out_shape += [out(VECTOR)] + [out(shape) for shape in FACES]
    held = pltpu.VMEM(VECTOR if last else (1, 8, CASES), F32)
    return pl.pallas_call(
        functools.partial(step_kernel, same, last),
        grid=(SPECIES + 1,),
        in_specs=[SMEM, pair(8, CASES), whole(1, M), whole(M, 1), ANY]
        + [per_species(M, CASES)] * (len(vectors) + 1),
        out_specs=out_specs,
        out_shape=out_shape,
        scratch_shapes=SCRATCH + [held],
        compiler_params=params(),
        cost_estimate=cost(4e9, 20e6),
        name="step",
    )(info, back, row, column, flux, *vectors, q)


def finish_kernel(first_ref, back0_ref, back1_ref, sums_ref, p0_ref, p1_ref, p2_ref, out_ref):
    k = pl.program_id(0)
    sums = jnp.sum(sums_ref[...], axis=0)
    row = lax.broadcasted_iota(jnp.int32, (8, CASES), 0)
    pq = jnp.sum(jnp.where(row == k, sums, 0.0), axis=0, keepdims=True)
    ww = jnp.sum(jnp.where(row == k + SPECIES, sums, 0.0), axis=0, keepdims=True)
    initial = merged(first_ref)
    alpha0 = merged(back0_ref)[6:7]
    alpha1 = merged(back1_ref)[6:7]
    alpha2 = ww / pq
    for f in range(6):
        here = slice(STARTS[f], STARTS[f] + SIZES[f])
        value = initial[8 + f : 9 + f] + alpha0 * p0_ref[0, here, :]
        value = value + alpha1 * p1_ref[0, here, :]
        out_ref[0, here, :] = value + alpha2 * p2_ref[0, here, :]


def finish(first, back0, back1, sums, p0, p1, p2):
    return pl.pallas_call(
        finish_kernel,
        grid=(SPECIES,),
        in_specs=[pair(64, CASES), pair(8, CASES), pair(8, CASES), whole(NCOL, 8, CASES)]
        + [per_species(M, CASES)] * 3,
        out_specs=per_species(M, CASES),
        out_shape=out(VECTOR),
        compiler_params=params(),
        cost_estimate=cost(1e7, 8e6),
        name="finish",
    )(first, back0, back1, sums, p0, p1, p2)


def exchange(blocks):
    def moved(value, axis, pairs):
        return lax.ppermute(value, axis, pairs)

    def along_x(step):
        return [(c, c + step) for c in range(NCOL) if 0 <= c + step < NCOL]

    def along_y(step):
        return [(c, c + step) for c in range(NCOL) if 0 <= c % YCOLS + step < YCOLS]

    def along_z(step):
        return [(l, l + step) for l in range(NLAY) if 0 <= l + step < NLAY]

    return [
        moved(blocks[1], "col", along_x(YCOLS)),
        moved(blocks[0], "col", along_x(-YCOLS)),
        moved(blocks[3], "col", along_y(1)),
        moved(blocks[2], "col", along_y(-1)),
        moved(blocks[5], "lay", along_z(1)),
        moved(blocks[4], "lay", along_z(-1)),
    ]


def swap(value, axis):
    return lax.all_to_all(value, axis, 0, 0, tiled=True)


def to_columns(value):
    return swap(jnp.broadcast_to(value[None], (NCOL,) + value.shape), "col")


def shards(flux_operator, dof_order, local_gap, rigid_load):
    flux = flux_operator[0, 0]
    order = dof_order[0, 0]
    gap = local_gap[0, 0]
    load = rigid_load[0, 0]
    info = jnp.stack([lax.axis_index("col"), lax.axis_index("lay")]).astype(jnp.int32)
    inverse = jnp.asarray(coarse_inverse())

    row, column = order.reshape(1, M), order.reshape(M, 1)
    rt, message, *faces = prep(row, column, flux, gap, load)
    arrived = exchange(faces)
    packed_start = mid0(info, swap(message, "lay"))
    back_first = swap(solve0(info, inverse, swap(packed_start, "col")), "lay")
    p0, *faces = start(gap, rt, back_first, row, column, flux, arrived)

    q, message = dots(info, [p0], faces, exchange(faces))
    gathered = swap(mid(info, swap(message, "lay")), "col")
    back0 = swap(solve(info, inverse, gathered), "lay")
    p1, w1, *faces = step(info, back0, row, column, flux, [p0], q, False)

    q, message = dots(info, [p1, w1], faces, exchange(faces))
    gathered = swap(mid(info, swap(message, "lay")), "col")
    back1 = swap(solve(info, inverse, gathered), "lay")
    p2, message = step(info, back1, row, column, flux, [p1, w1], q, True)

    sums = to_columns(jnp.sum(swap(message, "lay"), axis=0))
    return finish(back_first, back0, back1, sums, p0, p1, p2)[None, None]


def solution(mesh):
    return jax.shard_map(
        shards,
        mesh=mesh,
        in_specs=(
            P("col", "lay", None, None, None),
            P("col", "lay", None),
            P("col", "lay", None, None, None),
            P("col", "lay", None, None),
        ),
        out_specs=P("col", "lay", None, None, None),
        check_vma=False,
    )
```

time: 399 us -> 352 us (0.88)
  Pallas kernels: 78 us -> 56.7 us
  blocking collectives: 122 us -> 104 us
  starting transfers between devices: 106 us -> 95.4 us
  waiting for transfers between devices: 59.2 us -> 66.8 us
  local copies, waits for them, and re-layouts: 32.2 us -> 26 us
    all_to_all x9 -> x8, blocking collectives: 122 us -> 104 us  [swap(): return lax.all_to_all(value, axis, 0, 0, tiled=True)]
    all_to_all x2 -> x3, starting transfers between devices: 35.9 us -> 21.1 us  [swap(): return lax.all_to_all(value, axis, 0, 0, tiled=True)]
    pallas_call x6 -> x7, Pallas kernels: 55.9 us -> 42.3 us  [the longest x2 20.9 us: step(): pl.pallas_call(functools.partial(step_kernel, same, last), grid=(SPECIES...]
    ppermute x18, waiting for transfers between devices: 49.6 us -> 62.6 us  [moved(): return lax.ppermute(value, axis, pairs)]
    pallas_call x1, Pallas kernels: 9.76 us -> 3.31 us  [prep(): pl.pallas_call(prep_kernel, grid=(SPECIES,), in_specs=[whole(1, M), whole...]
    all_to_all x2 -> x3, waiting for transfers between devices: 9.64 us -> 4.15 us  [swap(): return lax.all_to_all(value, axis, 0, 0, tiled=True)]
    unnamed x68 -> x52, local copies, waits for them, and re-layouts: 30.2 us -> 25.1 us
    ppermute x18, starting transfers between devices: 70.1 us -> 74.3 us  [moved(): return lax.ppermute(value, axis, pairs)]
  transfers between devices with their start and end apart: 20 -> 21, of which waited for: 10 -> 10; matrix products, arithmetic and copies ran while one was open for 0% -> 0% of each run, Pallas kernels for 1% -> 1%
where the time goes in v2:
time: 352 us; the launch traced here: 350 us
  blocking collectives  104 us (30%)
  starting transfers between devices  95.4 us (27%)
  waiting for transfers between devices  66.8 us (19%)
  Pallas kernels  56.7 us (16%)
  local copies, waits for them, and re-layouts  26 us (7%)
    all_to_all x8, blocking collectives, swap(): return lax.all_to_all(value, axis, 0, 0, tiled=True)  104 us
    ppermute x18, starting transfers between devices, moved(): return lax.ppermute(value, axis, pairs)  74.3 us
    ppermute x18, waiting for transfers between devices, moved(): return lax.ppermute(value, axis, pairs)  62.6 us
    unnamed x52, local copies, waits for them, and re-layouts  25.1 us
    all_to_all x3, starting transfers between devices, swap(): return lax.all_to_all(value, axis, 0, 0, tiled=True)  21.1 us
    pallas_call x2, Pallas kernels, step(): pl.pallas_call(functools.partial(step_kernel, same, last), grid=(SPECIES...  20.9 us
    pallas_call x1, Pallas kernels, start(): pl.pallas_call(start_kernel, grid=(SPECIES + 1,), in_specs=[per_species(M...  14.3 us
  transfers between devices with their start and end apart: 21, of which 10 were waited for; matrix products, arithmetic and copies ran while one was open for 0% of the time, Pallas kernels for 1%

profile of v2, /device:TPU:1, one launch (start us, length us, event | category | flops | bytes accessed | tf_op | source)
XLA Modules:
  0.0 349.9 jit_solution(12684201350680734877)
XLA Ops:
  11.3 6.6 %all-to-all-start = ((f32[8,8,128]{2,1,0:T(8,128)}), f32[8,8,128]{2,1,0:T(8,128)S(1)}, u32[]{:S(2)}, u32[]{:S(2)}) async-start(f32[8,8,128]{2,1,0:T(8,128)} %get-tuple-element.34), calls=%async_computation | async-start | bytes 65536 | tf_op jit(solution)/shard_map/all_to_all | solution.py:703
  18.5 4.1 %all-to-all-done.got_ref = f32[8,8,128]{2,1,0:T(8,128)S(1)} async-done(((f32[8,8,128]{2,1,0:T(8,128)}), f32[8,8,128]{2,1,0:T(8,128)S(1)}, u32[]{:S(2)}, u32[]{:S(2)}) %all-to-all-start) | async-done | bytes 32800 | tf_op jit(solution)/shard_map/all_to_all | solution.py:703
  25.0 10.5 %all-to-all-start.1 = ((f32[32,4,8,128]{3,2,1,0:T(8,128)}), f32[32,4,8,128]{3,2,1,0:T(8,128)S(1)}, u32[]{:S(2)}, u32[]{:S(2)}) async-start(f32[32,4,8,128]{3,2,1,0:T(8,128)} %pack_start.1), calls=%async_computation.1 | async-start | bytes 1048576 | tf_op jit(solution)/shard_map/all_to_all | solution.py:703
  38.6 8.1 %collective-permute-start = (f32[4,208,128]{2,1,0:T(8,128)S(1)}, f32[4,208,128]{2,1,0:T(8,128)}, u32[]{:S(2)}, u32[]{:S(2)}) collective-permute-start(f32[4,208,128]{2,1,0:T(8,128)S(1)} %get-tuple-element.36), channel_id=1, source_target_pairs={{0,32},{8,40},{16,48},{24,56},{32,64},{40,72},{48,80},{56,88},{64,... | collective-permute-start | bytes 1277960 | tf_op jit(solution)/shard_map/ppermute | solution.py:681
  63.3 16.5 %collective-permute-done.1.refs_1_ = f32[4,208,128]{2,1,0:T(8,128)} collective-permute-done((f32[4,208,128]{2,1,0:T(8,128)S(1)}, f32[4,208,128]{2,1,0:T(8,128)}, u32[]{:S(2)}, u32[]{:S(2)}) %collective-permute-start.1) | collective-permute-done | bytes 426016 | tf_op jit(solution)/shard_map/ppermute | solution.py:681
  82.4 14.3 %start.1 = (f32[4,1024,128]{2,1,0:T(8,128)S(1)}, f32[4,192,128]{2,1,0:T(8,128)S(1)}, f32[4,192,128]{2,1,0:T(8,128)S(1)}, f32[4,192,128]{2,1,0:T(8,128)S(1)}, f32...) custom-call(f32[4,1024,128]{2,1,0:T(8,128)S(1)} %bitcast.13, ...), custom_call_target="tpu_custom_call" | custom-call | flops 4000000000 | bytes 20000000 | tf_op jit(solution)/shard_map/start/pallas_call | solution.py:476
  96.7 4.2 %collective-permute-start.11 = (f32[4,128,128]{2,1,0:T(8,128)S(1)}, f32[4,128,128]{2,1,0:T(8,128)S(1)}, u32[]{:S(2)}, u32[]{:S(2)}) collective-permute-start(f32[4,128,128]{2,1,0:T(8,128)S(1)} %get-tuple-element.47.refs_5_), channel_id=1, source_target_pairs={{1,0},{2,1},{3,2},{4,3},{5,4},{6,5},{7,6},{9,8},{10,9},{11,10},{12... | collective-permute-start | bytes 786440 | tf_op jit(solution)/shard_map/ppermute | solution.py:681
  102.2 20.1 %collective-permute-start.6 = (f32[4,192,128]{2,1,0:T(8,128)S(1)}, f32[4,192,128]{2,1,0:T(8,128)S(1)}, u32[]{:S(2)}, u32[]{:S(2)}) collective-permute-start(f32[4,192,128]{2,1,0:T(8,128)S(1)} %get-tuple-element.44.refs_2_), channel_id=1, source_target_pairs={{0,32},{8,40},{16,48},{24,56},{32,64},{40,72},{48,80},{56,88},{64,... | collective-permute-start | bytes 1179656 | tf_op jit(solution)/shard_map/ppermute | solution.py:681
  140.0 7.6 %collective-permute-done.9.refs_10_ = f32[4,192,128]{2,1,0:T(8,128)S(1)} collective-permute-done((f32[4,192,128]{2,1,0:T(8,128)S(1)}, f32[4,192,128]{2,1,0:T(8,128)S(1)}, u32[]{:S(2)}, u32[]{:S(2)}) %collective-permute-start.9) | collective-permute-done | bytes 393248 | tf_op jit(solution)/shard_map/ppermute | solution.py:681
  147.6 6.0 %collective-permute-done.8.refs_9_ = f32[4,192,128]{2,1,0:T(8,128)S(1)} collective-permute-done((f32[4,192,128]{2,1,0:T(8,128)S(1)}, f32[4,192,128]{2,1,0:T(8,128)S(1)}, u32[]{:S(2)}, u32[]{:S(2)}) %collective-permute-start.8) | collective-permute-done | bytes 393248 | tf_op jit(solution)/shard_map/ppermute | solution.py:681
  156.5 8.1 %all_to_all.55.got_ref = f32[8,8,128]{2,1,0:T(8,128)} all-to-all(f32[8,8,128]{2,1,0:T(8,128)S(1)} %get-tuple-element.49), channel_id=1, replica_groups=mesh['col'=32,'lay'=8] {'lay'}, dimensions={0} | all-to-all | bytes 65536 | tf_op jit(solution)/shard_map/all_to_all | solution.py:703
  166.1 26.8 %all_to_all.56.gathered_ref = f32[32,8,128]{2,1,0:T(8,128)} all-to-all(f32[32,8,128]{2,1,0:T(8,128)} %combine_layers.2), channel_id=1, replica_groups=mesh['col'=32,'lay'=8] {'col'}, dimensions={0} | all-to-all | bytes 262144 | tf_op jit(solution)/shard_map/all_to_all | solution.py:703
  195.1 10.1 %all_to_all.57.back_ref.back0_ref = f32[8,8,128]{2,1,0:T(8,128)S(1)} all-to-all(f32[8,8,128]{2,1,0:T(8,128)} %solve_step.2), channel_id=1, replica_groups=mesh['col'=32,'lay'=8] {'lay'}, dimensions={0} | all-to-all | bytes 65536 | tf_op jit(solution)/shard_map/all_to_all | solution.py:703
  208.3 10.3 %step.2 = (f32[4,1024,128]{2,1,0:T(8,128)S(1)}, f32[4,1024,128]{2,1,0:T(8,128)S(1)}, f32[4,192,128]{2,1,0:T(8,128)S(1)}, f32[4,192,128]{2,1,0:T(8,128)S(1)}, f32...) custom-call(s32[2]{0:T(128)S(1)} %copy-done.15, ...), custom_call_target="tpu_custom_call" | custom-call | flops 4000000000 | bytes 20000000 | tf_op jit(solution)/shard_map/step/pallas_call | solution.py:634
  222.5 7.9 %collective-permute-start.12 = (f32[4,192,128]{2,1,0:T(8,128)S(1)}, f32[4,192,128]{2,1,0:T(8,128)S(1)}, u32[]{:S(2)}, u32[]{:S(2)}) collective-permute-start(f32[4,192,128]{2,1,0:T(8,128)S(1)} %get-tuple-element.54.refs_3_), channel_id=1, source_target_pairs={{0,32},{8,40},{16,48},{24,56},{32,64},{40,72},{48,80},{56,88},{64,... | collective-permute-start | bytes 1179656 | tf_op jit(solution)/shard_map/ppermute | solution.py:681
  235.8 4.0 %collective-permute-start.16 = (f32[4,128,128]{2,1,0:T(8,128)S(1)}, f32[4,128,128]{2,1,0:T(8,128)S(1)}, u32[]{:S(2)}, u32[]{:S(2)}) collective-permute-start(f32[4,128,128]{2,1,0:T(8,128)S(1)} %get-tuple-element.58.refs_7_), channel_id=1, source_target_pairs={{0,1},{1,2},{2,3},{3,4},{4,5},{5,6},{6,7},{8,9},{9,10},{10,11},{11... | collective-permute-start | bytes 786440 | tf_op jit(solution)/shard_map/ppermute | solution.py:681
  243.2 14.7 %collective-permute-done.15.refs_11_ = f32[4,192,128]{2,1,0:T(8,128)S(1)} collective-permute-done((f32[4,192,128]{2,1,0:T(8,128)S(1)}, f32[4,192,128]{2,1,0:T(8,128)S(1)}, u32[]{:S(2)}, u32[]{:S(2)}) %collective-permute-start.15) | collective-permute-done | bytes 393248 | tf_op jit(solution)/shard_map/ppermute | solution.py:681
  257.8 5.7 %collective-permute-done.14.refs_10_ = f32[4,192,128]{2,1,0:T(8,128)S(1)} collective-permute-done((f32[4,192,128]{2,1,0:T(8,128)S(1)}, f32[4,192,128]{2,1,0:T(8,128)S(1)}, u32[]{:S(2)}, u32[]{:S(2)}) %collective-permute-start.14) | collective-permute-done | bytes 393248 | tf_op jit(solution)/shard_map/ppermute | solution.py:681
  266.5 8.3 %all_to_all.58.got_ref = f32[8,8,128]{2,1,0:T(8,128)} all-to-all(f32[8,8,128]{2,1,0:T(8,128)S(1)} %get-tuple-element.59), channel_id=1, replica_groups=mesh['col'=32,'lay'=8] {'lay'}, dimensions={0} | all-to-all | bytes 65536 | tf_op jit(solution)/shard_map/all_to_all | solution.py:703
  276.4 20.5 %all_to_all.59.gathered_ref = f32[32,8,128]{2,1,0:T(8,128)} all-to-all(f32[32,8,128]{2,1,0:T(8,128)} %combine_layers.3), channel_id=1, replica_groups=mesh['col'=32,'lay'=8] {'col'}, dimensions={0} | all-to-all | bytes 262144 | tf_op jit(solution)/shard_map/all_to_all | solution.py:703
  299.1 10.1 %all_to_all.60.back_ref.back1_ref = f32[8,8,128]{2,1,0:T(8,128)S(1)} all-to-all(f32[8,8,128]{2,1,0:T(8,128)} %solve_step.3), channel_id=1, replica_groups=mesh['col'=32,'lay'=8] {'lay'}, dimensions={0} | all-to-all | bytes 65536 | tf_op jit(solution)/shard_map/all_to_all | solution.py:703
  312.3 10.6 %step.3 = (f32[4,1024,128]{2,1,0:T(8,128)S(1)}, f32[8,8,128]{2,1,0:T(8,128)S(1)}) custom-call(s32[2]{0:T(128)S(1)} %copy-done.16, f32[8,8,128]{2,1,0:T(8,128)S(1)} %all_to_all.60.back_ref.back1_ref, s32[1,1024]{1,0:T(1,128)S(1)} %bitcast.18, s32[1024,1]{1,0:T(8,128)S(1)} %copy.6.col_ref, bf16[4,1024,1024]{2,1,0:T(8,128)(2,1)} %bitcast.10, ...), custom_call_target="tpu_custom_call" | custom-call | flops 4000000000 | bytes 20000000 | tf_op jit(solution)/shard_map/step/pallas_call | solution.py:634
  324.3 7.8 %all_to_all.61 = f32[8,8,128]{2,1,0:T(8,128)S(1)} all-to-all(f32[8,8,128]{2,1,0:T(8,128)S(1)} %get-tuple-element.61), channel_id=1, replica_groups=mesh['col'=32,'lay'=8] {'lay'}, dimensions={0} | all-to-all | bytes 65536 | tf_op jit(solution)/shard_map/all_to_all | solution.py:703
  332.1 12.4 %all_to_all.62.sums_ref = f32[32,8,128]{2,1,0:T(8,128)S(1)} all-to-all(f32[32,8,128]{2,1,0:T(8,128)S(1)} %broadcast_in_dim.4), channel_id=1, replica_groups=mesh['col'=32,'lay'=8] {'col'}, dimensions={0} | all-to-all | bytes 262144 | tf_op jit(solution)/shard_map/all_to_all | solution.py:703
  (95 shorter events, 94.2 us)
Async XLA Ops:
  11.3 68.5 %copy-start.18 = (s32[1,1,1024]{2,1,0:T(1,128)S(1)}, s32[1,1,1024]{2,1,0:T(1,128)}, u32[]{:S(2)}) copy-start(s32[1,1,1024]{2,1,0:T(1,128)} %param.6) | copy-start | bytes 12292
  11.3 11.4 %all-to-all-start = ((f32[8,8,128]{2,1,0:T(8,128)}), f32[8,8,128]{2,1,0:T(8,128)S(1)}, u32[]{:S(2)}, u32[]{:S(2)}) async-start(f32[8,8,128]{2,1,0:T(8,128)} %get-tuple-element.34), calls=%async_computation | async-start | bytes 65536 | tf_op jit(solution)/shard_map/all_to_all | solution.py:703
  25.0 29.9 %all-to-all-start.1 = ((f32[32,4,8,128]{3,2,1,0:T(8,128)}), f32[32,4,8,128]{3,2,1,0:T(8,128)S(1)}, u32[]{:S(2)}, u32[]{:S(2)}) async-start(f32[32,4,8,128]{3,2,1,0:T(8,128)} %pack_start.1), calls=%async_computation.1 | async-start | bytes 1048576 | tf_op jit(solution)/shard_map/all_to_all | solution.py:703
  35.5 16.7 %collective-permute-start.4 = (f32[4,136,128]{2,1,0:T(8,128)}, f32[4,136,128]{2,1,0:T(8,128)S(1)}, u32[]{:S(2)}, u32[]{:S(2)}) collective-permute-start(f32[4,136,128]{2,1,0:T(8,128)} %copy-done.24), channel_id=1, source_target_pairs={{0,1},{1,2},{2,3},{3,4},{4,5},{5,6},{6,7},{8,9},{9,10},{10,11},{11... | collective-permute-start | bytes 835592 | tf_op jit(solution)/shard_map/ppermute | solution.py:681
  38.6 24.7 %collective-permute-start = (f32[4,208,128]{2,1,0:T(8,128)S(1)}, f32[4,208,128]{2,1,0:T(8,128)}, u32[]{:S(2)}, u32[]{:S(2)}) collective-permute-start(f32[4,208,128]{2,1,0:T(8,128)S(1)} %get-tuple-element.36), channel_id=1, source_target_pairs={{0,32},{8,40},{16,48},{24,56},{32,64},{40,72},{48,80},{56,88},{64,... | collective-permute-start | bytes 1277960 | tf_op jit(solution)/shard_map/ppermute | solution.py:681
  46.7 33.1 %collective-permute-start.1 = (f32[4,208,128]{2,1,0:T(8,128)S(1)}, f32[4,208,128]{2,1,0:T(8,128)}, u32[]{:S(2)}, u32[]{:S(2)}) collective-permute-start(f32[4,208,128]{2,1,0:T(8,128)S(1)} %get-tuple-element.37), channel_id=1, source_target_pairs={{32,0},{40,8},{48,16},{56,24},{64,32},{72,40},{80,48},{88,56},{96,... | collective-permute-start | bytes 1277960 | tf_op jit(solution)/shard_map/ppermute | solution.py:681
  48.0 31.8 %collective-permute-start.2 = (f32[4,208,128]{2,1,0:T(8,128)S(1)}, f32[4,208,128]{2,1,0:T(8,128)}, u32[]{:S(2)}, u32[]{:S(2)}) collective-permute-start(f32[4,208,128]{2,1,0:T(8,128)S(1)} %get-tuple-element.38), channel_id=1, source_target_pairs={{0,8},{8,16},{16,24},{32,40},{40,48},{48,56},{64,72},{72,80},{80,8... | collective-permute-start | bytes 1277960 | tf_op jit(solution)/shard_map/ppermute | solution.py:681
  51.0 28.8 %collective-permute-start.3 = (f32[4,208,128]{2,1,0:T(8,128)S(1)}, f32[4,208,128]{2,1,0:T(8,128)}, u32[]{:S(2)}, u32[]{:S(2)}) collective-permute-start(f32[4,208,128]{2,1,0:T(8,128)S(1)} %get-tuple-element.39), channel_id=1, source_target_pairs={{8,0},{16,8},{24,16},{40,32},{48,40},{56,48},{72,64},{80,72},{88,8... | collective-permute-start | bytes 1277960 | tf_op jit(solution)/shard_map/ppermute | solution.py:681
  53.0 10.3 %collective-permute-start.5 = (f32[4,136,128]{2,1,0:T(8,128)S(1)}, f32[4,136,128]{2,1,0:T(8,128)}, u32[]{:S(2)}, u32[]{:S(2)}) collective-permute-start(f32[4,136,128]{2,1,0:T(8,128)S(1)} %get-tuple-element.41), channel_id=1, source_target_pairs={{1,0},{2,1},{3,2},{4,3},{5,4},{6,5},{7,6},{9,8},{10,9},{11,10},{12... | collective-permute-start | bytes 835592 | tf_op jit(solution)/shard_map/ppermute | solution.py:681
  59.3 20.5 %all-to-all-start.2 = ((f32[8,64,128]{2,1,0:T(8,128)}), f32[8,64,128]{2,1,0:T(8,128)S(1)}, u32[]{:S(2)}, u32[]{:S(2)}) async-start(f32[8,64,128]{2,1,0:T(8,128)} %solve_start.1), calls=%async_computation.2 | async-start | bytes 524288 | tf_op jit(solution)/shard_map/all_to_all | solution.py:703
  82.4 71.3 %copy-start.14 = (s32[2]{0:T(128)S(1)}, s32[2]{0:T(128)}, u32[]{:S(2)}) copy-start(s32[2]{0:T(128)} %pad_add_fusion.info_ref) | copy-start | bytes 28
  96.7 58.4 %copy-start.1 = (f32[4,1024,128]{2,1,0:T(8,128)}, f32[4,1024,128]{2,1,0:T(8,128)S(1)}, u32[]{:S(2)}) copy-start(f32[4,1024,128]{2,1,0:T(8,128)S(1)} %get-tuple-element.42.refs_0_.p0_ref) | copy-start | bytes 6291460
  96.7 30.9 %collective-permute-start.11 = (f32[4,128,128]{2,1,0:T(8,128)S(1)}, f32[4,128,128]{2,1,0:T(8,128)S(1)}, u32[]{:S(2)}, u32[]{:S(2)}) collective-permute-start(f32[4,128,128]{2,1,0:T(8,128)S(1)} %get-tuple-element.47.refs_5_), channel_id=1, source_target_pairs={{1,0},{2,1},{3,2},{4,3},{5,4},{6,5},{7,6},{9,8},{10,9},{11,10},{12... | collective-permute-start | bytes 786440 | tf_op jit(solution)/shard_map/ppermute | solution.py:681
  100.9 37.5 %collective-permute-start.7 = (f32[4,192,128]{2,1,0:T(8,128)S(1)}, f32[4,192,128]{2,1,0:T(8,128)S(1)}, u32[]{:S(2)}, u32[]{:S(2)}) collective-permute-start(f32[4,192,128]{2,1,0:T(8,128)S(1)} %get-tuple-element.43.refs_1_), channel_id=1, source_target_pairs={{32,0},{40,8},{48,16},{56,24},{64,32},{72,40},{80,48},{88,56},{96,... | collective-permute-start | bytes 1179656 | tf_op jit(solution)/shard_map/ppermute | solution.py:681
  102.2 37.8 %collective-permute-start.6 = (f32[4,192,128]{2,1,0:T(8,128)S(1)}, f32[4,192,128]{2,1,0:T(8,128)S(1)}, u32[]{:S(2)}, u32[]{:S(2)}) collective-permute-start(f32[4,192,128]{2,1,0:T(8,128)S(1)} %get-tuple-element.44.refs_2_), channel_id=1, source_target_pairs={{0,32},{8,40},{16,48},{24,56},{32,64},{40,72},{48,80},{56,88},{64,... | collective-permute-start | bytes 1179656 | tf_op jit(solution)/shard_map/ppermute | solution.py:681
  122.3 25.3 %collective-permute-start.9 = (f32[4,192,128]{2,1,0:T(8,128)S(1)}, f32[4,192,128]{2,1,0:T(8,128)S(1)}, u32[]{:S(2)}, u32[]{:S(2)}) collective-permute-start(f32[4,192,128]{2,1,0:T(8,128)S(1)} %get-tuple-element.45.refs_3_), channel_id=1, source_target_pairs={{8,0},{16,8},{24,16},{40,32},{48,40},{56,48},{72,64},{80,72},{88,8... | collective-permute-start | bytes 1179656 | tf_op jit(solution)/shard_map/ppermute | solution.py:681
  123.6 30.0 %collective-permute-start.8 = (f32[4,192,128]{2,1,0:T(8,128)S(1)}, f32[4,192,128]{2,1,0:T(8,128)S(1)}, u32[]{:S(2)}, u32[]{:S(2)}) collective-permute-start(f32[4,192,128]{2,1,0:T(8,128)S(1)} %get-tuple-element.46.refs_4_), channel_id=1, source_target_pairs={{0,8},{8,16},{16,24},{32,40},{40,48},{48,56},{64,72},{72,80},{80,8... | collective-permute-start | bytes 1179656 | tf_op jit(solution)/shard_map/ppermute | solution.py:681
  127.7 6.9 %collective-permute-start.10 = (f32[4,128,128]{2,1,0:T(8,128)S(1)}, f32[4,128,128]{2,1,0:T(8,128)S(1)}, u32[]{:S(2)}, u32[]{:S(2)}) collective-permute-start(f32[4,128,128]{2,1,0:T(8,128)S(1)} %get-tuple-element.48.refs_6_), channel_id=1, source_target_pairs={{0,1},{1,2},{2,3},{3,4},{4,5},{5,6},{6,7},{8,9},{9,10},{10,11},{11... | collective-permute-start | bytes 786440 | tf_op jit(solution)/shard_map/ppermute | solution.py:681
  218.6 17.2 %collective-permute-start.17 = (f32[4,128,128]{2,1,0:T(8,128)S(1)}, f32[4,128,128]{2,1,0:T(8,128)S(1)}, u32[]{:S(2)}, u32[]{:S(2)}) collective-permute-start(f32[4,128,128]{2,1,0:T(8,128)S(1)} %get-tuple-element.57.refs_6_), channel_id=1, source_target_pairs={{1,0},{2,1},{3,2},{4,3},{5,4},{6,5},{7,6},{9,8},{10,9},{11,10},{12... | collective-permute-start | bytes 786440 | tf_op jit(solution)/shard_map/ppermute | solution.py:681
  221.2 21.9 %collective-permute-start.13 = (f32[4,192,128]{2,1,0:T(8,128)S(1)}, f32[4,192,128]{2,1,0:T(8,128)S(1)}, u32[]{:S(2)}, u32[]{:S(2)}) collective-permute-start(f32[4,192,128]{2,1,0:T(8,128)S(1)} %get-tuple-element.53.refs_2_), channel_id=1, source_target_pairs={{32,0},{40,8},{48,16},{56,24},{64,32},{72,40},{80,48},{88,56},{96,... | collective-permute-start | bytes 1179656 | tf_op jit(solution)/shard_map/ppermute | solution.py:681
  222.5 20.6 %collective-permute-start.12 = (f32[4,192,128]{2,1,0:T(8,128)S(1)}, f32[4,192,128]{2,1,0:T(8,128)S(1)}, u32[]{:S(2)}, u32[]{:S(2)}) collective-permute-start(f32[4,192,128]{2,1,0:T(8,128)S(1)} %get-tuple-element.54.refs_3_), channel_id=1, source_target_pairs={{0,32},{8,40},{16,48},{24,56},{32,64},{40,72},{48,80},{56,88},{64,... | collective-permute-start | bytes 1179656 | tf_op jit(solution)/shard_map/ppermute | solution.py:681
  230.5 27.4 %collective-permute-start.15 = (f32[4,192,128]{2,1,0:T(8,128)S(1)}, f32[4,192,128]{2,1,0:T(8,128)S(1)}, u32[]{:S(2)}, u32[]{:S(2)}) collective-permute-start(f32[4,192,128]{2,1,0:T(8,128)S(1)} %get-tuple-element.55.refs_4_), channel_id=1, source_target_pairs={{8,0},{16,8},{24,16},{40,32},{48,40},{56,48},{72,64},{80,72},{88,8... | collective-permute-start | bytes 1179656 | tf_op jit(solution)/shard_map/ppermute | solution.py:681
  231.8 31.8 %collective-permute-start.14 = (f32[4,192,128]{2,1,0:T(8,128)S(1)}, f32[4,192,128]{2,1,0:T(8,128)S(1)}, u32[]{:S(2)}, u32[]{:S(2)}) collective-permute-start(f32[4,192,128]{2,1,0:T(8,128)S(1)} %get-tuple-element.56.refs_5_), channel_id=1, source_target_pairs={{0,8},{8,16},{16,24},{32,40},{40,48},{48,56},{64,72},{72,80},{80,8... | collective-permute-start | bytes 1179656 | tf_op jit(solution)/shard_map/ppermute | solution.py:681
  235.8 7.3 %collective-permute-start.16 = (f32[4,128,128]{2,1,0:T(8,128)S(1)}, f32[4,128,128]{2,1,0:T(8,128)S(1)}, u32[]{:S(2)}, u32[]{:S(2)}) collective-permute-start(f32[4,128,128]{2,1,0:T(8,128)S(1)} %get-tuple-element.58.refs_7_), channel_id=1, source_target_pairs={{0,1},{1,2},{2,3},{3,4},{4,5},{5,6},{6,7},{8,9},{9,10},{10,11},{11... | collective-permute-start | bytes 786440 | tf_op jit(solution)/shard_map/ppermute | solution.py:681
  (23 other events, 216.4 us)

commit v3 on v2

--- a/solution.py
+++ b/solution.py
@@ -24,7 +24,8 @@
 HALF = CASES // 2
 F32 = jnp.float32
 BF16 = jnp.bfloat16
-VMEM_LIMIT = 40 * 1024 * 1024
+MIB = 1024 * 1024
+VMEM_LIMIT = 40 * MIB
 
 
 def coarse_inverse():
@@ -40,10 +41,14 @@
     return np.linalg.inv(matrix).astype(np.float32)
 
 
-def params():
+def params(limit=VMEM_LIMIT):
     return pltpu.CompilerParams(
-        dimension_semantics=("arbitrary",), vmem_limit_bytes=VMEM_LIMIT
+        dimension_semantics=("arbitrary",), vmem_limit_bytes=limit
     )
+
+
+def small(limit):
+    return pltpu.CompilerParams(vmem_limit_bytes=limit * MIB)
 
 
 def cost(flops, nbytes):
@@ -225,6 +230,7 @@
         in_specs=[SMEM, pl.BlockSpec(memory_space=pltpu.VMEM)],
         out_specs=pl.BlockSpec(memory_space=pltpu.VMEM),
         out_shape=out((NCOL, 4, 8, CASES)),
+        compiler_params=small(6),
         cost_estimate=cost(1e5, 6e5),
         name="pack_start",
     )(info, got)
@@ -283,7 +289,7 @@
         out_specs=pl.BlockSpec(memory_space=pltpu.VMEM),
         out_shape=out((8, 64, CASES)),
         scratch_shapes=[pltpu.VMEM((6, COUNT, CASES), F32)],
-        compiler_params=pltpu.CompilerParams(vmem_limit_bytes=VMEM_LIMIT),
+        compiler_params=small(16),
         cost_estimate=cost(1e8, 2e6),
         name="solve_start",
     )(info, inverse, gathered)
@@ -315,9 +321,30 @@
         in_specs=[SMEM, pl.BlockSpec(memory_space=pltpu.VMEM)],
         out_specs=pl.BlockSpec(memory_space=pltpu.VMEM),
         out_shape=out((NCOL, 8, CASES)),
+        compiler_params=small(4),
         cost_estimate=cost(1e5, 3e5),
         name="combine_layers",
     )(info, got)
+
+
+def last_kernel(got_ref, out_ref):
+    total = got_ref[0]
+    for l in range(1, NLAY):
+        total = total + got_ref[l]
+    for c in range(NCOL):
+        out_ref[c] = total
+
+
+def last_mid(got):
+    return pl.pallas_call(
+        last_kernel,
+        in_specs=[pl.BlockSpec(memory_space=pltpu.VMEM)],
+        out_specs=pl.BlockSpec(memory_space=pltpu.VMEM),
+        out_shape=out((NCOL, 8, CASES)),
+        compiler_params=small(4),
+        cost_estimate=cost(1e5, 3e5),
+        name="combine_last",
+    )(got)
 
 
 def solve_kernel(info_ref, inv_ref, gathered_ref, out_ref, y_ref):
@@ -355,6 +382,7 @@
         out_specs=pl.BlockSpec(memory_space=pltpu.VMEM),
         out_shape=out((8, 8, CASES)),
         scratch_shapes=[pltpu.VMEM((COUNT, CASES), F32)],
+        compiler_params=small(6),
         cost_estimate=cost(1e8, 1e6),
         name="solve_step",
     )(info, inverse, gathered)
@@ -560,7 +588,7 @@
         + [per_species(s, CASES) for s in SIZES] * 2,
         out_specs=[per_species(M, CASES), pair(8, CASES)],
         out_shape=[out(VECTOR), out((8, 8, CASES))],
-        compiler_params=params(),
+        compiler_params=params(16 * MIB),
         cost_estimate=cost(1e7, 10e6),
         name="dots",
     )(info, *vectors, *faces, *arrived)
@@ -670,7 +698,7 @@
         + [per_species(M, CASES)] * 3,
         out_specs=per_species(M, CASES),
         out_shape=out(VECTOR),
-        compiler_params=params(),
+        compiler_params=params(16 * MIB),
         cost_estimate=cost(1e7, 8e6),
         name="finish",
     )(first, back0, back1, sums, p0, p1, p2)
@@ -703,10 +731,6 @@
     return lax.all_to_all(value, axis, 0, 0, tiled=True)
 
 
-def to_columns(value):
-    return swap(jnp.broadcast_to(value[None], (NCOL,) + value.shape), "col")
-
-
 def shards(flux_operator, dof_order, local_gap, rigid_load):
     flux = flux_operator[0, 0]
     order = dof_order[0, 0]
@@ -732,7 +756,7 @@
     back1 = swap(solve(info, inverse, gathered), "lay")
     p2, message = step(info, back1, row, column, flux, [p1, w1], q, True)
 
-    sums = to_columns(jnp.sum(swap(message, "lay"), axis=0))
+    sums = swap(last_mid(swap(message, "lay")), "col")
     return finish(back_first, back0, back1, sums, p0, p1, p2)[None, None]
 
 

time: 352 us -> 332 us (0.943)
  local copies, waits for them, and re-layouts: 26 us -> 14.1 us
  Pallas kernels: 56.7 us -> 52.1 us
  blocking collectives: 104 us -> 100 us
    unnamed x52 -> x32, local copies, waits for them, and re-layouts: 25.1 us -> 13.2 us
    all_to_all x8, blocking collectives: 104 us -> 100 us  [swap(): return lax.all_to_all(value, axis, 0, 0, tiled=True)]
where the time goes in v3:
time: 332 us; the launch traced here: 330 us
  blocking collectives  100 us (30%)
  starting transfers between devices  95.6 us (29%)
  waiting for transfers between devices  67.8 us (20%)
  Pallas kernels  52.1 us (16%)
  local copies, waits for them, and re-layouts  14.1 us (4%)
    all_to_all x8, blocking collectives, swap(): return lax.all_to_all(value, axis, 0, 0, tiled=True)  100 us
    ppermute x18, starting transfers between devices, moved(): return lax.ppermute(value, axis, pairs)  74.5 us
    ppermute x18, waiting for transfers between devices, moved(): return lax.ppermute(value, axis, pairs)  63.1 us
    all_to_all x3, starting transfers between devices, swap(): return lax.all_to_all(value, axis, 0, 0, tiled=True)  21.1 us
    pallas_call x2, Pallas kernels, step(): pl.pallas_call(functools.partial(step_kernel, same, last), grid=(SPECIES...  20.9 us
    pallas_call x1, Pallas kernels, start(): pl.pallas_call(start_kernel, grid=(SPECIES + 1,), in_specs=[per_species(M...  14.3 us
    unnamed x32, local copies, waits for them, and re-layouts  13.2 us
  transfers between devices with their start and end apart: 21, of which 10 were waited for; matrix products, arithmetic and copies ran while one was open for 0% of the time, Pallas kernels for 1%

profile of v3, /device:TPU:1, one launch (start us, length us, event | category | flops | bytes accessed | tf_op | source)
XLA Modules:
  0.0 330.4 jit_solution(431605330052118357)
XLA Ops:
  15.1 6.6 %all-to-all-start = ((f32[8,8,128]{2,1,0:T(8,128)}), f32[8,8,128]{2,1,0:T(8,128)S(1)}, u32[]{:S(2)}, u32[]{:S(2)}) async-start(f32[8,8,128]{2,1,0:T(8,128)} %get-tuple-element.34), calls=%async_computation | async-start | bytes 65536 | tf_op jit(solution)/shard_map/all_to_all | solution.py:731
  21.8 4.7 %all-to-all-done.got_ref = f32[8,8,128]{2,1,0:T(8,128)S(1)} async-done(((f32[8,8,128]{2,1,0:T(8,128)}), f32[8,8,128]{2,1,0:T(8,128)S(1)}, u32[]{:S(2)}, u32[]{:S(2)}) %all-to-all-start) | async-done | bytes 32800 | tf_op jit(solution)/shard_map/all_to_all | solution.py:731
  28.0 10.5 %all-to-all-start.1 = ((f32[32,4,8,128]{3,2,1,0:T(8,128)}), f32[32,4,8,128]{3,2,1,0:T(8,128)S(1)}, u32[]{:S(2)}, u32[]{:S(2)}) async-start(f32[32,4,8,128]{3,2,1,0:T(8,128)} %pack_start.1), calls=%async_computation.1 | async-start | bytes 1048576 | tf_op jit(solution)/shard_map/all_to_all | solution.py:731
  41.6 8.1 %collective-permute-start = (f32[4,208,128]{2,1,0:T(8,128)}, f32[4,208,128]{2,1,0:T(8,128)}, u32[]{:S(2)}, u32[]{:S(2)}) collective-permute-start(f32[4,208,128]{2,1,0:T(8,128)} %copy-done.11), channel_id=1, source_target_pairs={{0,32},{8,40},{16,48},{24,56},{32,64},{40,72},{48,80},{56,88},{64,... | collective-permute-start | bytes 1277960 | tf_op jit(solution)/shard_map/ppermute | solution.py:709
  65.6 17.1 %collective-permute-done.1.refs_1_ = f32[4,208,128]{2,1,0:T(8,128)} collective-permute-done((f32[4,208,128]{2,1,0:T(8,128)}, f32[4,208,128]{2,1,0:T(8,128)}, u32[]{:S(2)}, u32[]{:S(2)}) %collective-permute-start.1) | collective-permute-done | bytes 426016 | tf_op jit(solution)/shard_map/ppermute | solution.py:709
  83.7 14.3 %start.1 = (f32[4,1024,128]{2,1,0:T(8,128)S(1)}, f32[4,192,128]{2,1,0:T(8,128)S(1)}, f32[4,192,128]{2,1,0:T(8,128)S(1)}, f32[4,192,128]{2,1,0:T(8,128)S(1)}, f32...) custom-call(f32[4,1024,128]{2,1,0:T(8,128)S(1)} %bitcast.13, ...), custom_call_target="tpu_custom_call" | custom-call | flops 4000000000 | bytes 20000000 | tf_op jit(solution)/shard_map/start/pallas_call | solution.py:504
  98.0 4.3 %collective-permute-start.11 = (f32[4,128,128]{2,1,0:T(8,128)S(1)}, f32[4,128,128]{2,1,0:T(8,128)S(1)}, u32[]{:S(2)}, u32[]{:S(2)}) collective-permute-start(f32[4,128,128]{2,1,0:T(8,128)S(1)} %get-tuple-element.47.refs_5_), channel_id=1, source_target_pairs={{1,0},{2,1},{3,2},{4,3},{5,4},{6,5},{7,6},{9,8},{10,9},{11,10},{12... | collective-permute-start | bytes 786440 | tf_op jit(solution)/shard_map/ppermute | solution.py:709
  103.6 20.1 %collective-permute-start.6 = (f32[4,192,128]{2,1,0:T(8,128)S(1)}, f32[4,192,128]{2,1,0:T(8,128)S(1)}, u32[]{:S(2)}, u32[]{:S(2)}) collective-permute-start(f32[4,192,128]{2,1,0:T(8,128)S(1)} %get-tuple-element.44.refs_2_), channel_id=1, source_target_pairs={{0,32},{8,40},{16,48},{24,56},{32,64},{40,72},{48,80},{56,88},{64,... | collective-permute-start | bytes 1179656 | tf_op jit(solution)/shard_map/ppermute | solution.py:709
  137.3 4.1 %collective-permute-done.6.refs_7_ = f32[4,192,128]{2,1,0:T(8,128)S(1)} collective-permute-done((f32[4,192,128]{2,1,0:T(8,128)S(1)}, f32[4,192,128]{2,1,0:T(8,128)S(1)}, u32[]{:S(2)}, u32[]{:S(2)}) %collective-permute-start.6) | collective-permute-done | bytes 393248 | tf_op jit(solution)/shard_map/ppermute | solution.py:709
  141.4 7.7 %collective-permute-done.9.refs_10_ = f32[4,192,128]{2,1,0:T(8,128)S(1)} collective-permute-done((f32[4,192,128]{2,1,0:T(8,128)S(1)}, f32[4,192,128]{2,1,0:T(8,128)S(1)}, u32[]{:S(2)}, u32[]{:S(2)}) %collective-permute-start.9) | collective-permute-done | bytes 393248 | tf_op jit(solution)/shard_map/ppermute | solution.py:709
  149.1 6.0 %collective-permute-done.8.refs_9_ = f32[4,192,128]{2,1,0:T(8,128)S(1)} collective-permute-done((f32[4,192,128]{2,1,0:T(8,128)S(1)}, f32[4,192,128]{2,1,0:T(8,128)S(1)}, u32[]{:S(2)}, u32[]{:S(2)}) %collective-permute-start.8) | collective-permute-done | bytes 393248 | tf_op jit(solution)/shard_map/ppermute | solution.py:709
  156.6 7.4 %all_to_all.55.got_ref = f32[8,8,128]{2,1,0:T(8,128)S(1)} all-to-all(f32[8,8,128]{2,1,0:T(8,128)S(1)} %get-tuple-element.49), channel_id=1, replica_groups=mesh['col'=32,'lay'=8] {'lay'}, dimensions={0} | all-to-all | bytes 65536 | tf_op jit(solution)/shard_map/all_to_all | solution.py:731
  164.8 26.2 %all_to_all.56.gathered_ref = f32[32,8,128]{2,1,0:T(8,128)S(1)} all-to-all(f32[32,8,128]{2,1,0:T(8,128)S(1)} %combine_layers.2), channel_id=1, replica_groups=mesh['col'=32,'lay'=8] {'col'}, dimensions={0} | all-to-all | bytes 262144 | tf_op jit(solution)/shard_map/all_to_all | solution.py:731
  192.1 9.2 %all_to_all.57.back_ref.back0_ref = f32[8,8,128]{2,1,0:T(8,128)S(1)} all-to-all(f32[8,8,128]{2,1,0:T(8,128)S(1)} %solve_step.2), channel_id=1, replica_groups=mesh['col'=32,'lay'=8] {'lay'}, dimensions={0} | all-to-all | bytes 65536 | tf_op jit(solution)/shard_map/all_to_all | solution.py:731
  201.3 10.3 %step.2 = (f32[4,1024,128]{2,1,0:T(8,128)S(1)}, f32[4,1024,128]{2,1,0:T(8,128)S(1)}, f32[4,192,128]{2,1,0:T(8,128)S(1)}, f32[4,192,128]{2,1,0:T(8,128)S(1)}, f32...) custom-call(s32[2]{0:T(128)S(1)} %pad_add_fusion.info_ref, ...), custom_call_target="tpu_custom_call" | custom-call | flops 4000000000 | bytes 20000000 | tf_op jit(solution)/shard_map/step/pallas_call | solution.py:662
  215.6 7.9 %collective-permute-start.12 = (f32[4,192,128]{2,1,0:T(8,128)S(1)}, f32[4,192,128]{2,1,0:T(8,128)S(1)}, u32[]{:S(2)}, u32[]{:S(2)}) collective-permute-start(f32[4,192,128]{2,1,0:T(8,128)S(1)} %get-tuple-element.54.refs_3_), channel_id=1, source_target_pairs={{0,32},{8,40},{16,48},{24,56},{32,64},{40,72},{48,80},{56,88},{64,... | collective-permute-start | bytes 1179656 | tf_op jit(solution)/shard_map/ppermute | solution.py:709
  236.2 14.7 %collective-permute-done.15.refs_11_ = f32[4,192,128]{2,1,0:T(8,128)S(1)} collective-permute-done((f32[4,192,128]{2,1,0:T(8,128)S(1)}, f32[4,192,128]{2,1,0:T(8,128)S(1)}, u32[]{:S(2)}, u32[]{:S(2)}) %collective-permute-start.15) | collective-permute-done | bytes 393248 | tf_op jit(solution)/shard_map/ppermute | solution.py:709
  250.8 5.7 %collective-permute-done.14.refs_10_ = f32[4,192,128]{2,1,0:T(8,128)S(1)} collective-permute-done((f32[4,192,128]{2,1,0:T(8,128)S(1)}, f32[4,192,128]{2,1,0:T(8,128)S(1)}, u32[]{:S(2)}, u32[]{:S(2)}) %collective-permute-start.14) | collective-permute-done | bytes 393248 | tf_op jit(solution)/shard_map/ppermute | solution.py:709
  258.2 7.6 %all_to_all.58.got_ref = f32[8,8,128]{2,1,0:T(8,128)S(1)} all-to-all(f32[8,8,128]{2,1,0:T(8,128)S(1)} %get-tuple-element.59), channel_id=1, replica_groups=mesh['col'=32,'lay'=8] {'lay'}, dimensions={0} | all-to-all | bytes 65536 | tf_op jit(solution)/shard_map/all_to_all | solution.py:731
  266.5 20.4 %all_to_all.59.gathered_ref = f32[32,8,128]{2,1,0:T(8,128)S(1)} all-to-all(f32[32,8,128]{2,1,0:T(8,128)S(1)} %combine_layers.3), channel_id=1, replica_groups=mesh['col'=32,'lay'=8] {'col'}, dimensions={0} | all-to-all | bytes 262144 | tf_op jit(solution)/shard_map/all_to_all | solution.py:731
  288.0 9.2 %all_to_all.60.back_ref.back1_ref = f32[8,8,128]{2,1,0:T(8,128)S(1)} all-to-all(f32[8,8,128]{2,1,0:T(8,128)S(1)} %solve_step.3), channel_id=1, replica_groups=mesh['col'=32,'lay'=8] {'lay'}, dimensions={0} | all-to-all | bytes 65536 | tf_op jit(solution)/shard_map/all_to_all | solution.py:731
  297.3 10.6 %step.3 = (f32[4,1024,128]{2,1,0:T(8,128)S(1)}, f32[8,8,128]{2,1,0:T(8,128)S(1)}) custom-call(s32[2]{0:T(128)S(1)} %pad_add_fusion.info_ref, f32[8,8,128]{2,1,0:T(8,128)S(1)} %all_to_all.60.back_ref.back1_ref, s32[1,1024]{1,0:T(1,128)S(1)} %bitcast.18, s32[1024,1]{1,0:T(8,128)S(1)} %copy.6.col_ref, bf16[4,1024,1024]{2,1,0:T(8,128)(2,1)} %bitcast.10, ...), custom_call_target="tpu_custom_call" | custom-call | flops 4000000000 | bytes 20000000 | tf_op jit(solution)/shard_map/step/pallas_call | solution.py:662
  307.9 7.8 %all_to_all.61.got_ref = f32[8,8,128]{2,1,0:T(8,128)S(1)} all-to-all(f32[8,8,128]{2,1,0:T(8,128)S(1)} %get-tuple-element.61), channel_id=1, replica_groups=mesh['col'=32,'lay'=8] {'lay'}, dimensions={0} | all-to-all | bytes 65536 | tf_op jit(solution)/shard_map/all_to_all | solution.py:731
  315.7 12.4 %all_to_all.62.sums_ref = f32[32,8,128]{2,1,0:T(8,128)S(1)} all-to-all(f32[32,8,128]{2,1,0:T(8,128)S(1)} %combine_last.1), channel_id=1, replica_groups=mesh['col'=32,'lay'=8] {'col'}, dimensions={0} | all-to-all | bytes 262144 | tf_op jit(solution)/shard_map/all_to_all | solution.py:731
  (74 shorter events, 77.0 us)
Async XLA Ops:
  7.3 50.6 %copy-start.1 = (f32[256,256]{1,0:T(8,128)S(1)}, f32[256,256]{1,0:T(8,128)}, u32[]{:S(2)}) copy-start(f32[256,256]{1,0:T(8,128)} %constant.11.clone.inv_ref) | copy-start | bytes 786436
  15.1 67.7 %copy-start.3 = (f32[1,1,4,1024,128]{4,3,2,1,0:T(8,128)S(1)}, f32[1,1,4,1024,128]{4,3,2,1,0:T(8,128)}, u32[]{:S(2)}) copy-start(f32[1,1,4,1024,128]{4,3,2,1,0:T(8,128)} %param.7) | copy-start | bytes 6291460
  15.1 67.7 %copy-start.6 = (s32[1,1,1024]{2,1,0:T(1,128)S(1)}, s32[1,1,1024]{2,1,0:T(1,128)}, u32[]{:S(2)}) copy-start(s32[1,1,1024]{2,1,0:T(1,128)} %param.6) | copy-start | bytes 12292
  15.1 11.4 %all-to-all-start = ((f32[8,8,128]{2,1,0:T(8,128)}), f32[8,8,128]{2,1,0:T(8,128)S(1)}, u32[]{:S(2)}, u32[]{:S(2)}) async-start(f32[8,8,128]{2,1,0:T(8,128)} %get-tuple-element.34), calls=%async_computation | async-start | bytes 65536 | tf_op jit(solution)/shard_map/all_to_all | solution.py:731
  28.0 29.9 %all-to-all-start.1 = ((f32[32,4,8,128]{3,2,1,0:T(8,128)}), f32[32,4,8,128]{3,2,1,0:T(8,128)S(1)}, u32[]{:S(2)}, u32[]{:S(2)}) async-start(f32[32,4,8,128]{3,2,1,0:T(8,128)} %pack_start.1), calls=%async_computation.1 | async-start | bytes 1048576 | tf_op jit(solution)/shard_map/all_to_all | solution.py:731
  38.5 16.7 %collective-permute-start.4 = (f32[4,136,128]{2,1,0:T(8,128)}, f32[4,136,128]{2,1,0:T(8,128)S(1)}, u32[]{:S(2)}, u32[]{:S(2)}) collective-permute-start(f32[4,136,128]{2,1,0:T(8,128)} %copy-done.15), channel_id=1, source_target_pairs={{0,1},{1,2},{2,3},{3,4},{4,5},{5,6},{6,7},{8,9},{9,10},{10,11},{11... | collective-permute-start | bytes 835592 | tf_op jit(solution)/shard_map/ppermute | solution.py:709
  41.6 24.1 %collective-permute-start = (f32[4,208,128]{2,1,0:T(8,128)}, f32[4,208,128]{2,1,0:T(8,128)}, u32[]{:S(2)}, u32[]{:S(2)}) collective-permute-start(f32[4,208,128]{2,1,0:T(8,128)} %copy-done.11), channel_id=1, source_target_pairs={{0,32},{8,40},{16,48},{24,56},{32,64},{40,72},{48,80},{56,88},{64,... | collective-permute-start | bytes 1277960 | tf_op jit(solution)/shard_map/ppermute | solution.py:709
  49.7 33.1 %collective-permute-start.1 = (f32[4,208,128]{2,1,0:T(8,128)}, f32[4,208,128]{2,1,0:T(8,128)}, u32[]{:S(2)}, u32[]{:S(2)}) collective-permute-start(f32[4,208,128]{2,1,0:T(8,128)} %copy-done.10), channel_id=1, source_target_pairs={{32,0},{40,8},{48,16},{56,24},{64,32},{72,40},{80,48},{88,56},{96,... | collective-permute-start | bytes 1277960 | tf_op jit(solution)/shard_map/ppermute | solution.py:709
  51.0 31.8 %collective-permute-start.2 = (f32[4,208,128]{2,1,0:T(8,128)}, f32[4,208,128]{2,1,0:T(8,128)}, u32[]{:S(2)}, u32[]{:S(2)}) collective-permute-start(f32[4,208,128]{2,1,0:T(8,128)} %copy-done.9), channel_id=1, source_target_pairs={{0,8},{8,16},{16,24},{32,40},{40,48},{48,56},{64,72},{72,80},{80,8... | collective-permute-start | bytes 1277960 | tf_op jit(solution)/shard_map/ppermute | solution.py:709
  53.9 28.8 %collective-permute-start.3 = (f32[4,208,128]{2,1,0:T(8,128)}, f32[4,208,128]{2,1,0:T(8,128)}, u32[]{:S(2)}, u32[]{:S(2)}) collective-permute-start(f32[4,208,128]{2,1,0:T(8,128)} %copy-done.8), channel_id=1, source_target_pairs={{8,0},{16,8},{24,16},{40,32},{48,40},{56,48},{72,64},{80,72},{88,8... | collective-permute-start | bytes 1277960 | tf_op jit(solution)/shard_map/ppermute | solution.py:709
  55.9 9.7 %collective-permute-start.5 = (f32[4,136,128]{2,1,0:T(8,128)}, f32[4,136,128]{2,1,0:T(8,128)}, u32[]{:S(2)}, u32[]{:S(2)}) collective-permute-start(f32[4,136,128]{2,1,0:T(8,128)} %copy-done.12), channel_id=1, source_target_pairs={{1,0},{2,1},{3,2},{4,3},{5,4},{6,5},{7,6},{9,8},{10,9},{11,10},{12... | collective-permute-start | bytes 835592 | tf_op jit(solution)/shard_map/ppermute | solution.py:709
  61.6 21.1 %all-to-all-start.2 = ((f32[8,64,128]{2,1,0:T(8,128)}), f32[8,64,128]{2,1,0:T(8,128)S(1)}, u32[]{:S(2)}, u32[]{:S(2)}) async-start(f32[8,64,128]{2,1,0:T(8,128)} %copy-done.4), calls=%async_computation.2 | async-start | bytes 524288 | tf_op jit(solution)/shard_map/all_to_all | solution.py:731
  98.0 30.9 %collective-permute-start.11 = (f32[4,128,128]{2,1,0:T(8,128)S(1)}, f32[4,128,128]{2,1,0:T(8,128)S(1)}, u32[]{:S(2)}, u32[]{:S(2)}) collective-permute-start(f32[4,128,128]{2,1,0:T(8,128)S(1)} %get-tuple-element.47.refs_5_), channel_id=1, source_target_pairs={{1,0},{2,1},{3,2},{4,3},{5,4},{6,5},{7,6},{9,8},{10,9},{11,10},{12... | collective-permute-start | bytes 786440 | tf_op jit(solution)/shard_map/ppermute | solution.py:709
  102.3 35.0 %collective-permute-start.7 = (f32[4,192,128]{2,1,0:T(8,128)S(1)}, f32[4,192,128]{2,1,0:T(8,128)S(1)}, u32[]{:S(2)}, u32[]{:S(2)}) collective-permute-start(f32[4,192,128]{2,1,0:T(8,128)S(1)} %get-tuple-element.43.refs_1_), channel_id=1, source_target_pairs={{32,0},{40,8},{48,16},{56,24},{64,32},{72,40},{80,48},{88,56},{96,... | collective-permute-start | bytes 1179656 | tf_op jit(solution)/shard_map/ppermute | solution.py:709
  103.6 37.7 %collective-permute-start.6 = (f32[4,192,128]{2,1,0:T(8,128)S(1)}, f32[4,192,128]{2,1,0:T(8,128)S(1)}, u32[]{:S(2)}, u32[]{:S(2)}) collective-permute-start(f32[4,192,128]{2,1,0:T(8,128)S(1)} %get-tuple-element.44.refs_2_), channel_id=1, source_target_pairs={{0,32},{8,40},{16,48},{24,56},{32,64},{40,72},{48,80},{56,88},{64,... | collective-permute-start | bytes 1179656 | tf_op jit(solution)/shard_map/ppermute | solution.py:709
  123.7 25.4 %collective-permute-start.9 = (f32[4,192,128]{2,1,0:T(8,128)S(1)}, f32[4,192,128]{2,1,0:T(8,128)S(1)}, u32[]{:S(2)}, u32[]{:S(2)}) collective-permute-start(f32[4,192,128]{2,1,0:T(8,128)S(1)} %get-tuple-element.45.refs_3_), channel_id=1, source_target_pairs={{8,0},{16,8},{24,16},{40,32},{48,40},{56,48},{72,64},{80,72},{88,8... | collective-permute-start | bytes 1179656 | tf_op jit(solution)/shard_map/ppermute | solution.py:709
  125.0 30.1 %collective-permute-start.8 = (f32[4,192,128]{2,1,0:T(8,128)S(1)}, f32[4,192,128]{2,1,0:T(8,128)S(1)}, u32[]{:S(2)}, u32[]{:S(2)}) collective-permute-start(f32[4,192,128]{2,1,0:T(8,128)S(1)} %get-tuple-element.46.refs_4_), channel_id=1, source_target_pairs={{0,8},{8,16},{16,24},{32,40},{40,48},{48,56},{64,72},{72,80},{80,8... | collective-permute-start | bytes 1179656 | tf_op jit(solution)/shard_map/ppermute | solution.py:709
  129.0 6.9 %collective-permute-start.10 = (f32[4,128,128]{2,1,0:T(8,128)S(1)}, f32[4,128,128]{2,1,0:T(8,128)S(1)}, u32[]{:S(2)}, u32[]{:S(2)}) collective-permute-start(f32[4,128,128]{2,1,0:T(8,128)S(1)} %get-tuple-element.48.refs_6_), channel_id=1, source_target_pairs={{0,1},{1,2},{2,3},{3,4},{4,5},{5,6},{6,7},{8,9},{9,10},{10,11},{11... | collective-permute-start | bytes 786440 | tf_op jit(solution)/shard_map/ppermute | solution.py:709
  211.6 17.2 %collective-permute-start.17 = (f32[4,128,128]{2,1,0:T(8,128)S(1)}, f32[4,128,128]{2,1,0:T(8,128)S(1)}, u32[]{:S(2)}, u32[]{:S(2)}) collective-permute-start(f32[4,128,128]{2,1,0:T(8,128)S(1)} %get-tuple-element.57.refs_6_), channel_id=1, source_target_pairs={{1,0},{2,1},{3,2},{4,3},{5,4},{6,5},{7,6},{9,8},{10,9},{11,10},{12... | collective-permute-start | bytes 786440 | tf_op jit(solution)/shard_map/ppermute | solution.py:709
  214.3 21.9 %collective-permute-start.13 = (f32[4,192,128]{2,1,0:T(8,128)S(1)}, f32[4,192,128]{2,1,0:T(8,128)S(1)}, u32[]{:S(2)}, u32[]{:S(2)}) collective-permute-start(f32[4,192,128]{2,1,0:T(8,128)S(1)} %get-tuple-element.53.refs_2_), channel_id=1, source_target_pairs={{32,0},{40,8},{48,16},{56,24},{64,32},{72,40},{80,48},{88,56},{96,... | collective-permute-start | bytes 1179656 | tf_op jit(solution)/shard_map/ppermute | solution.py:709
  215.6 20.6 %collective-permute-start.12 = (f32[4,192,128]{2,1,0:T(8,128)S(1)}, f32[4,192,128]{2,1,0:T(8,128)S(1)}, u32[]{:S(2)}, u32[]{:S(2)}) collective-permute-start(f32[4,192,128]{2,1,0:T(8,128)S(1)} %get-tuple-element.54.refs_3_), channel_id=1, source_target_pairs={{0,32},{8,40},{16,48},{24,56},{32,64},{40,72},{48,80},{56,88},{64,... | collective-permute-start | bytes 1179656 | tf_op jit(solution)/shard_map/ppermute | solution.py:709
  223.5 27.4 %collective-permute-start.15 = (f32[4,192,128]{2,1,0:T(8,128)S(1)}, f32[4,192,128]{2,1,0:T(8,128)S(1)}, u32[]{:S(2)}, u32[]{:S(2)}) collective-permute-start(f32[4,192,128]{2,1,0:T(8,128)S(1)} %get-tuple-element.55.refs_4_), channel_id=1, source_target_pairs={{8,0},{16,8},{24,16},{40,32},{48,40},{56,48},{72,64},{80,72},{88,8... | collective-permute-start | bytes 1179656 | tf_op jit(solution)/shard_map/ppermute | solution.py:709
  224.8 31.8 %collective-permute-start.14 = (f32[4,192,128]{2,1,0:T(8,128)S(1)}, f32[4,192,128]{2,1,0:T(8,128)S(1)}, u32[]{:S(2)}, u32[]{:S(2)}) collective-permute-start(f32[4,192,128]{2,1,0:T(8,128)S(1)} %get-tuple-element.56.refs_5_), channel_id=1, source_target_pairs={{0,8},{8,16},{16,24},{32,40},{40,48},{48,56},{64,72},{72,80},{80,8... | collective-permute-start | bytes 1179656 | tf_op jit(solution)/shard_map/ppermute | solution.py:709
  228.8 7.3 %collective-permute-start.16 = (f32[4,128,128]{2,1,0:T(8,128)S(1)}, f32[4,128,128]{2,1,0:T(8,128)S(1)}, u32[]{:S(2)}, u32[]{:S(2)}) collective-permute-start(f32[4,128,128]{2,1,0:T(8,128)S(1)} %get-tuple-element.58.refs_7_), channel_id=1, source_target_pairs={{0,1},{1,2},{2,3},{3,4},{4,5},{5,6},{6,7},{8,9},{9,10},{10,11},{11... | collective-permute-start | bytes 786440 | tf_op jit(solution)/shard_map/ppermute | solution.py:709
  (13 other events, 13.2 us)

commit v4 on v3

--- a/solution.py
+++ b/solution.py
@@ -91,18 +91,20 @@
 
 
 def fill_gather(col_ref, o_ref):
-    lanes = lax.broadcasted_iota(jnp.int32, (CHUNK, M), 1)
+    lanes = lax.broadcasted_iota(jnp.int16, (CHUNK, M), 1)
+    one, zero = jnp.ones((), BF16), jnp.zeros((), BF16)
     for i in range(0, M, CHUNK):
-        hit = col_ref[i : i + CHUNK, :] == lanes
-        o_ref[i : i + CHUNK, :] = jnp.where(hit, 1.0, 0.0).astype(BF16)
+        hit = col_ref[i : i + CHUNK, :].astype(jnp.int16) == lanes
+        o_ref[i : i + CHUNK, :] = jnp.where(hit, one, zero)
 
 
 def fill_scatter(row_ref, ot_ref):
-    row = row_ref[...]
-    index = lax.broadcasted_iota(jnp.int32, (CHUNK, M), 0)
+    row = jnp.broadcast_to(row_ref[...], (CHUNK, M)).astype(jnp.int16)
+    index = lax.broadcasted_iota(jnp.int16, (CHUNK, M), 0)
+    one, zero = jnp.ones((), BF16), jnp.zeros((), BF16)
     for i in range(0, M, CHUNK):
-        hit = row == index + i
-        ot_ref[i : i + CHUNK, :] = jnp.where(hit, 1.0, 0.0).astype(BF16)
+        hit = row == index + jnp.int16(i)
+        ot_ref[i : i + CHUNK, :] = jnp.where(hit, one, zero)
 
 
 def prep_kernel(row_ref, col_ref, flux_ref, gap_ref, load_ref, *refs):
@@ -180,7 +182,7 @@
         ]
         + [out(shape) for shape in faces],
         scratch_shapes=[pltpu.VMEM((SPECIES, 48, M), BF16), pltpu.VMEM((M, M), BF16)],
-        compiler_params=params(),
+        compiler_params=params(60 * MIB),
         cost_estimate=cost(1e9, 20e6),
         name="prep",
     )(row, column, flux, gap, load.reshape(SPECIES, 1, CASES))

time: 332 us -> 326 us (0.982)
  local copies, waits for them, and re-layouts: 14.1 us -> 4.05 us
  Pallas kernels: 52.1 us -> 56.4 us
    unnamed x32 -> x16, local copies, waits for them, and re-layouts: 13.2 us -> 2.35 us
    pallas_call x1, Pallas kernels: 3.31 us -> 8.11 us  [prep(): pl.pallas_call(prep_kernel, grid=(SPECIES,), in_specs=[whole(1, M), whole...]
where the time goes in v4:
time: 326 us; the launch traced here: 325 us
  blocking collectives  100 us (31%)
  starting transfers between devices  95.5 us (29%)
  waiting for transfers between devices  68 us (21%)
  Pallas kernels  56.4 us (17%)
  local copies, waits for them, and re-layouts  4.05 us (1%)
    all_to_all x8, blocking collectives, swap(): return lax.all_to_all(value, axis, 0, 0, tiled=True)  100 us
    ppermute x18, starting transfers between devices, moved(): return lax.ppermute(value, axis, pairs)  74.3 us
    ppermute x18, waiting for transfers between devices, moved(): return lax.ppermute(value, axis, pairs)  63.3 us
    all_to_all x3, starting transfers between devices, swap(): return lax.all_to_all(value, axis, 0, 0, tiled=True)  21.3 us
    pallas_call x2, Pallas kernels, step(): pl.pallas_call(functools.partial(step_kernel, same, last), grid=(SPECIES...  20.6 us
    pallas_call x1, Pallas kernels, start(): pl.pallas_call(start_kernel, grid=(SPECIES + 1,), in_specs=[per_species(M...  14.1 us
    pallas_call x1, Pallas kernels, prep(): pl.pallas_call(prep_kernel, grid=(SPECIES,), in_specs=[whole(1, M), whole...  8.11 us
  transfers between devices with their start and end apart: 21, of which 10 were waited for; matrix products, arithmetic and copies ran while one was open for 0% of the time, Pallas kernels for 1%

profile of v4, /device:TPU:1, one launch (start us, length us, event | category | flops | bytes accessed | tf_op | source)
XLA Modules:
  0.0 324.8 jit_solution(16184238211536491055)
XLA Ops:
  1.7 8.1 %prep.1 = (f32[4,8,1024]{2,1,0:T(8,128)}, f32[8,8,128]{2,1,0:T(8,128)}, f32[4,208,128]{2,1,0:T(8,128)}, f32[4,208,128]{2,1,0:T(8,128)}, f32[4,208,128]{2,1,0:T(8...) custom-call(s32[1,1024]{1,0:T(1,128)} %bitcast.11, s32[1024,1]{1,0:T(8,128)} %copy.6.col_ref, ...), custom_call_target="tpu_custom_call" | custom-call | flops 1000000000 | bytes 20000000 | tf_op jit(solution)/shard_map/prep/pallas_call | solution.py:167
  9.9 6.7 %all-to-all-start = ((f32[8,8,128]{2,1,0:T(8,128)}), f32[8,8,128]{2,1,0:T(8,128)S(1)}, u32[]{:S(2)}, u32[]{:S(2)}) async-start(f32[8,8,128]{2,1,0:T(8,128)} %get-tuple-element.34), calls=%async_computation | async-start | bytes 65536 | tf_op jit(solution)/shard_map/all_to_all | solution.py:733
  16.7 4.7 %all-to-all-done.got_ref = f32[8,8,128]{2,1,0:T(8,128)S(1)} async-done(((f32[8,8,128]{2,1,0:T(8,128)}), f32[8,8,128]{2,1,0:T(8,128)S(1)}, u32[]{:S(2)}, u32[]{:S(2)}) %all-to-all-start) | async-done | bytes 32800 | tf_op jit(solution)/shard_map/all_to_all | solution.py:733
  22.9 10.5 %all-to-all-start.1 = ((f32[32,4,8,128]{3,2,1,0:T(8,128)}), f32[32,4,8,128]{3,2,1,0:T(8,128)S(1)}, u32[]{:S(2)}, u32[]{:S(2)}) async-start(f32[32,4,8,128]{3,2,1,0:T(8,128)} %pack_start.1), calls=%async_computation.1 | async-start | bytes 1048576 | tf_op jit(solution)/shard_map/all_to_all | solution.py:733
  36.5 8.1 %collective-permute-start = (f32[4,208,128]{2,1,0:T(8,128)}, f32[4,208,128]{2,1,0:T(8,128)}, u32[]{:S(2)}, u32[]{:S(2)}) collective-permute-start(f32[4,208,128]{2,1,0:T(8,128)} %get-tuple-element.36), channel_id=1, source_target_pairs={{0,32},{8,40},{16,48},{24,56},{32,64},{40,72},{48,80},{56,88},{64,... | collective-permute-start | bytes 1277960 | tf_op jit(solution)/shard_map/ppermute | solution.py:711
  60.6 17.1 %collective-permute-done.1.refs_1_ = f32[4,208,128]{2,1,0:T(8,128)} collective-permute-done((f32[4,208,128]{2,1,0:T(8,128)}, f32[4,208,128]{2,1,0:T(8,128)}, u32[]{:S(2)}, u32[]{:S(2)}) %collective-permute-start.1) | collective-permute-done | bytes 426016 | tf_op jit(solution)/shard_map/ppermute | solution.py:711
  78.7 14.1 %start.1 = (f32[4,1024,128]{2,1,0:T(8,128)S(1)}, f32[4,192,128]{2,1,0:T(8,128)S(1)}, f32[4,192,128]{2,1,0:T(8,128)S(1)}, f32[4,192,128]{2,1,0:T(8,128)S(1)}, f32...) custom-call(f32[4,1024,128]{2,1,0:T(8,128)S(1)} %bitcast.9, ...), custom_call_target="tpu_custom_call" | custom-call | flops 4000000000 | bytes 20000000 | tf_op jit(solution)/shard_map/start/pallas_call | solution.py:506
  92.8 4.2 %collective-permute-start.11 = (f32[4,128,128]{2,1,0:T(8,128)S(1)}, f32[4,128,128]{2,1,0:T(8,128)S(1)}, u32[]{:S(2)}, u32[]{:S(2)}) collective-permute-start(f32[4,128,128]{2,1,0:T(8,128)S(1)} %get-tuple-element.47.refs_5_), channel_id=1, source_target_pairs={{1,0},{2,1},{3,2},{4,3},{5,4},{6,5},{7,6},{9,8},{10,9},{11,10},{12... | collective-permute-start | bytes 786440 | tf_op jit(solution)/shard_map/ppermute | solution.py:711
  98.4 20.1 %collective-permute-start.6 = (f32[4,192,128]{2,1,0:T(8,128)S(1)}, f32[4,192,128]{2,1,0:T(8,128)S(1)}, u32[]{:S(2)}, u32[]{:S(2)}) collective-permute-start(f32[4,192,128]{2,1,0:T(8,128)S(1)} %get-tuple-element.44.refs_2_), channel_id=1, source_target_pairs={{0,32},{8,40},{16,48},{24,56},{32,64},{40,72},{48,80},{56,88},{64,... | collective-permute-start | bytes 1179656 | tf_op jit(solution)/shard_map/ppermute | solution.py:711
  136.1 7.7 %collective-permute-done.9.refs_10_ = f32[4,192,128]{2,1,0:T(8,128)S(1)} collective-permute-done((f32[4,192,128]{2,1,0:T(8,128)S(1)}, f32[4,192,128]{2,1,0:T(8,128)S(1)}, u32[]{:S(2)}, u32[]{:S(2)}) %collective-permute-start.9) | collective-permute-done | bytes 393248 | tf_op jit(solution)/shard_map/ppermute | solution.py:711
  143.9 6.0 %collective-permute-done.8.refs_9_ = f32[4,192,128]{2,1,0:T(8,128)S(1)} collective-permute-done((f32[4,192,128]{2,1,0:T(8,128)S(1)}, f32[4,192,128]{2,1,0:T(8,128)S(1)}, u32[]{:S(2)}, u32[]{:S(2)}) %collective-permute-start.8) | collective-permute-done | bytes 393248 | tf_op jit(solution)/shard_map/ppermute | solution.py:711
  151.4 7.4 %all_to_all.55.got_ref = f32[8,8,128]{2,1,0:T(8,128)S(1)} all-to-all(f32[8,8,128]{2,1,0:T(8,128)S(1)} %get-tuple-element.49), channel_id=1, replica_groups=mesh['col'=32,'lay'=8] {'lay'}, dimensions={0} | all-to-all | bytes 65536 | tf_op jit(solution)/shard_map/all_to_all | solution.py:733
  159.5 26.2 %all_to_all.56.gathered_ref = f32[32,8,128]{2,1,0:T(8,128)S(1)} all-to-all(f32[32,8,128]{2,1,0:T(8,128)S(1)} %combine_layers.2), channel_id=1, replica_groups=mesh['col'=32,'lay'=8] {'col'}, dimensions={0} | all-to-all | bytes 262144 | tf_op jit(solution)/shard_map/all_to_all | solution.py:733
  186.9 9.2 %all_to_all.57.back_ref.back0_ref = f32[8,8,128]{2,1,0:T(8,128)S(1)} all-to-all(f32[8,8,128]{2,1,0:T(8,128)S(1)} %solve_step.2), channel_id=1, replica_groups=mesh['col'=32,'lay'=8] {'lay'}, dimensions={0} | all-to-all | bytes 65536 | tf_op jit(solution)/shard_map/all_to_all | solution.py:733
  196.1 10.1 %step.2 = (f32[4,1024,128]{2,1,0:T(8,128)S(1)}, f32[4,1024,128]{2,1,0:T(8,128)S(1)}, f32[4,192,128]{2,1,0:T(8,128)S(1)}, f32[4,192,128]{2,1,0:T(8,128)S(1)}, f32...) custom-call(s32[2]{0:T(128)S(1)} %pad_add_fusion.info_ref, ...), custom_call_target="tpu_custom_call" | custom-call | flops 4000000000 | bytes 20000000 | tf_op jit(solution)/shard_map/step/pallas_call | solution.py:664
  210.2 7.9 %collective-permute-start.12 = (f32[4,192,128]{2,1,0:T(8,128)S(1)}, f32[4,192,128]{2,1,0:T(8,128)S(1)}, u32[]{:S(2)}, u32[]{:S(2)}) collective-permute-start(f32[4,192,128]{2,1,0:T(8,128)S(1)} %get-tuple-element.54.refs_3_), channel_id=1, source_target_pairs={{0,32},{8,40},{16,48},{24,56},{32,64},{40,72},{48,80},{56,88},{64,... | collective-permute-start | bytes 1179656 | tf_op jit(solution)/shard_map/ppermute | solution.py:711
  230.8 14.7 %collective-permute-done.15.refs_11_ = f32[4,192,128]{2,1,0:T(8,128)S(1)} collective-permute-done((f32[4,192,128]{2,1,0:T(8,128)S(1)}, f32[4,192,128]{2,1,0:T(8,128)S(1)}, u32[]{:S(2)}, u32[]{:S(2)}) %collective-permute-start.15) | collective-permute-done | bytes 393248 | tf_op jit(solution)/shard_map/ppermute | solution.py:711
  245.5 5.7 %collective-permute-done.14.refs_10_ = f32[4,192,128]{2,1,0:T(8,128)S(1)} collective-permute-done((f32[4,192,128]{2,1,0:T(8,128)S(1)}, f32[4,192,128]{2,1,0:T(8,128)S(1)}, u32[]{:S(2)}, u32[]{:S(2)}) %collective-permute-start.14) | collective-permute-done | bytes 393248 | tf_op jit(solution)/shard_map/ppermute | solution.py:711
  252.8 7.6 %all_to_all.58.got_ref = f32[8,8,128]{2,1,0:T(8,128)S(1)} all-to-all(f32[8,8,128]{2,1,0:T(8,128)S(1)} %get-tuple-element.59), channel_id=1, replica_groups=mesh['col'=32,'lay'=8] {'lay'}, dimensions={0} | all-to-all | bytes 65536 | tf_op jit(solution)/shard_map/all_to_all | solution.py:733
  261.1 20.4 %all_to_all.59.gathered_ref = f32[32,8,128]{2,1,0:T(8,128)S(1)} all-to-all(f32[32,8,128]{2,1,0:T(8,128)S(1)} %combine_layers.3), channel_id=1, replica_groups=mesh['col'=32,'lay'=8] {'col'}, dimensions={0} | all-to-all | bytes 262144 | tf_op jit(solution)/shard_map/all_to_all | solution.py:733
  282.7 9.2 %all_to_all.60.back_ref.back1_ref = f32[8,8,128]{2,1,0:T(8,128)S(1)} all-to-all(f32[8,8,128]{2,1,0:T(8,128)S(1)} %solve_step.3), channel_id=1, replica_groups=mesh['col'=32,'lay'=8] {'lay'}, dimensions={0} | all-to-all | bytes 65536 | tf_op jit(solution)/shard_map/all_to_all | solution.py:733
  291.9 10.5 %step.3 = (f32[4,1024,128]{2,1,0:T(8,128)S(1)}, f32[8,8,128]{2,1,0:T(8,128)S(1)}) custom-call(s32[2]{0:T(128)S(1)} %pad_add_fusion.info_ref, f32[8,8,128]{2,1,0:T(8,128)S(1)} %all_to_all.60.back_ref.back1_ref, s32[1,1024]{1,0:T(1,128)S(1)} %bitcast.14, s32[1024,1]{1,0:T(8,128)S(1)} %copy-done, bf16[4,1024,1024]{2,1,0:T(8,128)(2,1)} %bitcast.18, ...), custom_call_target="tpu_custom_call" | custom-call | flops 4000000000 | bytes 20000000 | tf_op jit(solution)/shard_map/step/pallas_call | solution.py:664
  302.3 7.8 %all_to_all.61.got_ref = f32[8,8,128]{2,1,0:T(8,128)S(1)} all-to-all(f32[8,8,128]{2,1,0:T(8,128)S(1)} %get-tuple-element.61), channel_id=1, replica_groups=mesh['col'=32,'lay'=8] {'lay'}, dimensions={0} | all-to-all | bytes 65536 | tf_op jit(solution)/shard_map/all_to_all | solution.py:733
  310.2 12.5 %all_to_all.62.sums_ref = f32[32,8,128]{2,1,0:T(8,128)S(1)} all-to-all(f32[32,8,128]{2,1,0:T(8,128)S(1)} %combine_last.1), channel_id=1, replica_groups=mesh['col'=32,'lay'=8] {'col'}, dimensions={0} | all-to-all | bytes 262144 | tf_op jit(solution)/shard_map/all_to_all | solution.py:733
  (58 shorter events, 67.8 us)
Async XLA Ops:
  9.8 67.9 %copy-start.2 = (f32[1,1,4,1024,128]{4,3,2,1,0:T(8,128)S(1)}, f32[1,1,4,1024,128]{4,3,2,1,0:T(8,128)}, u32[]{:S(2)}) copy-start(f32[1,1,4,1024,128]{4,3,2,1,0:T(8,128)} %param.7) | copy-start | bytes 6291460
  9.8 67.9 %copy-start.4 = (s32[1,1,1024]{2,1,0:T(1,128)S(1)}, s32[1,1,1024]{2,1,0:T(1,128)}, u32[]{:S(2)}) copy-start(s32[1,1,1024]{2,1,0:T(1,128)} %param.6) | copy-start | bytes 12292
  9.8 67.9 %copy-start.7 = (f32[4,8,1024]{2,1,0:T(8,128)S(1)}, f32[4,8,1024]{2,1,0:T(8,128)}, u32[]{:S(2)}) copy-start(f32[4,8,1024]{2,1,0:T(8,128)} %get-tuple-element.35.rt_ref) | copy-start | bytes 393220
  9.9 11.5 %all-to-all-start = ((f32[8,8,128]{2,1,0:T(8,128)}), f32[8,8,128]{2,1,0:T(8,128)S(1)}, u32[]{:S(2)}, u32[]{:S(2)}) async-start(f32[8,8,128]{2,1,0:T(8,128)} %get-tuple-element.34), calls=%async_computation | async-start | bytes 65536 | tf_op jit(solution)/shard_map/all_to_all | solution.py:733
  22.9 29.9 %all-to-all-start.1 = ((f32[32,4,8,128]{3,2,1,0:T(8,128)}), f32[32,4,8,128]{3,2,1,0:T(8,128)S(1)}, u32[]{:S(2)}, u32[]{:S(2)}) async-start(f32[32,4,8,128]{3,2,1,0:T(8,128)} %pack_start.1), calls=%async_computation.1 | async-start | bytes 1048576 | tf_op jit(solution)/shard_map/all_to_all | solution.py:733
  33.4 16.7 %collective-permute-start.4 = (f32[4,136,128]{2,1,0:T(8,128)}, f32[4,136,128]{2,1,0:T(8,128)S(1)}, u32[]{:S(2)}, u32[]{:S(2)}) collective-permute-start(f32[4,136,128]{2,1,0:T(8,128)} %get-tuple-element.40), channel_id=1, source_target_pairs={{0,1},{1,2},{2,3},{3,4},{4,5},{5,6},{6,7},{8,9},{9,10},{10,11},{11... | collective-permute-start | bytes 835592 | tf_op jit(solution)/shard_map/ppermute | solution.py:711
  36.5 24.1 %collective-permute-start = (f32[4,208,128]{2,1,0:T(8,128)}, f32[4,208,128]{2,1,0:T(8,128)}, u32[]{:S(2)}, u32[]{:S(2)}) collective-permute-start(f32[4,208,128]{2,1,0:T(8,128)} %get-tuple-element.36), channel_id=1, source_target_pairs={{0,32},{8,40},{16,48},{24,56},{32,64},{40,72},{48,80},{56,88},{64,... | collective-permute-start | bytes 1277960 | tf_op jit(solution)/shard_map/ppermute | solution.py:711
  44.6 33.1 %collective-permute-start.1 = (f32[4,208,128]{2,1,0:T(8,128)}, f32[4,208,128]{2,1,0:T(8,128)}, u32[]{:S(2)}, u32[]{:S(2)}) collective-permute-start(f32[4,208,128]{2,1,0:T(8,128)} %get-tuple-element.37), channel_id=1, source_target_pairs={{32,0},{40,8},{48,16},{56,24},{64,32},{72,40},{80,48},{88,56},{96,... | collective-permute-start | bytes 1277960 | tf_op jit(solution)/shard_map/ppermute | solution.py:711
  45.9 31.8 %collective-permute-start.2 = (f32[4,208,128]{2,1,0:T(8,128)}, f32[4,208,128]{2,1,0:T(8,128)}, u32[]{:S(2)}, u32[]{:S(2)}) collective-permute-start(f32[4,208,128]{2,1,0:T(8,128)} %get-tuple-element.38), channel_id=1, source_target_pairs={{0,8},{8,16},{16,24},{32,40},{40,48},{48,56},{64,72},{72,80},{80,8... | collective-permute-start | bytes 1277960 | tf_op jit(solution)/shard_map/ppermute | solution.py:711
  48.8 28.8 %collective-permute-start.3 = (f32[4,208,128]{2,1,0:T(8,128)}, f32[4,208,128]{2,1,0:T(8,128)}, u32[]{:S(2)}, u32[]{:S(2)}) collective-permute-start(f32[4,208,128]{2,1,0:T(8,128)} %get-tuple-element.39), channel_id=1, source_target_pairs={{8,0},{16,8},{24,16},{40,32},{48,40},{56,48},{72,64},{80,72},{88,8... | collective-permute-start | bytes 1277960 | tf_op jit(solution)/shard_map/ppermute | solution.py:711
  50.8 9.7 %collective-permute-start.5 = (f32[4,136,128]{2,1,0:T(8,128)}, f32[4,136,128]{2,1,0:T(8,128)}, u32[]{:S(2)}, u32[]{:S(2)}) collective-permute-start(f32[4,136,128]{2,1,0:T(8,128)} %get-tuple-element.41), channel_id=1, source_target_pairs={{1,0},{2,1},{3,2},{4,3},{5,4},{6,5},{7,6},{9,8},{10,9},{11,10},{12... | collective-permute-start | bytes 835592 | tf_op jit(solution)/shard_map/ppermute | solution.py:711
  56.5 21.1 %all-to-all-start.2 = ((f32[8,64,128]{2,1,0:T(8,128)}), f32[8,64,128]{2,1,0:T(8,128)S(1)}, u32[]{:S(2)}, u32[]{:S(2)}) async-start(f32[8,64,128]{2,1,0:T(8,128)} %copy-done.3), calls=%async_computation.2 | async-start | bytes 524288 | tf_op jit(solution)/shard_map/all_to_all | solution.py:733
  92.8 30.9 %collective-permute-start.11 = (f32[4,128,128]{2,1,0:T(8,128)S(1)}, f32[4,128,128]{2,1,0:T(8,128)S(1)}, u32[]{:S(2)}, u32[]{:S(2)}) collective-permute-start(f32[4,128,128]{2,1,0:T(8,128)S(1)} %get-tuple-element.47.refs_5_), channel_id=1, source_target_pairs={{1,0},{2,1},{3,2},{4,3},{5,4},{6,5},{7,6},{9,8},{10,9},{11,10},{12... | collective-permute-start | bytes 786440 | tf_op jit(solution)/shard_map/ppermute | solution.py:711
  97.1 35.0 %collective-permute-start.7 = (f32[4,192,128]{2,1,0:T(8,128)S(1)}, f32[4,192,128]{2,1,0:T(8,128)S(1)}, u32[]{:S(2)}, u32[]{:S(2)}) collective-permute-start(f32[4,192,128]{2,1,0:T(8,128)S(1)} %get-tuple-element.43.refs_1_), channel_id=1, source_target_pairs={{32,0},{40,8},{48,16},{56,24},{64,32},{72,40},{80,48},{88,56},{96,... | collective-permute-start | bytes 1179656 | tf_op jit(solution)/shard_map/ppermute | solution.py:711
  98.4 37.8 %collective-permute-start.6 = (f32[4,192,128]{2,1,0:T(8,128)S(1)}, f32[4,192,128]{2,1,0:T(8,128)S(1)}, u32[]{:S(2)}, u32[]{:S(2)}) collective-permute-start(f32[4,192,128]{2,1,0:T(8,128)S(1)} %get-tuple-element.44.refs_2_), channel_id=1, source_target_pairs={{0,32},{8,40},{16,48},{24,56},{32,64},{40,72},{48,80},{56,88},{64,... | collective-permute-start | bytes 1179656 | tf_op jit(solution)/shard_map/ppermute | solution.py:711
  118.4 25.4 %collective-permute-start.9 = (f32[4,192,128]{2,1,0:T(8,128)S(1)}, f32[4,192,128]{2,1,0:T(8,128)S(1)}, u32[]{:S(2)}, u32[]{:S(2)}) collective-permute-start(f32[4,192,128]{2,1,0:T(8,128)S(1)} %get-tuple-element.45.refs_3_), channel_id=1, source_target_pairs={{8,0},{16,8},{24,16},{40,32},{48,40},{56,48},{72,64},{80,72},{88,8... | collective-permute-start | bytes 1179656 | tf_op jit(solution)/shard_map/ppermute | solution.py:711
  119.7 30.1 %collective-permute-start.8 = (f32[4,192,128]{2,1,0:T(8,128)S(1)}, f32[4,192,128]{2,1,0:T(8,128)S(1)}, u32[]{:S(2)}, u32[]{:S(2)}) collective-permute-start(f32[4,192,128]{2,1,0:T(8,128)S(1)} %get-tuple-element.46.refs_4_), channel_id=1, source_target_pairs={{0,8},{8,16},{16,24},{32,40},{40,48},{48,56},{64,72},{72,80},{80,8... | collective-permute-start | bytes 1179656 | tf_op jit(solution)/shard_map/ppermute | solution.py:711
  123.8 6.9 %collective-permute-start.10 = (f32[4,128,128]{2,1,0:T(8,128)S(1)}, f32[4,128,128]{2,1,0:T(8,128)S(1)}, u32[]{:S(2)}, u32[]{:S(2)}) collective-permute-start(f32[4,128,128]{2,1,0:T(8,128)S(1)} %get-tuple-element.48.refs_6_), channel_id=1, source_target_pairs={{0,1},{1,2},{2,3},{3,4},{4,5},{5,6},{6,7},{8,9},{9,10},{10,11},{11... | collective-permute-start | bytes 786440 | tf_op jit(solution)/shard_map/ppermute | solution.py:711
  206.2 17.2 %collective-permute-start.17 = (f32[4,128,128]{2,1,0:T(8,128)S(1)}, f32[4,128,128]{2,1,0:T(8,128)S(1)}, u32[]{:S(2)}, u32[]{:S(2)}) collective-permute-start(f32[4,128,128]{2,1,0:T(8,128)S(1)} %get-tuple-element.57.refs_6_), channel_id=1, source_target_pairs={{1,0},{2,1},{3,2},{4,3},{5,4},{6,5},{7,6},{9,8},{10,9},{11,10},{12... | collective-permute-start | bytes 786440 | tf_op jit(solution)/shard_map/ppermute | solution.py:711
  208.9 21.9 %collective-permute-start.13 = (f32[4,192,128]{2,1,0:T(8,128)S(1)}, f32[4,192,128]{2,1,0:T(8,128)S(1)}, u32[]{:S(2)}, u32[]{:S(2)}) collective-permute-start(f32[4,192,128]{2,1,0:T(8,128)S(1)} %get-tuple-element.53.refs_2_), channel_id=1, source_target_pairs={{32,0},{40,8},{48,16},{56,24},{64,32},{72,40},{80,48},{88,56},{96,... | collective-permute-start | bytes 1179656 | tf_op jit(solution)/shard_map/ppermute | solution.py:711
  210.2 20.6 %collective-permute-start.12 = (f32[4,192,128]{2,1,0:T(8,128)S(1)}, f32[4,192,128]{2,1,0:T(8,128)S(1)}, u32[]{:S(2)}, u32[]{:S(2)}) collective-permute-start(f32[4,192,128]{2,1,0:T(8,128)S(1)} %get-tuple-element.54.refs_3_), channel_id=1, source_target_pairs={{0,32},{8,40},{16,48},{24,56},{32,64},{40,72},{48,80},{56,88},{64,... | collective-permute-start | bytes 1179656 | tf_op jit(solution)/shard_map/ppermute | solution.py:711
  218.1 27.4 %collective-permute-start.15 = (f32[4,192,128]{2,1,0:T(8,128)S(1)}, f32[4,192,128]{2,1,0:T(8,128)S(1)}, u32[]{:S(2)}, u32[]{:S(2)}) collective-permute-start(f32[4,192,128]{2,1,0:T(8,128)S(1)} %get-tuple-element.55.refs_4_), channel_id=1, source_target_pairs={{8,0},{16,8},{24,16},{40,32},{48,40},{56,48},{72,64},{80,72},{88,8... | collective-permute-start | bytes 1179656 | tf_op jit(solution)/shard_map/ppermute | solution.py:711
  219.4 31.8 %collective-permute-start.14 = (f32[4,192,128]{2,1,0:T(8,128)S(1)}, f32[4,192,128]{2,1,0:T(8,128)S(1)}, u32[]{:S(2)}, u32[]{:S(2)}) collective-permute-start(f32[4,192,128]{2,1,0:T(8,128)S(1)} %get-tuple-element.56.refs_5_), channel_id=1, source_target_pairs={{0,8},{8,16},{16,24},{32,40},{40,48},{48,56},{64,72},{72,80},{80,8... | collective-permute-start | bytes 1179656 | tf_op jit(solution)/shard_map/ppermute | solution.py:711
  223.4 7.3 %collective-permute-start.16 = (f32[4,128,128]{2,1,0:T(8,128)S(1)}, f32[4,128,128]{2,1,0:T(8,128)S(1)}, u32[]{:S(2)}, u32[]{:S(2)}) collective-permute-start(f32[4,128,128]{2,1,0:T(8,128)S(1)} %get-tuple-element.58.refs_7_), channel_id=1, source_target_pairs={{0,1},{1,2},{2,3},{3,4},{4,5},{5,6},{6,7},{8,9},{9,10},{10,11},{11... | collective-permute-start | bytes 786440 | tf_op jit(solution)/shard_map/ppermute | solution.py:711
  (5 other events, 121.3 us)
